TPU v7x, 32 devices: a whole 2x2x4 slice. The times are simulated.
32 devices in a mesh: row: 4 (over y, x), col: 8 (over z, core).
Axes of the slice: x: 2, y: 2, z: 4, core: 2. Of those that a mesh axis runs over, the one named last changes fastest.
Arguments:
- amplitudes: bfloat16 [24576, 24576], P('row', 'col'), may hold values from -4 to 4
- cholesky: bfloat16 [24576, 512], P('row'), may hold values from -6 to 6
- gaps: float32 [24576], replicated, may hold values from 0.5 to 2
Outputs:
- final_amplitudes: bfloat16 [24576, 24576], P('row', 'col')
All inputs are finite; a program needn't handle non-finite values.
Results may differ from a plain program's by a relative error of at most 0.0057.
Values may be sent and summed in bfloat16 or wider, within the bound.
No kernel may reach another device: no remote copies, remote signals or barrier semaphores. Data moves between devices by JAX's collectives and lax.ppermute only.
A program may use at most 128 MiB of HBM per device.

v0:
```python
import jax
import jax.numpy as jnp
from jax import lax
from jax.sharding import PartitionSpec as P

P_SIZE = 24576
L = 512


def spread(value, axis, source):
    kept = jnp.where(lax.axis_index(axis) == source, value, 0).astype(value.dtype)
    return lax.psum(kept, axis)


def shards(amplitudes, cholesky, gaps):
    rows_dev = amplitudes.shape[0]
    cols_dev = amplitudes.shape[1]
    col_index = lax.axis_index("col")
    row_index = lax.axis_index("row")
    first_col = col_index * cols_dev
    root_row = first_col // rows_dev
    offset = first_col - root_row * rows_dev
    dress_scale = P_SIZE ** (-0.5)
    score_scale = L ** (-0.5)
    chol_cols = spread(lax.dynamic_slice_in_dim(cholesky, offset, cols_dev, 0), "row", root_row)
    gap_rows = lax.dynamic_slice_in_dim(gaps, row_index * rows_dev, rows_dev, 0)
    gap_cols = lax.dynamic_slice_in_dim(gaps, first_col, cols_dev, 0)
    pieces = rows_dev // lax.axis_size("col")
    own_rows = lax.dynamic_slice_in_dim(cholesky, col_index * pieces, pieces, 0).astype(jnp.float32)
    current = amplitudes

    def partial_term(first_row, row_count, tile=current):
        return jnp.dot(tile, chol_cols, preferred_element_type=jnp.float32)

    summed = lax.psum_scatter(
        partial_term(jnp.int32(0), lax.axis_size("col") * pieces),
        "col",
        scatter_dimension=0,
        tiled=True,
    )
    dressed = (own_rows + summed * dress_scale).astype(jnp.bfloat16)
    w_rows = lax.all_gather(dressed, "col", axis=0, tiled=True)
    w_cols = spread(lax.dynamic_slice_in_dim(w_rows, offset, cols_dev, 0), "row", root_row)
    product = lax.dot_general(
        w_rows, w_cols, (((1,), (1,)), ((), ())), preferred_element_type=jnp.float32
    )
    current = (-(product * score_scale) / (gap_rows[:, None] + gap_cols[None, :])).astype(
        jnp.bfloat16
    )
    return current


def solution(mesh):
    in_specs = (P("row", "col"), P("row", None), P())
    out_specs = P("row", "col")
    return jax.shard_map(shards, mesh=mesh, in_specs=in_specs, out_specs=out_specs, check_vma=False)
```

profile of v0, /device:TPU:0, one launch (start us, length us, event | category | flops | bytes accessed | tf_op | source)
XLA Modules:
  0.0 456.9 jit_solution(3350266267648194016)
XLA Ops:
  6.5 0.0 all-reduce.3.cloned.1.call-start
  6.5 3.8 constant_dynamic-slice_fusion
  10.3 3.2 copy.7
  13.5 1.9 broadcast_select_fusion
  15.4 0.0 all-reduce.3.cloned.1.call-update
  15.4 0.0 reduce-scatter.2.cloned.1.call-start
  15.4 90.0 %all-reduce.3.cloned.1.call-done = bf16[3072,512]{0,1:T(8,128)(2,1)} async-done(((bf16[3072,512]{0,1:T(8,128)(2,1)}), bf16[3072,512]{0,1:T(8,128)(2,1)}) %all-reduce.3.cloned.1.call-update) | async-done | bytes 3145744 | tf_op jit(solution)/shard_map/psum | solution.py:12
  105.4 27.6 %convolution_bitcast_fusion = f32[6144,512]{0,1:T(8,128)} fusion(bf16[3072,512]{0,1:T(8,128)(2,1)} %all-reduce.3.cloned.1.call-done, bf16[6144,3072]{1,0:T(8,128)(2,1)} %param.3), kind=kOutput, calls=%fused_computation.1 | convolution fusion | flops 19327352832 | bytes 53477376 | tf_op jit(solution)/shard_map/dot_general | solution.py:33
  133.0 0.0 reduce-scatter.2.cloned.1.call-update
  133.0 0.0 all-gather.2.cloned.1.call-start
  133.1 1.2 constant_dynamic-slice_fusion.1
  134.3 0.3 copy.6
  134.6 127.8 %reduce-scatter.2.cloned.1.call-done = f32[768,512]{0,1:T(8,128)} async-done(((f32[6144,512]{0,1:T(8,128)}), f32[768,512]{0,1:T(8,128)}) %reduce-scatter.2.cloned.1.call-update) | async-done | bytes 1572880 | tf_op jit(solution)/shard_map/reduce_scatter | solution.py:35
  262.4 2.5 add_convert_fusion
  264.9 0.0 all-gather.2.cloned.1.call-update
  264.9 0.2 all-reduce.5.cloned.1.call-start
  265.1 63.0 %all-gather.2.cloned.1.call-done = bf16[6144,512]{0,1:T(8,128)(2,1)} async-done(((bf16[768,512]{0,1:T(8,128)(2,1)}), bf16[6144,512]{0,1:T(8,128)(2,1)}) %all-gather.2.cloned.1.call-update) | async-done | bytes 6291472 | tf_op jit(solution)/shard_map/all_gather | solution.py:42
  328.1 4.2 dynamic-slice_select_fusion
  332.3 0.0 all-reduce.5.cloned.1.call-update
  332.4 0.7 dynamic_slice.19
  333.1 0.7 dynamic_slice.18
  333.8 84.6 %all-reduce.5.cloned.1.call-done = bf16[3072,512]{0,1:T(8,128)(2,1)} async-done(((bf16[3072,512]{0,1:T(8,128)(2,1)}), bf16[3072,512]{0,1:T(8,128)(2,1)}) %all-reduce.5.cloned.1.call-update) | async-done | bytes 3145744 | tf_op jit(solution)/shard_map/psum | solution.py:12
  418.4 31.9 %divide_convert_fusion = bf16[6144,3072]{1,0:T(8,128)(2,1)} fusion(f32[3072]{0:T(1024)S(1)} %dynamic_slice.19, f32[6144]{0:T(1024)S(1)} %dynamic_slice.18, bf16[6144,512]{0,1:T(8,128)(2,1)} %all-gather.2.cloned.1.call-done, bf16[3072,512]{0,1:T(8,128)(2,1)} %all-reduce.5.cloned.1.call-done), kind=kOutput, calls=%fused_computation | convolution fusion | flops 19421724672 | bytes 47222784 | tf_op jit(solution)/shard_map/dot_general | solution.py:44
Async XLA Ops:
  6.5 98.9 %all-reduce.3.cloned.1.call-start = ((), (), s32[]{:S(2)}) async-start(), calls=%async_computation.1 | async-start | bytes 6291456 | tf_op jit(solution)/shard_map/psum | solution.py:12
  15.4 247.0 %reduce-scatter.2.cloned.1.call-start = ((), (), s32[]{:S(2)}) async-start(), calls=%async_computation.2 | async-start | bytes 14155776 | tf_op jit(solution)/shard_map/reduce_scatter | solution.py:35
  133.0 195.1 %all-gather.2.cloned.1.call-start = ((), (), s32[]{:S(2)}) async-start(), calls=%async_computation.3 | async-start | bytes 7077888 | tf_op jit(solution)/shard_map/all_gather | solution.py:42
  264.9 153.5 %all-reduce.5.cloned.1.call-start = ((), (), s32[]{:S(2)}) async-start(), calls=%async_computation.4 | async-start | bytes 6291456 | tf_op jit(solution)/shard_map/psum | solution.py:12
Sparse Core Ops, SparseCore 0:
  15.5 89.8 all-reduce.2
  133.2 129.1 reduce-scatter.1
  265.0 63.0 all-gather.1
  332.5 85.8 all-reduce.4
where the time goes:
time: 457 us
  waiting for transfers between devices  365 us (80%)
  matrix products  59.5 us (13%)
  between operations  13.2 us (3%)
  local copies, waits for them, and re-layouts  9.85 us (2%)
  other arithmetic  8.55 us (2%)
    psum x2, waiting for transfers between devices, spread(): return lax.psum(kept, axis)  175 us
    reduce_scatter x1, waiting for transfers between devices, shards(): lax.psum_scatter(partial_term(jnp.int32(0), lax.axis_size('col') * pieces...  128 us
    all_gather x1, waiting for transfers between devices, shards(): w_rows = lax.all_gather(dressed, 'col', axis=0, tiled=True)  63 us
    dot_general x1, matrix products, shards(): lax.dot_general(w_rows, w_cols, (((1,), (1,)), ((), ())), preferred_eleme...  31.9 us
    dot_general x1, matrix products, partial_term(): return jnp.dot(tile, chol_cols, preferred_element_type=jnp.float32)  27.6 us
  transfers between devices with their start and end apart: 4, of which 4 were waited for; matrix products, arithmetic and copies ran while one was open for 1% of the time, Pallas kernels for 0%

commit v1 on v0

v1 whole, which is shorter than its diff:
```python
import functools

import jax
import jax.numpy as jnp
from jax import lax
from jax.experimental import pallas as pl
from jax.experimental.pallas import tpu as pltpu
from jax.sharding import PartitionSpec as P

BF16, F32 = jnp.bfloat16, jnp.float32
VMEM_LIMIT = 56 * 1024 * 1024
SHARES = (1, 2, 1)


def spread(value, axis, source):
    kept = jnp.where(lax.axis_index(axis) == source, value, 0).astype(value.dtype)
    return lax.psum(kept, axis)


def general_shards(amplitudes, cholesky, gaps):
    rows_dev, cols_dev = amplitudes.shape
    pairs, vectors = gaps.shape[0], cholesky.shape[1]
    first_col = lax.axis_index("col") * cols_dev
    root_row = first_col // rows_dev
    offset = first_col - root_row * rows_dev
    chol_cols = spread(
        lax.dynamic_slice_in_dim(cholesky, offset, cols_dev, 0), "row", root_row
    )
    gap_rows = lax.dynamic_slice_in_dim(
        gaps, lax.axis_index("row") * rows_dev, rows_dev, 0
    )
    gap_cols = lax.dynamic_slice_in_dim(gaps, first_col, cols_dev, 0)
    pieces = rows_dev // lax.axis_size("col")
    own_rows = lax.dynamic_slice_in_dim(
        cholesky, lax.axis_index("col") * pieces, pieces, 0
    ).astype(F32)
    summed = lax.psum_scatter(
        jnp.dot(amplitudes, chol_cols, preferred_element_type=F32),
        "col",
        scatter_dimension=0,
        tiled=True,
    )
    dressed = (own_rows + summed * pairs**-0.5).astype(BF16)
    w_rows = lax.all_gather(dressed, "col", axis=0, tiled=True)
    w_cols = spread(
        lax.dynamic_slice_in_dim(w_rows, offset, cols_dev, 0), "row", root_row
    )
    product = lax.dot_general(
        w_rows, w_cols, (((1,), (1,)), ((), ())), preferred_element_type=F32
    )
    return (
        -(product * vectors**-0.5) / (gap_rows[:, None] + gap_cols[None, :])
    ).astype(BF16)


def params():
    return pltpu.CompilerParams(vmem_limit_bytes=VMEM_LIMIT)


def cost(flops, nbytes):
    return pl.CostEstimate(flops=flops, bytes_accessed=nbytes, transcendentals=0)


def partial_kernel(k_ref, a0_ref, a1_ref, c_ref, *refs):
    own_ref, oth_ref = refs[-2:]
    own_ref[...] = jnp.dot(a0_ref[...], c_ref[...], preferred_element_type=F32)
    oth_ref[...] = jnp.dot(
        a1_ref[...], c_ref[...], preferred_element_type=F32
    ).astype(BF16)


def partial_sums(core, tile, vectors, after):
    rows = tile.shape[0]
    depth, width = vectors.shape
    half = rows // 2
    step = min(256, half)
    per_half = half // step
    return pl.pallas_call(
        partial_kernel,
        grid_spec=pltpu.PrefetchScalarGridSpec(
            num_scalar_prefetch=1,
            grid=(per_half,),
            in_specs=[
                pl.BlockSpec((step, depth), lambda i, k: (k[0] * per_half + i, 0)),
                pl.BlockSpec((step, depth), lambda i, k: ((1 - k[0]) * per_half + i, 0)),
                pl.BlockSpec((depth, width), lambda i, k: (0, 0)),
            ]
            + [pl.BlockSpec(memory_space=pl.ANY)] * len(after),
            out_specs=[
                pl.BlockSpec((step, width), lambda i, k: (i, 0)),
                pl.BlockSpec((step, width), lambda i, k: (i, 0)),
            ],
        ),
        out_shape=[
            jax.ShapeDtypeStruct((half, width), F32),
            jax.ShapeDtypeStruct((half, width), BF16),
        ],
        compiler_params=params(),
        cost_estimate=cost(2 * rows * depth * max(width, 256), 2 * rows * depth + 3 * rows * width),
        name="partial_sums",
    )(core, tile, tile, vectors, *after)


def final_kernel(shares, k_ref, *refs):
    own, oth, cols = refs[:shares], refs[shares : 2 * shares], refs[2 * shares : 3 * shares]
    gr_ref, gc_ref, out_ref, w_cols, w_rows = refs[3 * shares :]
    step = pl.program_id(0)

    @pl.when(step == 0)
    def _():
        first = 0
        for c_ref in cols:
            w_cols[:, first : first + c_ref.shape[1]] = c_ref[...]
            first += c_ref.shape[1]

    mine = (2 * step) // pl.num_programs(0) == k_ref[0]
    first = 0
    for own_ref, oth_ref in zip(own, oth):
        w_rows[:, first : first + own_ref.shape[1]] = jnp.where(mine, own_ref[...], oth_ref[...])
        first += own_ref.shape[1]
    piece = min(768, w_cols.shape[0])
    for first in range(0, w_cols.shape[0], piece):
        here = slice(first, first + piece)
        product = lax.dot_general(
            w_rows[...], w_cols[here, :], (((1,), (1,)), ((), ())), preferred_element_type=F32
        )
        wide = jnp.concatenate([gr_ref[...]] * (piece // gr_ref.shape[1]), axis=1)
        out_ref[:, here] = (product / (wide + gc_ref[:, here])).astype(BF16)


def final_product(core, own, oth, cols, gap_rows, gap_cols):
    shares = len(own)
    half, width = own[0].shape[0], cols[0].shape[0]
    vectors = sum(c.shape[1] for c in cols)
    step = min(768, half)
    per_half = half // step
    return pl.pallas_call(
        functools.partial(final_kernel, shares),
        grid_spec=pltpu.PrefetchScalarGridSpec(
            num_scalar_prefetch=1,
            grid=(2 * per_half,),
            in_specs=[
                pl.BlockSpec((step, w.shape[1]), lambda i, k: (lax.rem(i, per_half), 0))
                for w in (*own, *oth)
            ]
            + [pl.BlockSpec(c.shape, lambda i, k: (0, 0)) for c in cols]
            + [
                pl.BlockSpec((step, gap_rows.shape[1]), lambda i, k: (i, 0)),
                pl.BlockSpec((1, width), lambda i, k: (0, 0)),
            ],
            out_specs=pl.BlockSpec((step, width), lambda i, k: (i, 0)),
            scratch_shapes=[
                pltpu.VMEM((width, vectors), BF16),
                pltpu.VMEM((step, vectors), BF16),
            ],
        ),
        out_shape=jax.ShapeDtypeStruct((2 * half, width), BF16),
        compiler_params=params(),
        cost_estimate=cost(4 * half * width * vectors, 4 * half * width),
        name="final_product",
    )(core, *own, *oth, *cols, gap_rows, gap_cols)


def planned_shards(amplitudes, cholesky, gaps):
    rows_dev, cols_dev = amplitudes.shape
    pairs, vectors = gaps.shape[0], cholesky.shape[1]
    n_col = lax.axis_size("col")
    planes = n_col // 2
    row, col = lax.axis_index("row"), lax.axis_index("col")
    plane, core = col // 2, col % 2
    core_arg = core.astype(jnp.int32).reshape(1)
    half = rows_dev // 2
    groups = [[2 * plane_ + core_ for plane_ in range(planes)] for core_ in range(2)]

    def in_plane(*hops):
        pairs_list = [
            ((plane_ ^ source) * n_col + 2 * plane_ + core_, (plane_ ^ target) * n_col + 2 * plane_ + core_)
            for source, target in hops
            for plane_ in range(planes)
            for core_ in range(2)
        ]
        return lambda value: lax.ppermute(value, ("row", "col"), pairs_list)

    root_x, root_y = in_plane((0, 1)), in_plane((0, 2))
    x_far, y_far = in_plane((1, 3)), in_plane((2, 3))
    swap = lambda value: lax.ppermute(value, "col", [(i, i ^ 1) for i in range(n_col)])
    is_root = row == plane

    def tied(value, others):
        return lax.optimization_barrier((value, *others))[0]

    def to_plane(low, high):
        low_x, high_y = root_x(low), root_y(high)
        low_far, high_far = x_far(low_x), y_far(high_y)
        high_x, low_y = root_x(high), root_y(low)
        everywhere = jnp.concatenate(
            [
                jnp.where(is_root, low, low_x + low_y + low_far),
                jnp.where(is_root, high, high_x + high_y + high_far),
            ],
            axis=0,
        )
        return everywhere, (low_x, high_y), (high_x, low_y)

    scale = pairs**-0.5
    gap_scale = -(vectors**0.5)
    gap_rows = lax.dynamic_slice_in_dim(gaps, row * rows_dev, rows_dev, 0) * gap_scale
    gap_rows = jnp.broadcast_to(gap_rows[:, None], (rows_dev, 128))
    gap_cols = (lax.dynamic_slice_in_dim(gaps, col * cols_dev, cols_dev, 0) * gap_scale)[None, :]

    first = 0
    own, oth, cols = [], [], []
    sent = after = hops = ()
    for share in SHARES:
        width = vectors * share // sum(SHARES)
        low = lax.dynamic_slice(cholesky, (core * half, first), (half // 2, width))
        high = lax.dynamic_slice(cholesky, (core * half + half // 2, first), (half // 2, width))
        chol_cols, _, sent = to_plane(tied(low, sent), tied(high, sent))
        mine, other = partial_sums(core_arg, amplitudes, chol_cols, after)
        pair = (mine + swap(other).astype(F32)).astype(BF16)
        summed = lax.psum_scatter(
            pair, "col", scatter_dimension=0, tiled=True, axis_index_groups=groups
        )
        piece = summed.shape[0]
        chol = lax.dynamic_slice(cholesky, (core * half + plane * piece, first), (piece, width))
        dressed = (chol.astype(F32) + tied(summed, hops).astype(F32) * scale).astype(BF16)
        w_own = lax.all_gather(dressed, "col", axis=0, tiled=True, axis_index_groups=groups)
        own.append(w_own)
        oth.append(swap(w_own))
        everywhere, early, _ = to_plane(w_own[: half // 2], w_own[half // 2 :])
        cols.append(everywhere)
        after = (pair,) if len(own) == 1 else (dressed,)
        hops = (everywhere,) if len(own) == 1 else early
        first += width
    return final_product(core_arg, own, oth, cols, gap_rows, gap_cols)


def solution(mesh):
    in_specs = (P("row", "col"), P("row", None), P())
    out_specs = P("row", "col")
    fits = (mesh.shape["row"], mesh.shape["col"]) == (4, 8)
    shards = planned_shards if fits else general_shards
    return jax.shard_map(
        shards, mesh=mesh, in_specs=in_specs, out_specs=out_specs, check_vma=False
    )
```

time: 457 us -> 374 us (0.82)
  waiting for transfers between devices: 365 us -> 84.2 us
  starting transfers between devices: 0.31 us -> 97.8 us
  Pallas kernels: 0 us -> 89.4 us
  matrix products: 59.5 us -> 0 us
  blocking collectives: 0 us -> 48.3 us
  other arithmetic: 8.55 us -> 32.2 us
    psum x2 -> x0, waiting for transfers between devices: 175 us -> none  [spread(): return lax.psum(kept, axis)]
    reduce_scatter x1 -> x3, waiting for transfers between devices: 128 us -> 15.2 us  [planned_shards(): lax.psum_scatter(pair, 'col', scatter_dimension=0, tiled=True, axis_index...]
    ppermute x0 -> x42, starting transfers between devices: none -> 97.7 us  [the longest x36 97.2 us: in_plane(): return lambda value: lax.ppermute(value, ('row', 'col'), pairs_list)]
    pallas_call x0 -> x4, Pallas kernels: none -> 89.4 us  [the longest x3 61.4 us: partial_sums(): pl.pallas_call(partial_kernel, grid_spec=pltpu.PrefetchScalarGridSpec(num...]
    ppermute x0 -> x42, waiting for transfers between devices: none -> 64.2 us  [the longest x36 61.6 us: in_plane(): return lambda value: lax.ppermute(value, ('row', 'col'), pairs_list)]
    dot_general x2 -> x0, matrix products: 59.5 us -> none  [the longest x1 31.9 us: shards(): lax.dot_general(w_rows, w_cols, (((1,), (1,)), ((), ())), preferred_eleme...]
    all_gather x1, waiting for transfers between devices: 63 us -> 4.7 us  [planned_shards(): lax.all_gather(dressed, 'col', axis=0, tiled=True, axis_index_groups=groups)]
    all_gather x0 -> x2, blocking collectives: none -> 48.3 us  [planned_shards(): lax.all_gather(dressed, 'col', axis=0, tiled=True, axis_index_groups=groups)]
  transfers between devices with their start and end apart: 4 -> 46, of which waited for: 4 -> 18; matrix products, arithmetic and copies ran while one was open for 1% -> 8% of each run, Pallas kernels for 0% -> 16%
where the time goes in v1:
time: 374 us; the launch traced here: 372 us
  starting transfers between devices  97.8 us (26%)
  Pallas kernels  89.4 us (24%)
  waiting for transfers between devices  84.2 us (23%)
  blocking collectives  48.3 us (13%)
  other arithmetic  32.2 us (9%)
  between operations  13.5 us (4%)
  local copies, waits for them, and re-layouts  6.95 us (2%)
    ppermute x36, starting transfers between devices, in_plane(): return lambda value: lax.ppermute(value, ('row', 'col'), pairs_list)  97.2 us
    ppermute x36, waiting for transfers between devices, in_plane(): return lambda value: lax.ppermute(value, ('row', 'col'), pairs_list)  61.6 us
    pallas_call x3, Pallas kernels, partial_sums(): pl.pallas_call(partial_kernel, grid_spec=pltpu.PrefetchScalarGridSpec(num...  61.4 us
    all_gather x2, blocking collectives, planned_shards(): lax.all_gather(dressed, 'col', axis=0, tiled=True, axis_index_groups=groups)  48.3 us
    pallas_call x1, Pallas kernels, final_product(): pl.pallas_call(functools.partial(final_kernel, shares), grid_spec=pltpu.P...  28 us
    reduce_scatter x3, waiting for transfers between devices, planned_shards(): lax.psum_scatter(pair, 'col', scatter_dimension=0, tiled=True, axis_index...  15.2 us
  transfers between devices with their start and end apart: 46, of which 18 were waited for; matrix products, arithmetic and copies ran while one was open for 8% of the time, Pallas kernels for 16%

profile of v1, /device:TPU:0, one launch (start us, length us, event | category | flops | bytes accessed | tf_op | source)
XLA Modules:
  0.0 372.4 jit_solution(13256690398269256666)
XLA Ops:
  8.0 4.9 %collective-permute-start.4 = (bf16[1536,128]{1,0:T(8,128)(2,1)S(1)}, bf16[1536,128]{1,0:T(8,128)(2,1)S(1)}, u32[]{:S(2)}, u32[]{:S(2)}) collective-permute-start(bf16[1536,128]{1,0:T(8,128)(2,1)S(1)} %get-tuple-element.30), channel_id=1, source_target_pairs={{0,16},{1,17},{10,26},{11,27},{20,4},{21,5},{30,14},{31,15}} | collective-permute-start | bytes 1179656 | tf_op jit(solution)/shard_map/ppermute | solution.py:182
  25.3 4.4 %collective-permute-done.1 = bf16[1536,128]{1,0:T(8,128)(2,1)} collective-permute-done((bf16[1536,128]{1,0:T(8,128)(2,1)S(1)}, bf16[1536,128]{1,0:T(8,128)(2,1)}, u32[]{:S(2)}, u32[]{:S(2)}) %collective-permute-start.1) | collective-permute-done | bytes 393248 | tf_op jit(solution)/shard_map/ppermute | solution.py:182
  29.7 5.4 %collective-permute-start.11 = (bf16[1536,256]{1,0:T(8,128)(2,1)S(1)}, bf16[1536,256]{1,0:T(8,128)(2,1)}, u32[]{:S(2)}, u32[]{:S(2)}) collective-permute-start(bf16[1536,256]{1,0:T(8,128)(2,1)S(1)} %get-tuple-element.20), channel_id=1, source_target_pairs={{0,16},{1,17},{10,26},{11,27},{20,4},{21,5},{30,14},{31,15}} | collective-permute-start | bytes 2359304 | tf_op jit(solution)/shard_map/ppermute | solution.py:182
  41.3 20.0 %partial_sums.3 = (f32[3072,128]{1,0:T(8,128)}, bf16[3072,128]{1,0:T(8,128)(2,1)}) custom-call(s32[1]{0:T(128)} %bitcast.k_ref, bf16[6144,3072]{1,0:T(8,128)(2,1)} %a1_ref.5, bf16[6144,3072]{1,0:T(8,128)(2,1)} %a1_ref.5, bf16[3072,128]{1,0:T(8,128)(2,1)} %pad_maximum_fusion.2.c_ref), custom_call_target="tpu_custom_call" | custom-call | flops 9663676416 | bytes 40108032 | tf_op jit(solution)/shard_map/partial_sums/pallas_call | solution.py:78
  61.4 5.7 %collective-permute-start.10 = (bf16[1536,256]{1,0:T(8,128)(2,1)S(1)}, bf16[1536,256]{1,0:T(8,128)(2,1)S(1)}, u32[]{:S(2)}, u32[]{:S(2)}) collective-permute-start(bf16[1536,256]{1,0:T(8,128)(2,1)S(1)} %get-tuple-element.20), channel_id=1, source_target_pairs={{0,8},{1,9},{10,2},{11,3},{20,28},{21,29},{30,22},{31,23}} | collective-permute-start | bytes 2359304 | tf_op jit(solution)/shard_map/ppermute | solution.py:182
  68.7 5.2 %collective-permute-start.8 = (bf16[1536,256]{1,0:T(8,128)(2,1)S(1)}, bf16[1536,256]{1,0:T(8,128)(2,1)}, u32[]{:S(2)}, u32[]{:S(2)}) collective-permute-start(bf16[1536,256]{1,0:T(8,128)(2,1)S(1)} %get-tuple-element.19), channel_id=1, source_target_pairs={{0,16},{1,17},{10,26},{11,27},{20,4},{21,5},{30,14},{31,15}} | collective-permute-start | bytes 2359304 | tf_op jit(solution)/shard_map/ppermute | solution.py:182
  78.0 6.5 %collective-permute-done.10 = bf16[1536,256]{1,0:T(8,128)(2,1)S(1)} collective-permute-done((bf16[1536,256]{1,0:T(8,128)(2,1)S(1)}, bf16[1536,256]{1,0:T(8,128)(2,1)S(1)}, u32[]{:S(2)}, u32[]{:S(2)}) %collective-permute-start.10) | collective-permute-done | bytes 786464 | tf_op jit(solution)/shard_map/ppermute | solution.py:182
  86.0 4.1 %collective-permute-done.8 = bf16[1536,256]{1,0:T(8,128)(2,1)} collective-permute-done((bf16[1536,256]{1,0:T(8,128)(2,1)S(1)}, bf16[1536,256]{1,0:T(8,128)(2,1)}, u32[]{:S(2)}, u32[]{:S(2)}) %collective-permute-start.8) | collective-permute-done | bytes 786464 | tf_op jit(solution)/shard_map/ppermute | solution.py:182
  93.2 21.2 %partial_sums.4 = (f32[3072,256]{1,0:T(8,128)}, bf16[3072,256]{1,0:T(8,128)(2,1)}) custom-call(s32[1]{0:T(128)} %bitcast.k_ref, bf16[6144,3072]{1,0:T(8,128)(2,1)} %a1_ref.5, bf16[6144,3072]{1,0:T(8,128)(2,1)} %a1_ref.5, bf16[3072,256]{1,0:T(8,128)(2,1)} %pad_maximum_fusion.c_ref, bf16[3072,128]{1,0:T(8,128)(2,1)} %add_convert_fusion.2.refs_0_), custom_call_target="tpu_custom_call" | custom-call | flops 9663676416 | bytes 42467328 | tf_op jit(solution)/shard_map/partial_sums/pallas_call | solution.py:78
  118.0 3.4 add_convert_fusion
  121.5 30.0 %all_gather.9.refs_0_ = bf16[3072,128]{1,0:T(8,128)(2,1)S(1)} all-gather(bf16[768,128]{1,0:T(8,128)(2,1)S(1)} %add_convert_fusion.5), channel_id=1, replica_groups={{0,2,4,6},{1,3,5,7},{8,10,12,14},{9,11,13,15},{16,18,20,22},{17,19,21,2..., dimensions={0}, use_global_device_ids=true | all-gather | bytes 983040 | tf_op jit(solution)/shard_map/all_gather | solution.py:227
  156.0 4.9 %collective-permute-done.14 = bf16[1536,128]{1,0:T(8,128)(2,1)S(1)} collective-permute-done((bf16[1536,128]{1,0:T(8,128)(2,1)S(1)}, bf16[1536,128]{1,0:T(8,128)(2,1)S(1)}, u32[]{:S(2)}, u32[]{:S(2)}) %collective-permute-start.14) | collective-permute-done | bytes 393248 | tf_op jit(solution)/shard_map/ppermute | solution.py:182
  162.3 4.4 %collective-permute-start.18 = (bf16[1536,128]{1,0:T(8,128)(2,1)S(1)}, bf16[1536,128]{1,0:T(8,128)(2,1)S(1)}, u32[]{:S(2)}, u32[]{:S(2)}) collective-permute-start(bf16[1536,128]{1,0:T(8,128)(2,1)S(1)} %get-tuple-element.40), channel_id=1, source_target_pairs={{0,16},{1,17},{10,26},{11,27},{20,4},{21,5},{30,14},{31,15}} | collective-permute-start | bytes 1179656 | tf_op jit(solution)/shard_map/ppermute | solution.py:182
  166.7 6.3 %collective-permute-start.20 = (bf16[1536,128]{1,0:T(8,128)(2,1)S(1)}, bf16[1536,128]{1,0:T(8,128)(2,1)S(1)}, u32[]{:S(2)}, u32[]{:S(2)}) collective-permute-start(bf16[1536,128]{1,0:T(8,128)(2,1)S(1)} %get-tuple-element.24), channel_id=1, source_target_pairs={{0,8},{1,9},{10,2},{11,3},{20,28},{21,29},{30,22},{31,23}} | collective-permute-start | bytes 1179656 | tf_op jit(solution)/shard_map/ppermute | solution.py:182
  175.0 3.8 %collective-permute-start.21 = (bf16[1536,128]{1,0:T(8,128)(2,1)S(1)}, bf16[1536,128]{1,0:T(8,128)(2,1)S(1)}, u32[]{:S(2)}, u32[]{:S(2)}) collective-permute-start(bf16[1536,128]{1,0:T(8,128)(2,1)S(1)} %get-tuple-element.24), channel_id=1, source_target_pairs={{0,16},{1,17},{10,26},{11,27},{20,4},{21,5},{30,14},{31,15}} | collective-permute-start | bytes 1179656 | tf_op jit(solution)/shard_map/ppermute | solution.py:182
  182.6 3.5 collective-permute-done.17
  189.3 4.4 %collective-permute-start.23 = (bf16[1536,128]{1,0:T(8,128)(2,1)S(1)}, bf16[1536,128]{1,0:T(8,128)(2,1)S(1)}, u32[]{:S(2)}, u32[]{:S(2)}) collective-permute-start(bf16[1536,128]{1,0:T(8,128)(2,1)S(1)} %get-tuple-element.25), channel_id=1, source_target_pairs={{0,8},{1,9},{10,2},{11,3},{20,28},{21,29},{30,22},{31,23}} | collective-permute-start | bytes 1179656 | tf_op jit(solution)/shard_map/ppermute | solution.py:182
  194.5 4.4 %collective-permute-done.23 = bf16[1536,128]{1,0:T(8,128)(2,1)S(1)} collective-permute-done((bf16[1536,128]{1,0:T(8,128)(2,1)S(1)}, bf16[1536,128]{1,0:T(8,128)(2,1)S(1)}, u32[]{:S(2)}, u32[]{:S(2)}) %collective-permute-start.23) | collective-permute-done | bytes 393248 | tf_op jit(solution)/shard_map/ppermute | solution.py:182
  199.9 20.2 %partial_sums.5 = (f32[3072,128]{1,0:T(8,128)}, bf16[3072,128]{1,0:T(8,128)(2,1)}) custom-call(s32[1]{0:T(128)} %bitcast.k_ref, bf16[6144,3072]{1,0:T(8,128)(2,1)} %a1_ref.5, bf16[6144,3072]{1,0:T(8,128)(2,1)} %a1_ref.5, bf16[3072,128]{1,0:T(8,128)(2,1)} %pad_maximum_fusion.4.c_ref, bf16[768,256]{1,0:T(8,128)(2,1)} %add_convert_fusion.3.refs_0_), custom_call_target="tpu_custom_call" | custom-call | flops 9663676416 | bytes 40108032 | tf_op jit(solution)/shard_map/partial_sums/pallas_call | solution.py:78
  220.1 4.7 %all-gather.2.cloned.1.call-done.refs_1_ = bf16[3072,256]{1,0:T(8,128)(2,1)} async-done(((bf16[768,256]{1,0:T(8,128)(2,1)}), bf16[3072,256]{1,0:T(8,128)(2,1)}) %all-gather.2.cloned.1.call-update) | async-done | bytes 1572880 | tf_op jit(solution)/shard_map/all_gather | solution.py:227
  226.1 4.3 %collective-permute-start.27 = (bf16[1536,256]{1,0:T(8,128)(2,1)S(1)}, bf16[1536,256]{1,0:T(8,128)(2,1)}, u32[]{:S(2)}, u32[]{:S(2)}) collective-permute-start(bf16[1536,256]{1,0:T(8,128)(2,1)S(1)} %slice.26), channel_id=1, source_target_pairs={{0,8},{1,9},{10,2},{11,3},{20,28},{21,29},{30,22},{31,23}} | collective-permute-start | bytes 2359304 | tf_op jit(solution)/shard_map/ppermute | solution.py:182
  232.5 13.6 %collective-permute-done.27 = bf16[1536,256]{1,0:T(8,128)(2,1)} collective-permute-done((bf16[1536,256]{1,0:T(8,128)(2,1)S(1)}, bf16[1536,256]{1,0:T(8,128)(2,1)}, u32[]{:S(2)}, u32[]{:S(2)}) %collective-permute-start.27) | collective-permute-done | bytes 786464 | tf_op jit(solution)/shard_map/ppermute | solution.py:182
  252.4 5.4 %collective-permute-start.28 = (bf16[1536,256]{1,0:T(8,128)(2,1)}, bf16[1536,256]{1,0:T(8,128)(2,1)}, u32[]{:S(2)}, u32[]{:S(2)}) collective-permute-start(bf16[1536,256]{1,0:T(8,128)(2,1)} %get-tuple-element.36), channel_id=1, source_target_pairs={{0,16},{1,17},{10,26},{11,27},{20,4},{21,5},{30,14},{31,15}} | collective-permute-start | bytes 2359304 | tf_op jit(solution)/shard_map/ppermute | solution.py:182
  257.7 15.2 %reduce-scatter.8.cloned.1.call-done = bf16[768,128]{1,0:T(8,128)(2,1)} async-done(((bf16[3072,128]{1,0:T(8,128)(2,1)}), bf16[768,128]{1,0:T(8,128)(2,1)}) %reduce-scatter.8.cloned.1.call-update) | async-done | bytes 196624 | tf_op jit(solution)/shard_map/reduce_scatter | solution.py:221
  275.1 18.3 %all_gather.11.refs_2_ = bf16[3072,128]{1,0:T(8,128)(2,1)S(1)} all-gather(bf16[768,128]{1,0:T(8,128)(2,1)S(1)} %add_convert_fusion.4), channel_id=1, replica_groups={{0,2,4,6},{1,3,5,7},{8,10,12,14},{9,11,13,15},{16,18,20,22},{17,19,21,2..., dimensions={0}, use_global_device_ids=true | all-gather | bytes 983040 | tf_op jit(solution)/shard_map/all_gather | solution.py:227
  293.5 3.6 collective-permute-start.36
  298.5 3.9 %collective-permute-done.36 = bf16[1536,128]{1,0:T(8,128)(2,1)S(1)} collective-permute-done((bf16[1536,128]{1,0:T(8,128)(2,1)S(1)}, bf16[1536,128]{1,0:T(8,128)(2,1)S(1)}, u32[]{:S(2)}, u32[]{:S(2)}) %collective-permute-start.36) | collective-permute-done | bytes 393248 | tf_op jit(solution)/shard_map/ppermute | solution.py:182
  303.1 5.9 %collective-permute-start.34 = (bf16[1536,256]{1,0:T(8,128)(2,1)}, bf16[1536,256]{1,0:T(8,128)(2,1)}, u32[]{:S(2)}, u32[]{:S(2)}) collective-permute-start(bf16[1536,256]{1,0:T(8,128)(2,1)} %get-tuple-element.36), channel_id=1, source_target_pairs={{0,8},{1,9},{10,2},{11,3},{20,28},{21,29},{30,22},{31,23}} | collective-permute-start | bytes 2359304 | tf_op jit(solution)/shard_map/ppermute | solution.py:182
  316.0 3.4 collective-permute-done.34
  319.4 4.4 %collective-permute-start.39 = (bf16[1536,128]{1,0:T(8,128)(2,1)}, bf16[1536,128]{1,0:T(8,128)(2,1)S(1)}, u32[]{:S(2)}, u32[]{:S(2)}) collective-permute-start(bf16[1536,128]{1,0:T(8,128)(2,1)} %get-tuple-element.38), channel_id=1, source_target_pairs={{0,8},{1,9},{10,2},{11,3},{20,28},{21,29},{30,22},{31,23}} | collective-permute-start | bytes 1179656 | tf_op jit(solution)/shard_map/ppermute | solution.py:182
  327.7 5.4 %collective-permute-done.39 = bf16[1536,128]{1,0:T(8,128)(2,1)S(1)} collective-permute-done((bf16[1536,128]{1,0:T(8,128)(2,1)}, bf16[1536,128]{1,0:T(8,128)(2,1)S(1)}, u32[]{:S(2)}, u32[]{:S(2)}) %collective-permute-start.39) | collective-permute-done | bytes 393248 | tf_op jit(solution)/shard_map/ppermute | solution.py:182
  337.9 28.0 %final_product.1 = bf16[6144,3072]{1,0:T(8,128)(2,1)} custom-call(s32[1]{0:T(128)} %bitcast.k_ref, bf16[3072,128]{1,0:T(8,128)(2,1)} %copy-done, bf16[3072,256]{1,0:T(8,128)(2,1)} %all-gather.2.cloned.1.call-done.refs_1_, bf16[3072,128]{1,0:T(8,128)(2,1)} %copy-done.1, bf16[3072,128]{1,0:T(8,128)(2,1)} %copy-done.6, bf16[3072,256]{1,0:T(8,128)(2,1)} %copy-done.5, ...), custom_call_target="tpu_custom_call" | custom-call | flops 19327352832 | bytes 37748736 | tf_op jit(solution)/shard_map/final_product/pallas_call | solution.py:137
  (118 shorter events, 80.0 us)
Async XLA Ops:
  6.5 107.9 %reduce-scatter.4.cloned.1.call-start = ((), (), s32[]{:S(2)}) async-start(), calls=%async_computation.3 | async-start | bytes 983040 | tf_op jit(solution)/shard_map/reduce_scatter | solution.py:221
  8.0 14.4 %collective-permute-start.4 = (bf16[1536,128]{1,0:T(8,128)(2,1)S(1)}, bf16[1536,128]{1,0:T(8,128)(2,1)S(1)}, u32[]{:S(2)}, u32[]{:S(2)}) collective-permute-start(bf16[1536,128]{1,0:T(8,128)(2,1)S(1)} %get-tuple-element.30), channel_id=1, source_target_pairs={{0,16},{1,17},{10,26},{11,27},{20,4},{21,5},{30,14},{31,15}} | collective-permute-start | bytes 1179656 | tf_op jit(solution)/shard_map/ppermute | solution.py:182
  12.9 12.4 %collective-permute-start.3 = (bf16[1536,128]{1,0:T(8,128)(2,1)S(1)}, bf16[1536,128]{1,0:T(8,128)(2,1)}, u32[]{:S(2)}, u32[]{:S(2)}) collective-permute-start(bf16[1536,128]{1,0:T(8,128)(2,1)S(1)} %get-tuple-element.30), channel_id=1, source_target_pairs={{0,8},{1,9},{10,2},{11,3},{20,28},{21,29},{30,22},{31,23}} | collective-permute-start | bytes 1179656 | tf_op jit(solution)/shard_map/ppermute | solution.py:182
  15.0 14.7 %collective-permute-start.1 = (bf16[1536,128]{1,0:T(8,128)(2,1)S(1)}, bf16[1536,128]{1,0:T(8,128)(2,1)}, u32[]{:S(2)}, u32[]{:S(2)}) collective-permute-start(bf16[1536,128]{1,0:T(8,128)(2,1)S(1)} %get-tuple-element.31), channel_id=1, source_target_pairs={{0,16},{1,17},{10,26},{11,27},{20,4},{21,5},{30,14},{31,15}} | collective-permute-start | bytes 1179656 | tf_op jit(solution)/shard_map/ppermute | solution.py:182
  17.0 20.2 %collective-permute-start = (bf16[1536,128]{1,0:T(8,128)(2,1)S(1)}, bf16[1536,128]{1,0:T(8,128)(2,1)}, u32[]{:S(2)}, u32[]{:S(2)}) collective-permute-start(bf16[1536,128]{1,0:T(8,128)(2,1)S(1)} %get-tuple-element.31), channel_id=1, source_target_pairs={{0,8},{1,9},{10,2},{11,3},{20,28},{21,29},{30,22},{31,23}} | collective-permute-start | bytes 1179656 | tf_op jit(solution)/shard_map/ppermute | solution.py:182
  22.4 15.5 %collective-permute-start.5 = (bf16[1536,128]{1,0:T(8,128)(2,1)S(1)}, bf16[1536,128]{1,0:T(8,128)(2,1)}, u32[]{:S(2)}, u32[]{:S(2)}) collective-permute-start(bf16[1536,128]{1,0:T(8,128)(2,1)S(1)} %collective-permute-done.4), channel_id=1, source_target_pairs={{16,24},{17,25},{26,18},{27,19},{4,12},{5,13},{14,6},{15,7}} | collective-permute-start | bytes 1179656 | tf_op jit(solution)/shard_map/ppermute | solution.py:182
  29.7 37.4 %collective-permute-start.11 = (bf16[1536,256]{1,0:T(8,128)(2,1)S(1)}, bf16[1536,256]{1,0:T(8,128)(2,1)}, u32[]{:S(2)}, u32[]{:S(2)}) collective-permute-start(bf16[1536,256]{1,0:T(8,128)(2,1)S(1)} %get-tuple-element.20), channel_id=1, source_target_pairs={{0,16},{1,17},{10,26},{11,27},{20,4},{21,5},{30,14},{31,15}} | collective-permute-start | bytes 2359304 | tf_op jit(solution)/shard_map/ppermute | solution.py:182
  35.1 38.8 %collective-permute-start.7 = (bf16[1536,256]{1,0:T(8,128)(2,1)S(1)}, bf16[1536,256]{1,0:T(8,128)(2,1)}, u32[]{:S(2)}, u32[]{:S(2)}) collective-permute-start(bf16[1536,256]{1,0:T(8,128)(2,1)S(1)} %get-tuple-element.19), channel_id=1, source_target_pairs={{0,8},{1,9},{10,2},{11,3},{20,28},{21,29},{30,22},{31,23}} | collective-permute-start | bytes 2359304 | tf_op jit(solution)/shard_map/ppermute | solution.py:182
  61.3 14.1 %collective-permute-start.6 = (bf16[3072,128]{1,0:T(8,128)(2,1)}, bf16[3072,128]{1,0:T(8,128)(2,1)S(1)}, u32[]{:S(2)}, u32[]{:S(2)}) collective-permute-start(bf16[3072,128]{1,0:T(8,128)(2,1)} %get-tuple-element.18), channel_id=1, source_target_pairs={{0,1},{1,0},{2,3},{3,2},{4,5},{5,4},{6,7},{7,6},{8,9},{9,8},{10,11... | collective-permute-start | bytes 2359304 | tf_op jit(solution)/shard_map/ppermute | solution.py:186
  61.4 23.2 %collective-permute-start.10 = (bf16[1536,256]{1,0:T(8,128)(2,1)S(1)}, bf16[1536,256]{1,0:T(8,128)(2,1)S(1)}, u32[]{:S(2)}, u32[]{:S(2)}) collective-permute-start(bf16[1536,256]{1,0:T(8,128)(2,1)S(1)} %get-tuple-element.20), channel_id=1, source_target_pairs={{0,8},{1,9},{10,2},{11,3},{20,28},{21,29},{30,22},{31,23}} | collective-permute-start | bytes 2359304 | tf_op jit(solution)/shard_map/ppermute | solution.py:182
  67.1 17.4 %collective-permute-start.12 = (bf16[1536,256]{1,0:T(8,128)(2,1)}, bf16[1536,256]{1,0:T(8,128)(2,1)}, u32[]{:S(2)}, u32[]{:S(2)}) collective-permute-start(bf16[1536,256]{1,0:T(8,128)(2,1)} %collective-permute-done.11), channel_id=1, source_target_pairs={{16,24},{17,25},{26,18},{27,19},{4,12},{5,13},{14,6},{15,7}} | collective-permute-start | bytes 2359304 | tf_op jit(solution)/shard_map/ppermute | solution.py:182
  68.7 21.5 %collective-permute-start.8 = (bf16[1536,256]{1,0:T(8,128)(2,1)S(1)}, bf16[1536,256]{1,0:T(8,128)(2,1)}, u32[]{:S(2)}, u32[]{:S(2)}) collective-permute-start(bf16[1536,256]{1,0:T(8,128)(2,1)S(1)} %get-tuple-element.19), channel_id=1, source_target_pairs={{0,16},{1,17},{10,26},{11,27},{20,4},{21,5},{30,14},{31,15}} | collective-permute-start | bytes 2359304 | tf_op jit(solution)/shard_map/ppermute | solution.py:182
  73.9 16.3 %collective-permute-start.9 = (bf16[1536,256]{1,0:T(8,128)(2,1)}, bf16[1536,256]{1,0:T(8,128)(2,1)}, u32[]{:S(2)}, u32[]{:S(2)}) collective-permute-start(bf16[1536,256]{1,0:T(8,128)(2,1)} %collective-permute-done.7), channel_id=1, source_target_pairs={{8,24},{9,25},{2,18},{3,19},{28,12},{29,13},{22,6},{23,7}} | collective-permute-start | bytes 2359304 | tf_op jit(solution)/shard_map/ppermute | solution.py:182
  77.9 109.3 %reduce-scatter.6.cloned.1.call-start = ((), (), s32[]{:S(2)}) async-start(), calls=%async_computation.4 | async-start | bytes 1966080 | tf_op jit(solution)/shard_map/reduce_scatter | solution.py:221
  121.5 103.3 %all-gather.2.cloned.1.call-start = ((), (), s32[]{:S(2)}) async-start(), calls=%async_computation.5 | async-start | bytes 1966080 | tf_op jit(solution)/shard_map/all_gather | solution.py:227
  166.7 15.3 %collective-permute-start.20 = (bf16[1536,128]{1,0:T(8,128)(2,1)S(1)}, bf16[1536,128]{1,0:T(8,128)(2,1)S(1)}, u32[]{:S(2)}, u32[]{:S(2)}) collective-permute-start(bf16[1536,128]{1,0:T(8,128)(2,1)S(1)} %get-tuple-element.24), channel_id=1, source_target_pairs={{0,8},{1,9},{10,2},{11,3},{20,28},{21,29},{30,22},{31,23}} | collective-permute-start | bytes 1179656 | tf_op jit(solution)/shard_map/ppermute | solution.py:182
  173.0 13.2 %collective-permute-start.17 = (bf16[1536,128]{1,0:T(8,128)(2,1)S(1)}, bf16[1536,128]{1,0:T(8,128)(2,1)S(1)}, u32[]{:S(2)}, u32[]{:S(2)}) collective-permute-start(bf16[1536,128]{1,0:T(8,128)(2,1)S(1)} %get-tuple-element.40), channel_id=1, source_target_pairs={{0,8},{1,9},{10,2},{11,3},{20,28},{21,29},{30,22},{31,23}} | collective-permute-start | bytes 1179656 | tf_op jit(solution)/shard_map/ppermute | solution.py:182
  175.0 19.3 %collective-permute-start.21 = (bf16[1536,128]{1,0:T(8,128)(2,1)S(1)}, bf16[1536,128]{1,0:T(8,128)(2,1)S(1)}, u32[]{:S(2)}, u32[]{:S(2)}) collective-permute-start(bf16[1536,128]{1,0:T(8,128)(2,1)S(1)} %get-tuple-element.24), channel_id=1, source_target_pairs={{0,16},{1,17},{10,26},{11,27},{20,4},{21,5},{30,14},{31,15}} | collective-permute-start | bytes 1179656 | tf_op jit(solution)/shard_map/ppermute | solution.py:182
  178.8 14.8 %collective-permute-start.24 = (bf16[1536,128]{1,0:T(8,128)(2,1)S(1)}, bf16[1536,128]{1,0:T(8,128)(2,1)S(1)}, u32[]{:S(2)}, u32[]{:S(2)}) collective-permute-start(bf16[1536,128]{1,0:T(8,128)(2,1)S(1)} %get-tuple-element.25), channel_id=1, source_target_pairs={{0,16},{1,17},{10,26},{11,27},{20,4},{21,5},{30,14},{31,15}} | collective-permute-start | bytes 1179656 | tf_op jit(solution)/shard_map/ppermute | solution.py:182
  182.0 12.4 %collective-permute-start.22 = (bf16[1536,128]{1,0:T(8,128)(2,1)S(1)}, bf16[1536,128]{1,0:T(8,128)(2,1)S(1)}, u32[]{:S(2)}, u32[]{:S(2)}) collective-permute-start(bf16[1536,128]{1,0:T(8,128)(2,1)S(1)} %collective-permute-done.20), channel_id=1, source_target_pairs={{8,24},{9,25},{2,18},{3,19},{28,12},{29,13},{22,6},{23,7}} | collective-permute-start | bytes 1179656 | tf_op jit(solution)/shard_map/ppermute | solution.py:182
  189.2 83.8 %reduce-scatter.8.cloned.1.call-start = ((), (), s32[]{:S(2)}) async-start(), calls=%async_computation.6 | async-start | bytes 983040 | tf_op jit(solution)/shard_map/reduce_scatter | solution.py:221
  226.1 20.0 %collective-permute-start.27 = (bf16[1536,256]{1,0:T(8,128)(2,1)S(1)}, bf16[1536,256]{1,0:T(8,128)(2,1)}, u32[]{:S(2)}, u32[]{:S(2)}) collective-permute-start(bf16[1536,256]{1,0:T(8,128)(2,1)S(1)} %slice.26), channel_id=1, source_target_pairs={{0,8},{1,9},{10,2},{11,3},{20,28},{21,29},{30,22},{31,23}} | collective-permute-start | bytes 2359304 | tf_op jit(solution)/shard_map/ppermute | solution.py:182
  230.4 17.3 %collective-permute-start.26 = (bf16[3072,128]{1,0:T(8,128)(2,1)}, bf16[3072,128]{1,0:T(8,128)(2,1)S(1)}, u32[]{:S(2)}, u32[]{:S(2)}) collective-permute-start(bf16[3072,128]{1,0:T(8,128)(2,1)} %get-tuple-element.27), channel_id=1, source_target_pairs={{0,1},{1,0},{2,3},{3,2},{4,5},{5,4},{6,7},{7,6},{8,9},{9,8},{10,11... | collective-permute-start | bytes 2359304 | tf_op jit(solution)/shard_map/ppermute | solution.py:186
  230.4 19.0 %collective-permute-start.32 = (bf16[1536,256]{1,0:T(8,128)(2,1)S(1)}, bf16[1536,256]{1,0:T(8,128)(2,1)}, u32[]{:S(2)}, u32[]{:S(2)}) collective-permute-start(bf16[1536,256]{1,0:T(8,128)(2,1)S(1)} %slice.26), channel_id=1, source_target_pairs={{0,16},{1,17},{10,26},{11,27},{20,4},{21,5},{30,14},{31,15}} | collective-permute-start | bytes 2359304 | tf_op jit(solution)/shard_map/ppermute | solution.py:182
  252.4 21.7 %collective-permute-start.28 = (bf16[1536,256]{1,0:T(8,128)(2,1)}, bf16[1536,256]{1,0:T(8,128)(2,1)}, u32[]{:S(2)}, u32[]{:S(2)}) collective-permute-start(bf16[1536,256]{1,0:T(8,128)(2,1)} %get-tuple-element.36), channel_id=1, source_target_pairs={{0,16},{1,17},{10,26},{11,27},{20,4},{21,5},{30,14},{31,15}} | collective-permute-start | bytes 2359304 | tf_op jit(solution)/shard_map/ppermute | solution.py:182
  297.2 13.4 %collective-permute-start.37 = (bf16[1536,128]{1,0:T(8,128)(2,1)S(1)}, bf16[1536,128]{1,0:T(8,128)(2,1)S(1)}, u32[]{:S(2)}, u32[]{:S(2)}) collective-permute-start(bf16[1536,128]{1,0:T(8,128)(2,1)S(1)} %slice.28), channel_id=1, source_target_pairs={{0,16},{1,17},{10,26},{11,27},{20,4},{21,5},{30,14},{31,15}} | collective-permute-start | bytes 1179656 | tf_op jit(solution)/shard_map/ppermute | solution.py:182
  303.1 16.3 %collective-permute-start.34 = (bf16[1536,256]{1,0:T(8,128)(2,1)}, bf16[1536,256]{1,0:T(8,128)(2,1)}, u32[]{:S(2)}, u32[]{:S(2)}) collective-permute-start(bf16[1536,256]{1,0:T(8,128)(2,1)} %get-tuple-element.36), channel_id=1, source_target_pairs={{0,8},{1,9},{10,2},{11,3},{20,28},{21,29},{30,22},{31,23}} | collective-permute-start | bytes 2359304 | tf_op jit(solution)/shard_map/ppermute | solution.py:182
  311.4 12.4 %collective-permute-start.40 = (bf16[1536,128]{1,0:T(8,128)(2,1)}, bf16[1536,128]{1,0:T(8,128)(2,1)}, u32[]{:S(2)}, u32[]{:S(2)}) collective-permute-start(bf16[1536,128]{1,0:T(8,128)(2,1)} %get-tuple-element.38), channel_id=1, source_target_pairs={{0,16},{1,17},{10,26},{11,27},{20,4},{21,5},{30,14},{31,15}} | collective-permute-start | bytes 1179656 | tf_op jit(solution)/shard_map/ppermute | solution.py:182
  315.5 19.7 %collective-permute-start.29 = (bf16[3072,128]{1,0:T(8,128)(2,1)S(1)}, bf16[3072,128]{1,0:T(8,128)(2,1)S(1)}, u32[]{:S(2)}, u32[]{:S(2)}) collective-permute-start(bf16[3072,128]{1,0:T(8,128)(2,1)S(1)} %all_gather.9.refs_0_), channel_id=1, source_target_pairs={{0,1},{1,0},{2,3},{3,2},{4,5},{5,4},{6,7},{7,6},{8,9},{9,8},{10,11... | collective-permute-start | bytes 2359304 | tf_op jit(solution)/shard_map/ppermute | solution.py:186
  315.5 19.7 %collective-permute-start.30 = (bf16[3072,256]{1,0:T(8,128)(2,1)S(1)}, bf16[3072,256]{1,0:T(8,128)(2,1)S(1)}, u32[]{:S(2)}, u32[]{:S(2)}) collective-permute-start(bf16[3072,256]{1,0:T(8,128)(2,1)S(1)} %copy-done.2), channel_id=1, source_target_pairs={{0,1},{1,0},{2,3},{3,2},{4,5},{5,4},{6,7},{7,6},{8,9},{9,8},{10,11... | collective-permute-start | bytes 4718600 | tf_op jit(solution)/shard_map/ppermute | solution.py:186
  319.4 15.9 %collective-permute-start.31 = (bf16[3072,128]{1,0:T(8,128)(2,1)S(1)}, bf16[3072,128]{1,0:T(8,128)(2,1)S(1)}, u32[]{:S(2)}, u32[]{:S(2)}) collective-permute-start(bf16[3072,128]{1,0:T(8,128)(2,1)S(1)} %all_gather.11.refs_2_), channel_id=1, source_target_pairs={{0,1},{1,0},{2,3},{3,2},{4,5},{5,4},{6,7},{7,6},{8,9},{9,8},{10,11... | collective-permute-start | bytes 2359304 | tf_op jit(solution)/shard_map/ppermute | solution.py:186
  319.4 13.7 %collective-permute-start.39 = (bf16[1536,128]{1,0:T(8,128)(2,1)}, bf16[1536,128]{1,0:T(8,128)(2,1)S(1)}, u32[]{:S(2)}, u32[]{:S(2)}) collective-permute-start(bf16[1536,128]{1,0:T(8,128)(2,1)} %get-tuple-element.38), channel_id=1, source_target_pairs={{0,8},{1,9},{10,2},{11,3},{20,28},{21,29},{30,22},{31,23}} | collective-permute-start | bytes 1179656 | tf_op jit(solution)/shard_map/ppermute | solution.py:182
  (22 other events, 349.5 us)
Sparse Core Ops, SparseCore 0:
  78.0 23.5 reduce-scatter.3
  121.6 45.1 reduce-scatter.5
  189.3 35.4 all-gather.1
  248.9 24.0 reduce-scatter.7

commit v2 on v1

v2 whole, which is shorter than its diff:
```python
import functools

import jax
import jax.numpy as jnp
from jax import lax
from jax.experimental import pallas as pl
from jax.experimental.pallas import tpu as pltpu
from jax.sharding import PartitionSpec as P

BF16, F32 = jnp.bfloat16, jnp.float32
VMEM_LIMIT = 56 * 1024 * 1024
CHUNKS = 4


def spread(value, axis, source):
    kept = jnp.where(lax.axis_index(axis) == source, value, 0).astype(value.dtype)
    return lax.psum(kept, axis)


def general_shards(amplitudes, cholesky, gaps):
    rows_dev, cols_dev = amplitudes.shape
    pairs, vectors = gaps.shape[0], cholesky.shape[1]
    first_col = lax.axis_index("col") * cols_dev
    root_row = first_col // rows_dev
    offset = first_col - root_row * rows_dev
    chol_cols = spread(
        lax.dynamic_slice_in_dim(cholesky, offset, cols_dev, 0), "row", root_row
    )
    gap_rows = lax.dynamic_slice_in_dim(
        gaps, lax.axis_index("row") * rows_dev, rows_dev, 0
    )
    gap_cols = lax.dynamic_slice_in_dim(gaps, first_col, cols_dev, 0)
    pieces = rows_dev // lax.axis_size("col")
    own_rows = lax.dynamic_slice_in_dim(
        cholesky, lax.axis_index("col") * pieces, pieces, 0
    ).astype(F32)
    summed = lax.psum_scatter(
        jnp.dot(amplitudes, chol_cols, preferred_element_type=F32),
        "col",
        scatter_dimension=0,
        tiled=True,
    )
    dressed = (own_rows + summed * pairs**-0.5).astype(BF16)
    w_rows = lax.all_gather(dressed, "col", axis=0, tiled=True)
    w_cols = spread(
        lax.dynamic_slice_in_dim(w_rows, offset, cols_dev, 0), "row", root_row
    )
    product = lax.dot_general(
        w_rows, w_cols, (((1,), (1,)), ((), ())), preferred_element_type=F32
    )
    return (
        -(product * vectors**-0.5) / (gap_rows[:, None] + gap_cols[None, :])
    ).astype(BF16)


def params():
    return pltpu.CompilerParams(vmem_limit_bytes=VMEM_LIMIT)


def cost(flops, nbytes):
    return pl.CostEstimate(flops=flops, bytes_accessed=nbytes, transcendentals=0)


def partial_kernel(where_ref, a0_ref, a1_ref, *refs):
    lows, highs = refs[:4], refs[4:8]
    own_ref, oth_ref, c_ref, sems = refs[-4:]
    part = c_ref.shape[0] // 2

    @pl.when(pl.program_id(0) == 0)
    def _():
        for corner in range(4):

            @pl.when(where_ref[1] == corner)
            def _():
                low = pltpu.make_async_copy(lows[corner], c_ref.at[pl.ds(0, part)], sems.at[0])
                high = pltpu.make_async_copy(highs[corner], c_ref.at[pl.ds(part, part)], sems.at[1])
                low.start()
                high.start()
                low.wait()
                high.wait()

    own_ref[...] = jnp.dot(a0_ref[...], c_ref[...], preferred_element_type=F32)
    oth_ref[...] = jnp.dot(
        a1_ref[...], c_ref[...], preferred_element_type=F32
    ).astype(BF16)


TOKEN = jax.ShapeDtypeStruct((8, 128), F32)


def partial_sums(place, tile, lows, highs, start, size, after):
    rows, depth = tile.shape
    width = lows[0].shape[1]
    half = rows // 2
    step = size // 2
    first, per_half = start // step, half // step
    return pl.pallas_call(
        partial_kernel,
        grid_spec=pltpu.PrefetchScalarGridSpec(
            num_scalar_prefetch=1,
            grid=(size // step,),
            in_specs=[
                pl.BlockSpec((step, depth), lambda i, k: (k[0] * per_half + first + i, 0)),
                pl.BlockSpec((step, depth), lambda i, k: ((1 - k[0]) * per_half + first + i, 0)),
            ]
            + [pl.BlockSpec(memory_space=pl.ANY)] * (8 + len(after)),
            out_specs=[
                pl.BlockSpec((step, width), lambda i, k: (i, 0)),
                pl.BlockSpec((step, width), lambda i, k: (i, 0)),
            ],
            scratch_shapes=[
                pltpu.VMEM((depth, width), BF16),
                pltpu.SemaphoreType.DMA((2,)),
            ],
        ),
        out_shape=[
            jax.ShapeDtypeStruct((size, width), F32),
            jax.ShapeDtypeStruct((size, width), BF16),
        ],
        compiler_params=params(),
        cost_estimate=cost(4 * size * depth * width, 4 * size * (depth + 3 * width)),
        name="partial_sums",
    )(place, tile, tile, *lows, *highs, *after)


def block_out(rows, cols, gap_rows, gap_cols):
    product = lax.dot_general(
        rows, cols, (((1,), (1,)), ((), ())), preferred_element_type=F32
    )
    wide = jnp.concatenate([gap_rows] * (product.shape[1] // gap_rows.shape[1]), axis=1)
    return (product / (wide + gap_cols)).astype(BF16)


def new_rows_kernel(k_ref, own_ref, oth_ref, cols_ref, gr_ref, gc_ref, *refs):
    out_ref, wr_ref, token_ref = refs[-3:]
    token_ref[...] = jnp.zeros_like(token_ref)
    piece = own_ref.shape[0]
    wr_ref[...] = jnp.where(pl.program_id(0) == 0, own_ref[...], oth_ref[...])
    for first in range(0, cols_ref.shape[0], piece):
        here = slice(first, first + piece)
        out_ref[:, here] = block_out(wr_ref[...], cols_ref[here, :], gr_ref[...], gc_ref[:, here])


def new_rows(core, own, oth, cols, gap_rows, gap_cols, start, width, state, shape, after):
    rows, total_cols = shape
    size, vectors = own.shape
    per_half = rows // 2 // size
    first = start // size

    def row(i, k):
        return lax.rem(k[0] + i, 2) * per_half + first

    return pl.pallas_call(
        new_rows_kernel,
        grid_spec=pltpu.PrefetchScalarGridSpec(
            num_scalar_prefetch=1,
            grid=(2,),
            in_specs=[
                pl.BlockSpec((size, vectors), lambda i, k: (0, 0)),
                pl.BlockSpec((size, vectors), lambda i, k: (0, 0)),
                pl.BlockSpec((width, vectors), lambda i, k: (0, 0)),
                pl.BlockSpec((size, gap_rows.shape[1]), lambda i, k: (row(i, k), 0)),
                pl.BlockSpec((1, width), lambda i, k: (0, 0)),
            ]
            + [pl.BlockSpec(memory_space=pl.ANY)] * (len(state) + len(after)),
            out_specs=[
                pl.BlockSpec((size, width), lambda i, k: (row(i, k), 0)),
                pl.BlockSpec((size, vectors), lambda i, k: (row(i, k), 0)),
                pl.BlockSpec((8, 128), lambda i, k: (0, 0)),
            ],
        ),
        out_shape=[
            jax.ShapeDtypeStruct((rows, total_cols), BF16),
            jax.ShapeDtypeStruct((rows, vectors), BF16),
            TOKEN,
        ],
        input_output_aliases={6: 0, 7: 1} if state else {},
        compiler_params=params(),
        cost_estimate=cost(4 * size * width * vectors, 4 * size * width + 2 * width * vectors),
        name="new_rows",
    )(core, own, oth, cols, gap_rows, gap_cols, *state, *after)


def new_cols_kernel(wr_ref, cols_ref, gr_ref, gc_ref, *refs):
    out_ref, wc_ref, token_ref = refs[-3:]
    token_ref[...] = jnp.zeros_like(token_ref)
    out_ref[...] = block_out(wr_ref[...], cols_ref[...], gr_ref[...], gc_ref[...])
    wc_ref[...] = cols_ref[...]


def new_cols(wr, cols, gap_rows, gap_cols, start, out, wc, after):
    rows, vectors = wr.shape
    size = cols.shape[0]
    half, chunks = rows // 2 // size, start // size + 1
    wide = max(d for d in (1, 2) if chunks % d == 0 and half % d == 0)
    tm = wide * size
    per_half, count = half // wide, chunks // wide

    def row(i):
        return (i // count) * per_half + lax.rem(i, count)

    place = start // size
    more = [] if wc is None else [wc]
    return pl.pallas_call(
        new_cols_kernel,
        grid=(2 * count,),
        in_specs=[
            pl.BlockSpec((tm, vectors), lambda i: (row(i), 0)),
            pl.BlockSpec((size, vectors), lambda i: (0, 0)),
            pl.BlockSpec((tm, gap_rows.shape[1]), lambda i: (row(i), 0)),
            pl.BlockSpec((1, size), lambda i: (0, place)),
        ]
        + [pl.BlockSpec(memory_space=pl.ANY)] * (1 + len(more) + len(after)),
        out_specs=[
            pl.BlockSpec((tm, size), lambda i: (row(i), place)),
            pl.BlockSpec((size, vectors), lambda i: (place, 0)),
            pl.BlockSpec((8, 128), lambda i: (0, 0)),
        ],
        out_shape=[
            jax.ShapeDtypeStruct(out.shape, BF16),
            jax.ShapeDtypeStruct((out.shape[1], vectors), BF16),
            TOKEN,
        ],
        input_output_aliases={4: 0, 5: 1} if more else {4: 0},
        compiler_params=params(),
        cost_estimate=cost(4 * (start + size) * size * vectors, 8 * (start + size) * (size + vectors)),
        name="new_cols",
    )(wr, cols, gap_rows, gap_cols, out, *more, *after)


def last_cols_kernel(wr_ref, c0_ref, c1_ref, gr_ref, gc_ref, *refs):
    out_ref = refs[-1]
    size = c0_ref.shape[0]
    for i, c_ref in enumerate((c0_ref, c1_ref)):
        here = slice(i * size, (i + 1) * size)
        out_ref[:, here] = block_out(wr_ref[...], c_ref[...], gr_ref[...], gc_ref[:, here])


def last_cols(wr, cols, gap_rows, gap_cols, start, out, after):
    rows, vectors = wr.shape
    size = cols[0].shape[0]
    place = start // (2 * size)
    return pl.pallas_call(
        last_cols_kernel,
        grid=(rows // size,),
        in_specs=[
            pl.BlockSpec((size, vectors), lambda i: (i, 0)),
            pl.BlockSpec((size, vectors), lambda i: (0, 0)),
            pl.BlockSpec((size, vectors), lambda i: (0, 0)),
            pl.BlockSpec((size, gap_rows.shape[1]), lambda i: (i, 0)),
            pl.BlockSpec((1, 2 * size), lambda i: (0, place)),
        ]
        + [pl.BlockSpec(memory_space=pl.ANY)] * (1 + len(after)),
        out_specs=pl.BlockSpec((size, 2 * size), lambda i: (i, place)),
        out_shape=jax.ShapeDtypeStruct(out.shape, BF16),
        input_output_aliases={5: 0},
        compiler_params=params(),
        cost_estimate=cost(4 * rows * size * vectors, 4 * rows * size),
        name="last_cols",
    )(wr, *cols, gap_rows, gap_cols, out, *after)


def planned_shards(amplitudes, cholesky, gaps):
    rows_dev, cols_dev = amplitudes.shape
    pairs, vectors = gaps.shape[0], cholesky.shape[1]
    n_col = lax.axis_size("col")
    planes = n_col // 2
    row, col = lax.axis_index("row"), lax.axis_index("col")
    plane, core = col // 2, col % 2
    core_arg = core.astype(jnp.int32).reshape(1)
    half = rows_dev // 2

    def in_plane(*hops):
        pairs_list = [
            ((plane_ ^ source) * n_col + 2 * plane_ + core_, (plane_ ^ target) * n_col + 2 * plane_ + core_)
            for source, target in hops
            for plane_ in range(planes)
            for core_ in range(2)
        ]
        return lambda value: lax.ppermute(value, ("row", "col"), pairs_list)

    def in_line(*hops):
        pairs_list = [(2 * a + core_, 2 * b + core_) for a, b in hops for core_ in range(2)]
        return lambda value: lax.ppermute(value, "col", pairs_list)

    root_x, root_y = in_plane((0, 1)), in_plane((0, 2))
    x_far, y_far = in_plane((1, 3)), in_plane((2, 3))
    outer = in_line((0, 1), (1, 0), (2, 3), (3, 2))
    middle = in_line((1, 2), (2, 1))
    swap = lambda value: lax.ppermute(value, "col", [(i, i ^ 1) for i in range(n_col)])
    is_root = row == plane
    in_middle = (plane == 1) | (plane == 2)

    scale = pairs**-0.5
    gap_scale = -(vectors**0.5)
    gap_rows = lax.dynamic_slice_in_dim(gaps, row * rows_dev, rows_dev, 0) * gap_scale
    gap_rows = jnp.broadcast_to(gap_rows[:, None], (rows_dev, 128))
    gap_cols = (lax.dynamic_slice_in_dim(gaps, col * cols_dev, cols_dev, 0) * gap_scale)[None, :]

    part = cols_dev // 2
    low = lax.dynamic_slice_in_dim(cholesky, core * cols_dev, part, 0)
    high = lax.dynamic_slice_in_dim(cholesky, core * cols_dev + part, part, 0)
    low_x, high_y = root_x(low), root_y(high)
    high_x, low_y = root_x(high), root_y(low)
    low_x, gap_rows, gap_cols = lax.optimization_barrier((low_x, gap_rows, gap_cols))
    lows = [low, low_x, low_y, x_far(low_x)]
    highs = [high, high_x, high_y, y_far(high_y)]
    place_arg = jnp.stack([core, row ^ plane]).astype(jnp.int32)

    count = CHUNKS
    size = half // count

    def sums(i, after):
        return partial_sums(place_arg, amplitudes, lows, highs, i * size, size, after)

    def rows(c, known, after, state):
        return new_rows(
            core_arg, final[c], across[c], known, gap_rows, gap_cols,
            c * size, size * min(max(c, 1), count - 2), state, amplitudes.shape, after,
        )

    none = [None] * (count + 4)
    own, mine, dressed, final, cols = (list(none) for _ in range(5))
    sent, other, across, from_x, from_y, from_e, from_m, passed, token = ({} for _ in range(9))
    own[0], first = sums(0, [])
    other[0] = swap(first)
    out = wr = wc = None
    for t in range(count + 3):
        moved, sends = [], []

        def keep(place, key, value):
            place[key] = value
            moved.append((place, key))

        def move(place, key, transfer, value):
            keep(place, key, transfer(value))
            sends.append(value)

        send = None
        if 0 <= t - 2 < count:
            c = t - 2
            chol = lax.dynamic_slice_in_dim(cholesky, core * half + c * size, size, 0)
            total = mine[c].astype(F32) + from_e[c].astype(F32) + from_m[c].astype(F32)
            dressed[c] = send = (chol.astype(F32) + total * scale).astype(BF16)
        if t < count:
            if t == 1:
                other[1] = swap(sent[1])
            mine[t] = (own[t] + other[t].astype(F32)).astype(BF16)
            send = mine[t] if send is None else jnp.where(in_middle, send, mine[t])
        both = None
        if 0 <= t - 1 < count:
            both = (mine[t - 1].astype(F32) + from_e[t - 1].astype(F32)).astype(BF16)
        arrived = from_e.get(t - 1)
        if both is not None and send is not None and t >= 3:
            send, both, arrived = lax.optimization_barrier((send, both, arrived))
        elif send is not None and t >= 3:
            send, arrived = lax.optimization_barrier((send, arrived))
        if send is not None:
            move(from_e, t, outer, send)
        if both is not None:
            move(from_m, t - 1, middle, both)
        c = t - 3
        if 0 <= c < count:
            final[c] = jnp.where(in_middle, dressed[c], arrived)
            move(across, c, swap, final[c])
            if c < count - 1:
                move(from_x, c, root_x, final[c])
                move(from_y, c, root_y, final[c])
            else:
                low_x, high_y = root_x(final[c][: size // 2]), root_y(final[c][size // 2 :])
        if 0 <= t - 4 < count - 2:
            move(passed, t - 4, x_far, from_x[t - 4])
        if 1 <= t < count - 1:
            keep(other, t + 1, swap(sent[t + 1]))
        for i in (1, 2) if t == 0 else (t + 2,):
            if i < count:
                own[i], first = sums(i, sends)
                keep(sent, i, first)
        if t >= 5:
            c = t - 5
            cols[c] = jnp.where(is_root, final[c], from_x[c] + from_y[c] + passed[c])
            before = [*sends, *token.values()]
            if c == 0:
                out, wr, _ = rows(0, cols[0], before, [])
            out, wc, last = new_cols(wr, cols[c], gap_rows, gap_cols, c * size, out, wc, before)
            if t < count + 2:
                out, wr, last = rows(c + 1, wc, before, [out, wr])
                keep(token, 0, last)
        if t < count + 2:
            held = lax.optimization_barrier(tuple(place[key] for place, key in moved))
            for (place, key), value in zip(moved, held):
                place[key] = value
    c = count - 1
    low_far, high_far = x_far(from_x[c - 1][: size // 2]), y_far(from_y[c - 1][size // 2 :])
    low_x, high_y, low_far, high_far, final[c], across[c], last = lax.optimization_barrier(
        (low_x, high_y, low_far, high_far, final[c], across[c], last)
    )
    passed[c - 1] = jnp.concatenate([low_far, high_far], axis=0)
    low, high = final[c][: size // 2], final[c][size // 2 :]
    high_x, low_y = root_x(high), root_y(low)
    low_far, high_far = x_far(low_x), y_far(high_y)
    out, wr, _ = rows(c - 1, wc, [last, low_x, high_y], [out, wr])
    out, wr, last = rows(c, wc, [], [out, wr])
    high_x, low_y, low_far, high_far, last = lax.optimization_barrier(
        (high_x, low_y, low_far, high_far, last)
    )
    cols[c] = jnp.concatenate(
        [
            jnp.where(is_root, low, low_x + low_y + low_far),
            jnp.where(is_root, high, high_x + high_y + high_far),
        ],
        axis=0,
    )
    c = count - 2
    cols[c] = jnp.where(is_root, final[c], from_x[c] + from_y[c] + passed[c])
    return last_cols(wr, cols[c : c + 2], gap_rows, gap_cols, c * size, out, [last])


def solution(mesh):
    in_specs = (P("row", "col"), P("row", None), P())
    out_specs = P("row", "col")
    fits = (mesh.shape["row"], mesh.shape["col"]) == (4, 8)
    shards = planned_shards if fits else general_shards
    return jax.shard_map(
        shards, mesh=mesh, in_specs=in_specs, out_specs=out_specs, check_vma=False
    )
```

time: 374 us -> 328 us (0.88)
  blocking collectives: 48.3 us -> 0 us
  waiting for transfers between devices: 84.2 us -> 116 us
  starting transfers between devices: 97.8 us -> 72.2 us
  between operations: 13.5 us -> 0.67 us
  Pallas kernels: 89.4 us -> 96.1 us
    all_gather x2 -> x0, blocking collectives: 48.3 us -> none  [planned_shards(): lax.all_gather(dressed, 'col', axis=0, tiled=True, axis_index_groups=groups)]
    ppermute x36 -> x22, starting transfers between devices: 97.2 us -> 53.6 us  [in_plane(): return lambda value: lax.ppermute(value, ('row', 'col'), pairs_list)]
    ppermute x0 -> x10, waiting for transfers between devices: none -> 30.4 us  [in_line(): return lambda value: lax.ppermute(value, 'col', pairs_list)]
    pallas_call x1 -> x7, Pallas kernels: 28 us -> 49.8 us  [the longest x4 22.1 us: new_rows(): pl.pallas_call(new_rows_kernel, grid_spec=pltpu.PrefetchScalarGridSpec(nu...]
    ppermute x36 -> x22, waiting for transfers between devices: 61.6 us -> 82.8 us  [in_plane(): return lambda value: lax.ppermute(value, ('row', 'col'), pairs_list)]
    ppermute x0 -> x10, starting transfers between devices: none -> 17.9 us  [in_line(): return lambda value: lax.ppermute(value, 'col', pairs_list)]
    reduce_scatter x3 -> x0, waiting for transfers between devices: 15.2 us -> none  [planned_shards(): lax.psum_scatter(pair, 'col', scatter_dimension=0, tiled=True, axis_index...]
    pallas_call x3 -> x4, Pallas kernels: 61.4 us -> 46.3 us  [partial_sums(): pl.pallas_call(partial_kernel, grid_spec=pltpu.PrefetchScalarGridSpec(num...]
  transfers between devices with their start and end apart: 46 -> 40, of which waited for: 18 -> 12; matrix products, arithmetic and copies ran while one was open for 8% -> 6% of each run, Pallas kernels for 16% -> 21%
where the time goes in v2:
time: 328 us; the launch traced here: 327 us
  waiting for transfers between devices  116 us (35%)
  Pallas kernels  96.1 us (29%)
  starting transfers between devices  72.2 us (22%)
  other arithmetic  33.2 us (10%)
  local copies, waits for them, and re-layouts  9.1 us (3%)
    ppermute x22, waiting for transfers between devices, in_plane(): return lambda value: lax.ppermute(value, ('row', 'col'), pairs_list)  82.8 us
    ppermute x22, starting transfers between devices, in_plane(): return lambda value: lax.ppermute(value, ('row', 'col'), pairs_list)  53.6 us
    pallas_call x4, Pallas kernels, partial_sums(): pl.pallas_call(partial_kernel, grid_spec=pltpu.PrefetchScalarGridSpec(num...  46.3 us
    ppermute x10, waiting for transfers between devices, in_line(): return lambda value: lax.ppermute(value, 'col', pairs_list)  30.4 us
    pallas_call x4, Pallas kernels, new_rows(): pl.pallas_call(new_rows_kernel, grid_spec=pltpu.PrefetchScalarGridSpec(nu...  22.1 us
    ppermute x10, starting transfers between devices, in_line(): return lambda value: lax.ppermute(value, 'col', pairs_list)  17.9 us
    pallas_call x1, Pallas kernels, last_cols(): pl.pallas_call(last_cols_kernel, grid=(rows // size,), in_specs=[pl.Block...  16.8 us
    pallas_call x2, Pallas kernels, new_cols(): pl.pallas_call(new_cols_kernel, grid=(2 * count,), in_specs=[pl.BlockSpec...  10.9 us
  transfers between devices with their start and end apart: 40, of which 12 were waited for; matrix products, arithmetic and copies ran while one was open for 6% of the time, Pallas kernels for 21%

profile of v2, /device:TPU:0, one launch (start us, length us, event | category | flops | bytes accessed | tf_op | source)
XLA Modules:
  0.0 327.0 jit_solution(3318886089124096463)
XLA Ops:
  2.1 6.0 %collective-permute-start = (bf16[1536,512]{1,0:T(8,128)(2,1)S(1)}, bf16[1536,512]{1,0:T(8,128)(2,1)}, u32[]{:S(2)}, u32[]{:S(2)}) collective-permute-start(bf16[1536,512]{1,0:T(8,128)(2,1)S(1)} %get-tuple-element.158.refs_0_), channel_id=1, source_target_pairs={{0,8},{1,9},{10,2},{11,3},{20,28},{21,29},{30,22},{31,23}} | collective-permute-start | bytes 4718600 | tf_op jit(solution)/shard_map/ppermute | solution.py:280
  17.4 24.3 %collective-permute-done.refs_1_ = bf16[1536,512]{1,0:T(8,128)(2,1)} collective-permute-done((bf16[1536,512]{1,0:T(8,128)(2,1)S(1)}, bf16[1536,512]{1,0:T(8,128)(2,1)}, u32[]{:S(2)}, u32[]{:S(2)}) %collective-permute-start) | collective-permute-done | bytes 1572896 | tf_op jit(solution)/shard_map/ppermute | solution.py:280
  48.4 28.4 %collective-permute-done.1.refs_2_ = bf16[1536,512]{1,0:T(8,128)(2,1)} collective-permute-done((bf16[1536,512]{1,0:T(8,128)(2,1)S(1)}, bf16[1536,512]{1,0:T(8,128)(2,1)}, u32[]{:S(2)}, u32[]{:S(2)}) %collective-permute-start.1) | collective-permute-done | bytes 1572896 | tf_op jit(solution)/shard_map/ppermute | solution.py:280
  76.7 11.5 %partial_sums.4 = (f32[768,512]{1,0:T(8,128)}, bf16[768,512]{1,0:T(8,128)(2,1)}) custom-call(s32[2]{0:T(128)} %pad_add_fusion.where_ref, bf16[6144,3072]{1,0:T(8,128)(2,1)} %a1_ref.7, bf16[6144,3072]{1,0:T(8,128)(2,1)} %a1_ref.7, bf16[1536,512]{1,0:T(8,128)(2,1)} %copy-done.3, bf16[1536,512]{1,0:T(8,128)(2,1)} %collective-permute-done.refs_1_, ...), custom_call_target="tpu_custom_call" | custom-call | flops 4831838208 | bytes 14155776 | tf_op jit(solution)/shard_map/partial_sums/pallas_call | solution.py:97
  93.5 3.4 %collective-permute-start.7 = (bf16[768,512]{1,0:T(8,128)(2,1)}, bf16[768,512]{1,0:T(8,128)(2,1)S(1)}, u32[]{:S(2)}, u32[]{:S(2)}) collective-permute-start(bf16[768,512]{1,0:T(8,128)(2,1)} %add_convert_fusion.7.refs_8_), channel_id=1, source_target_pairs={{0,2},{1,3},{2,0},{3,1},{4,6},{5,7},{6,4},{7,5},{8,10},{9,11},{10,... | collective-permute-start | bytes 2359304 | tf_op jit(solution)/shard_map/ppermute | solution.py:284
  96.9 11.6 %partial_sums.6 = (f32[768,512]{1,0:T(8,128)}, bf16[768,512]{1,0:T(8,128)(2,1)}) custom-call(s32[2]{0:T(128)} %pad_add_fusion.where_ref, bf16[6144,3072]{1,0:T(8,128)(2,1)} %a1_ref.7, bf16[6144,3072]{1,0:T(8,128)(2,1)} %a1_ref.7, bf16[1536,512]{1,0:T(8,128)(2,1)} %copy-done.3, bf16[1536,512]{1,0:T(8,128)(2,1)} %collective-permute-done.refs_1_, ...), custom_call_target="tpu_custom_call" | custom-call | flops 4831838208 | bytes 14155776 | tf_op jit(solution)/shard_map/partial_sums/pallas_call | solution.py:97
  108.5 11.6 %partial_sums.5 = (f32[768,512]{1,0:T(8,128)}, bf16[768,512]{1,0:T(8,128)(2,1)}) custom-call(s32[2]{0:T(128)} %pad_add_fusion.where_ref, bf16[6144,3072]{1,0:T(8,128)(2,1)} %a1_ref.7, bf16[6144,3072]{1,0:T(8,128)(2,1)} %a1_ref.7, bf16[1536,512]{1,0:T(8,128)(2,1)} %copy-done.3, bf16[1536,512]{1,0:T(8,128)(2,1)} %collective-permute-done.refs_1_, ...), custom_call_target="tpu_custom_call" | custom-call | flops 4831838208 | bytes 14155776 | tf_op jit(solution)/shard_map/partial_sums/pallas_call | solution.py:97
  123.1 6.4 %collective-permute-start.9 = (bf16[768,512]{1,0:T(8,128)(2,1)S(1)}, bf16[768,512]{1,0:T(8,128)(2,1)S(1)}, u32[]{:S(2)}, u32[]{:S(2)}) collective-permute-start(bf16[768,512]{1,0:T(8,128)(2,1)S(1)} %add_convert_fusion.6.refs_8_), channel_id=1, source_target_pairs={{0,2},{1,3},{2,0},{3,1},{4,6},{5,7},{6,4},{7,5},{8,10},{9,11},{10,... | collective-permute-start | bytes 2359304 | tf_op jit(solution)/shard_map/ppermute | solution.py:284
  129.6 11.6 %partial_sums.7 = (f32[768,512]{1,0:T(8,128)}, bf16[768,512]{1,0:T(8,128)(2,1)}) custom-call(s32[2]{0:T(128)} %pad_add_fusion.where_ref, bf16[6144,3072]{1,0:T(8,128)(2,1)} %a1_ref.7, bf16[6144,3072]{1,0:T(8,128)(2,1)} %a1_ref.7, bf16[1536,512]{1,0:T(8,128)(2,1)} %copy-done.3, bf16[1536,512]{1,0:T(8,128)(2,1)} %collective-permute-done.refs_1_, ...), custom_call_target="tpu_custom_call" | custom-call | flops 4831838208 | bytes 14155776 | tf_op jit(solution)/shard_map/partial_sums/pallas_call | solution.py:97
  141.2 6.5 %collective-permute-done.9 = bf16[768,512]{1,0:T(8,128)(2,1)S(1)} collective-permute-done((bf16[768,512]{1,0:T(8,128)(2,1)S(1)}, bf16[768,512]{1,0:T(8,128)(2,1)S(1)}, u32[]{:S(2)}, u32[]{:S(2)}) %collective-permute-start.9) | collective-permute-done | bytes 786464 | tf_op jit(solution)/shard_map/ppermute | solution.py:284
  151.8 3.4 %broadcast_select_fusion.5 = (bf16[768,512]{1,0:T(8,128)(2,1)}, bf16[768,512]{1,0:T(8,128)(2,1)S(1)}, bf16[768,512]{1,0:T(8,128)(2,1)S(1)}) fusion(pred[]{:T(512)S(6)} %or.3, f32[768,512]{1,0:T(8,128)S(1)} %copy-done.26, bf16[768,512]{1,0:T(8,128)(2,1)} %collective-permute-done.11, bf16[768,512]{1,0:T(8,128)(2,1)} %copy-done.28, ...), kind=kLoop, calls=%fused_computation.26 | loop fusion | flops 5111808 | bytes 7864325 | tf_op jit(solution)/shard_map/jit(_where)/select_n | solution.py:349
  157.4 17.6 %collective-permute-done.12 = bf16[768,512]{1,0:T(8,128)(2,1)S(1)} collective-permute-done((bf16[768,512]{1,0:T(8,128)(2,1)}, bf16[768,512]{1,0:T(8,128)(2,1)S(1)}, u32[]{:S(2)}, u32[]{:S(2)}) %collective-permute-start.12) | collective-permute-done | bytes 786464 | tf_op jit(solution)/shard_map/ppermute | solution.py:284
  175.2 2.8 broadcast_select_fusion.4
  178.2 2.9 collective-permute-start.18
  183.5 14.2 %collective-permute-done.18 = bf16[768,512]{1,0:T(8,128)(2,1)} collective-permute-done((bf16[768,512]{1,0:T(8,128)(2,1)S(1)}, bf16[768,512]{1,0:T(8,128)(2,1)}, u32[]{:S(2)}, u32[]{:S(2)}) %collective-permute-start.18) | collective-permute-done | bytes 786464 | tf_op jit(solution)/shard_map/ppermute | solution.py:280
  202.2 3.2 add_convert_fusion.1
  206.4 3.9 %collective-permute-start.23 = (bf16[768,512]{1,0:T(8,128)(2,1)}, bf16[768,512]{1,0:T(8,128)(2,1)S(1)}, u32[]{:S(2)}, u32[]{:S(2)}) collective-permute-start(bf16[768,512]{1,0:T(8,128)(2,1)} %broadcast_select_fusion.2.own_ref), channel_id=1, source_target_pairs={{0,8},{1,9},{10,2},{11,3},{20,28},{21,29},{30,22},{31,23}} | collective-permute-start | bytes 2359304 | tf_op jit(solution)/shard_map/ppermute | solution.py:280
  215.7 12.3 %collective-permute-done.23.refs_4_.refs_5_.refs_6_ = bf16[768,512]{1,0:T(8,128)(2,1)S(1)} collective-permute-done((bf16[768,512]{1,0:T(8,128)(2,1)}, bf16[768,512]{1,0:T(8,128)(2,1)S(1)}, u32[]{:S(2)}, u32[]{:S(2)}) %collective-permute-start.23) | collective-permute-done | bytes 786464 | tf_op jit(solution)/shard_map/ppermute | solution.py:280
  229.4 3.0 collective-permute-done.20
  235.6 5.8 %collective-permute-start.28 = (bf16[768,512]{1,0:T(8,128)(2,1)S(1)}, bf16[768,512]{1,0:T(8,128)(2,1)}, u32[]{:S(2)}, u32[]{:S(2)}) collective-permute-start(bf16[768,512]{1,0:T(8,128)(2,1)S(1)} %broadcast_select_fusion.1.refs_1_.refs_2_.refs_3_.refs_4_.refs_5_.own_ref), channel_id=1, source_target_pairs={{0,8},{1,9},{10,2},{11,3},{20,28},{21,29},{30,22},{31,23}} | collective-permute-start | bytes 2359304 | tf_op jit(solution)/shard_map/ppermute | solution.py:280
  246.2 2.7 add_select_fusion.1.cols_ref
  248.9 4.5 %new_rows.4 = (bf16[6144,3072]{1,0:T(8,128)(2,1)}, bf16[6144,512]{1,0:T(8,128)(2,1)}, f32[8,128]{1,0:T(8,128)}) custom-call(s32[1]{0:T(128)} %bitcast.k_ref, bf16[768,512]{1,0:T(8,128)(2,1)} %copy-done.12, bf16[768,512]{1,0:T(8,128)(2,1)} %copy-done.27, bf16[768,512]{1,0:T(8,128)(2,1)} %add_select_fusion.1.cols_ref, f32[6144,128]{1,0:T(8,128)} %broadcast_in_dim.4.gr_ref, ...), custom_call_target="tpu_custom_call" | custom-call | flops 1207959552 | bytes 3145728 | tf_op jit(solution)/shard_map/new_rows/pallas_call | solution.py:153
  253.3 4.4 %new_cols.2 = (bf16[6144,3072]{1,0:T(8,128)(2,1)}, bf16[3072,512]{1,0:T(8,128)(2,1)}, f32[8,128]{1,0:T(8,128)}) custom-call(bf16[6144,512]{1,0:T(8,128)(2,1)} %get-tuple-element.117.wr_ref.refs_1_, bf16[768,512]{1,0:T(8,128)(2,1)} %add_select_fusion.1.cols_ref, f32[6144,128]{1,0:T(8,128)} %broadcast_in_dim.4.gr_ref, ...), custom_call_target="tpu_custom_call", output_to_operand_aliasing={{0}: (4, {})} | custom-call | flops 1207959552 | bytes 7864320 | tf_op jit(solution)/shard_map/new_cols/pallas_call | solution.py:204
  257.8 4.5 %new_rows.5 = (bf16[6144,3072]{1,0:T(8,128)(2,1)}, bf16[6144,512]{1,0:T(8,128)(2,1)}, f32[8,128]{1,0:T(8,128)}) custom-call(s32[1]{0:T(128)} %bitcast.k_ref, bf16[768,512]{1,0:T(8,128)(2,1)} %broadcast_select_fusion.2.own_ref, bf16[768,512]{1,0:T(8,128)(2,1)} %collective-permute-done.22.oth_ref, ...), custom_call_target="tpu_custom_call", output_to_operand_aliasing={{0}: (6, {}), {1}: (7, {})} | custom-call | flops 1207959552 | bytes 3145728 | tf_op jit(solution)/shard_map/new_rows/pallas_call | solution.py:153
  264.7 6.0 %collective-permute-start.31 = (bf16[384,512]{1,0:T(8,128)(2,1)S(1)}, bf16[384,512]{1,0:T(8,128)(2,1)S(1)}, u32[]{:S(2)}, u32[]{:S(2)}) collective-permute-start(bf16[384,512]{1,0:T(8,128)(2,1)S(1)} %get-tuple-element.164), channel_id=1, source_target_pairs={{0,8},{1,9},{10,2},{11,3},{20,28},{21,29},{30,22},{31,23}} | collective-permute-start | bytes 1179656 | tf_op jit(solution)/shard_map/ppermute | solution.py:280
  275.5 2.7 add_select_fusion.cols_ref
  278.2 6.4 %new_cols.3 = (bf16[6144,3072]{1,0:T(8,128)(2,1)}, bf16[3072,512]{1,0:T(8,128)(2,1)}, f32[8,128]{1,0:T(8,128)}) custom-call(bf16[6144,512]{1,0:T(8,128)(2,1)} %get-tuple-element.125.wr_ref.refs_1_, bf16[768,512]{1,0:T(8,128)(2,1)} %add_select_fusion.cols_ref, f32[6144,128]{1,0:T(8,128)} %broadcast_in_dim.4.gr_ref, ...), custom_call_target="tpu_custom_call", output_to_operand_aliasing={{0}: (4, {}), {1}: (5, {})} | custom-call | flops 2415919104 | bytes 15728640 | tf_op jit(solution)/shard_map/new_cols/pallas_call | solution.py:204
  286.4 3.6 %collective-permute-start.36 = (bf16[384,512]{1,0:T(8,128)(2,1)S(1)}, bf16[384,512]{1,0:T(8,128)(2,1)S(1)}, u32[]{:S(2)}, u32[]{:S(2)}) collective-permute-start(bf16[384,512]{1,0:T(8,128)(2,1)S(1)} %get-tuple-element.162), channel_id=1, source_target_pairs={{0,8},{1,9},{10,2},{11,3},{20,28},{21,29},{30,22},{31,23}} | collective-permute-start | bytes 1179656 | tf_op jit(solution)/shard_map/ppermute | solution.py:280
  293.0 6.5 %new_rows.6 = (bf16[6144,3072]{1,0:T(8,128)(2,1)}, bf16[6144,512]{1,0:T(8,128)(2,1)}, f32[8,128]{1,0:T(8,128)}) custom-call(s32[1]{0:T(128)} %bitcast.k_ref, bf16[768,512]{1,0:T(8,128)(2,1)} %copy-done, bf16[768,512]{1,0:T(8,128)(2,1)} %collective-permute-done.27.oth_ref, ...), custom_call_target="tpu_custom_call", output_to_operand_aliasing={{0}: (6, {}), {1}: (7, {})} | custom-call | flops 2415919104 | bytes 6291456 | tf_op jit(solution)/shard_map/new_rows/pallas_call | solution.py:153
  299.5 6.6 %new_rows.7 = (bf16[6144,3072]{1,0:T(8,128)(2,1)}, bf16[6144,512]{1,0:T(8,128)(2,1)}, f32[8,128]{1,0:T(8,128)}) custom-call(s32[1]{0:T(128)} %bitcast.k_ref, bf16[768,512]{1,0:T(8,128)(2,1)} %copy-done.4, bf16[768,512]{1,0:T(8,128)(2,1)} %copy-done.32, bf16[3072,512]{1,0:T(8,128)(2,1)} %get-tuple-element.133.cols_ref, ...), custom_call_target="tpu_custom_call", output_to_operand_aliasing={{0}: (6, {}), {1}: (7, {})} | custom-call | flops 2415919104 | bytes 6291456 | tf_op jit(solution)/shard_map/new_rows/pallas_call | solution.py:153
  306.1 2.8 fusion.4.c0_ref
  310.1 16.8 %last_cols.1 = bf16[6144,3072]{1,0:T(8,128)(2,1)} custom-call(bf16[6144,512]{1,0:T(8,128)(2,1)} %get-tuple-element.141.wr_ref, bf16[768,512]{1,0:T(8,128)(2,1)} %fusion.4.c0_ref, bf16[768,512]{1,0:T(8,128)(2,1)} %pad_maximum_fusion.c1_ref, f32[6144,128]{1,0:T(8,128)} %broadcast_in_dim.4.gr_ref, f32[1,3072]{1,0:T(1,128)} %bitcast.9, ...), custom_call_target="tpu_custom_call", output_to_operand_aliasing={{}: (5, {})} | custom-call | flops 9663676416 | bytes 18874368 | tf_op jit(solution)/shard_map/last_cols/pallas_call | solution.py:243
  (152 shorter events, 68.2 us)
Async XLA Ops:
  2.1 39.6 %collective-permute-start = (bf16[1536,512]{1,0:T(8,128)(2,1)S(1)}, bf16[1536,512]{1,0:T(8,128)(2,1)}, u32[]{:S(2)}, u32[]{:S(2)}) collective-permute-start(bf16[1536,512]{1,0:T(8,128)(2,1)S(1)} %get-tuple-element.158.refs_0_), channel_id=1, source_target_pairs={{0,8},{1,9},{10,2},{11,3},{20,28},{21,29},{30,22},{31,23}} | collective-permute-start | bytes 4718600 | tf_op jit(solution)/shard_map/ppermute | solution.py:280
  8.1 37.8 %collective-permute-start.4 = (bf16[1536,512]{1,0:T(8,128)(2,1)S(1)}, bf16[1536,512]{1,0:T(8,128)(2,1)}, u32[]{:S(2)}, u32[]{:S(2)}) collective-permute-start(bf16[1536,512]{1,0:T(8,128)(2,1)S(1)} %get-tuple-element.157.refs_4_), channel_id=1, source_target_pairs={{0,16},{1,17},{10,26},{11,27},{20,4},{21,5},{30,14},{31,15}} | collective-permute-start | bytes 4718600 | tf_op jit(solution)/shard_map/ppermute | solution.py:280
  10.5 66.2 %collective-permute-start.1 = (bf16[1536,512]{1,0:T(8,128)(2,1)S(1)}, bf16[1536,512]{1,0:T(8,128)(2,1)}, u32[]{:S(2)}, u32[]{:S(2)}) collective-permute-start(bf16[1536,512]{1,0:T(8,128)(2,1)S(1)} %get-tuple-element.158.refs_0_), channel_id=1, source_target_pairs={{0,16},{1,17},{10,26},{11,27},{20,4},{21,5},{30,14},{31,15}} | collective-permute-start | bytes 4718600 | tf_op jit(solution)/shard_map/ppermute | solution.py:280
  12.9 63.8 %collective-permute-start.3 = (bf16[1536,512]{1,0:T(8,128)(2,1)S(1)}, bf16[1536,512]{1,0:T(8,128)(2,1)}, u32[]{:S(2)}, u32[]{:S(2)}) collective-permute-start(bf16[1536,512]{1,0:T(8,128)(2,1)S(1)} %get-tuple-element.157.refs_4_), channel_id=1, source_target_pairs={{0,8},{1,9},{10,2},{11,3},{20,28},{21,29},{30,22},{31,23}} | collective-permute-start | bytes 4718600 | tf_op jit(solution)/shard_map/ppermute | solution.py:280
  44.0 32.8 %collective-permute-start.2 = (bf16[1536,512]{1,0:T(8,128)(2,1)}, bf16[1536,512]{1,0:T(8,128)(2,1)}, u32[]{:S(2)}, u32[]{:S(2)}) collective-permute-start(bf16[1536,512]{1,0:T(8,128)(2,1)} %collective-permute-done.refs_1_), channel_id=1, source_target_pairs={{8,24},{9,25},{2,18},{3,19},{28,12},{29,13},{22,6},{23,7}} | collective-permute-start | bytes 4718600 | tf_op jit(solution)/shard_map/ppermute | solution.py:280
  45.9 30.9 %collective-permute-start.5 = (bf16[1536,512]{1,0:T(8,128)(2,1)}, bf16[1536,512]{1,0:T(8,128)(2,1)}, u32[]{:S(2)}, u32[]{:S(2)}) collective-permute-start(bf16[1536,512]{1,0:T(8,128)(2,1)} %collective-permute-done.4.refs_6_), channel_id=1, source_target_pairs={{16,24},{17,25},{26,18},{27,19},{4,12},{5,13},{14,6},{15,7}} | collective-permute-start | bytes 4718600 | tf_op jit(solution)/shard_map/ppermute | solution.py:280
  93.5 26.6 %collective-permute-start.7 = (bf16[768,512]{1,0:T(8,128)(2,1)}, bf16[768,512]{1,0:T(8,128)(2,1)S(1)}, u32[]{:S(2)}, u32[]{:S(2)}) collective-permute-start(bf16[768,512]{1,0:T(8,128)(2,1)} %add_convert_fusion.7.refs_8_), channel_id=1, source_target_pairs={{0,2},{1,3},{2,0},{3,1},{4,6},{5,7},{6,4},{7,5},{8,10},{9,11},{10,... | collective-permute-start | bytes 2359304 | tf_op jit(solution)/shard_map/ppermute | solution.py:284
  121.9 19.3 %collective-permute-start.10 = (bf16[768,512]{1,0:T(8,128)(2,1)S(1)}, bf16[768,512]{1,0:T(8,128)(2,1)S(1)}, u32[]{:S(2)}, u32[]{:S(2)}) collective-permute-start(bf16[768,512]{1,0:T(8,128)(2,1)S(1)} %fusion.refs_9_), channel_id=1, source_target_pairs={{2,4},{3,5},{4,2},{5,3},{10,12},{11,13},{12,10},{13,11},{18,20},{1... | collective-permute-start | bytes 2359304 | tf_op jit(solution)/shard_map/ppermute | solution.py:284
  122.6 18.6 %collective-permute-start.11 = (bf16[768,512]{1,0:T(8,128)(2,1)}, bf16[768,512]{1,0:T(8,128)(2,1)}, u32[]{:S(2)}, u32[]{:S(2)}) collective-permute-start(bf16[768,512]{1,0:T(8,128)(2,1)} %get-tuple-element.87), channel_id=1, source_target_pairs={{0,1},{1,0},{2,3},{3,2},{4,5},{5,4},{6,7},{7,6},{8,9},{9,8},{10,11... | collective-permute-start | bytes 2359304 | tf_op jit(solution)/shard_map/ppermute | solution.py:290
  123.1 24.6 %collective-permute-start.9 = (bf16[768,512]{1,0:T(8,128)(2,1)S(1)}, bf16[768,512]{1,0:T(8,128)(2,1)S(1)}, u32[]{:S(2)}, u32[]{:S(2)}) collective-permute-start(bf16[768,512]{1,0:T(8,128)(2,1)S(1)} %add_convert_fusion.6.refs_8_), channel_id=1, source_target_pairs={{0,2},{1,3},{2,0},{3,1},{4,6},{5,7},{6,4},{7,5},{8,10},{9,11},{10,... | collective-permute-start | bytes 2359304 | tf_op jit(solution)/shard_map/ppermute | solution.py:284
  155.2 19.8 %collective-permute-start.12 = (bf16[768,512]{1,0:T(8,128)(2,1)}, bf16[768,512]{1,0:T(8,128)(2,1)S(1)}, u32[]{:S(2)}, u32[]{:S(2)}) collective-permute-start(bf16[768,512]{1,0:T(8,128)(2,1)} %get-tuple-element.154), channel_id=1, source_target_pairs={{0,2},{1,3},{2,0},{3,1},{4,6},{5,7},{6,4},{7,5},{8,10},{9,11},{10,... | collective-permute-start | bytes 2359304 | tf_op jit(solution)/shard_map/ppermute | solution.py:284
  157.4 17.6 %collective-permute-start.14 = (bf16[768,512]{1,0:T(8,128)(2,1)}, bf16[768,512]{1,0:T(8,128)(2,1)}, u32[]{:S(2)}, u32[]{:S(2)}) collective-permute-start(bf16[768,512]{1,0:T(8,128)(2,1)} %get-tuple-element.93), channel_id=1, source_target_pairs={{0,1},{1,0},{2,3},{3,2},{4,5},{5,4},{6,7},{7,6},{8,9},{9,8},{10,11... | collective-permute-start | bytes 2359304 | tf_op jit(solution)/shard_map/ppermute | solution.py:290
  178.2 19.4 %collective-permute-start.18 = (bf16[768,512]{1,0:T(8,128)(2,1)S(1)}, bf16[768,512]{1,0:T(8,128)(2,1)}, u32[]{:S(2)}, u32[]{:S(2)}) collective-permute-start(bf16[768,512]{1,0:T(8,128)(2,1)S(1)} %broadcast_select_fusion.3.own_ref), channel_id=1, source_target_pairs={{0,8},{1,9},{10,2},{11,3},{20,28},{21,29},{30,22},{31,23}} | collective-permute-start | bytes 2359304 | tf_op jit(solution)/shard_map/ppermute | solution.py:280
  181.1 18.7 %collective-permute-start.19 = (bf16[768,512]{1,0:T(8,128)(2,1)S(1)}, bf16[768,512]{1,0:T(8,128)(2,1)S(1)}, u32[]{:S(2)}, u32[]{:S(2)}) collective-permute-start(bf16[768,512]{1,0:T(8,128)(2,1)S(1)} %broadcast_select_fusion.3.own_ref), channel_id=1, source_target_pairs={{0,16},{1,17},{10,26},{11,27},{20,4},{21,5},{30,14},{31,15}} | collective-permute-start | bytes 2359304 | tf_op jit(solution)/shard_map/ppermute | solution.py:280
  182.5 19.7 %collective-permute-start.15 = (bf16[768,512]{1,0:T(8,128)(2,1)S(1)}, bf16[768,512]{1,0:T(8,128)(2,1)S(1)}, u32[]{:S(2)}, u32[]{:S(2)}) collective-permute-start(bf16[768,512]{1,0:T(8,128)(2,1)S(1)} %get-tuple-element.97), channel_id=1, source_target_pairs={{0,2},{1,3},{2,0},{3,1},{4,6},{5,7},{6,4},{7,5},{8,10},{9,11},{10,... | collective-permute-start | bytes 2359304 | tf_op jit(solution)/shard_map/ppermute | solution.py:284
  182.6 19.6 %collective-permute-start.16 = (bf16[768,512]{1,0:T(8,128)(2,1)S(1)}, bf16[768,512]{1,0:T(8,128)(2,1)S(1)}, u32[]{:S(2)}, u32[]{:S(2)}) collective-permute-start(bf16[768,512]{1,0:T(8,128)(2,1)S(1)} %fusion.2), channel_id=1, source_target_pairs={{2,4},{3,5},{4,2},{5,3},{10,12},{11,13},{12,10},{13,11},{18,20},{1... | collective-permute-start | bytes 2359304 | tf_op jit(solution)/shard_map/ppermute | solution.py:284
  206.4 21.6 %collective-permute-start.23 = (bf16[768,512]{1,0:T(8,128)(2,1)}, bf16[768,512]{1,0:T(8,128)(2,1)S(1)}, u32[]{:S(2)}, u32[]{:S(2)}) collective-permute-start(bf16[768,512]{1,0:T(8,128)(2,1)} %broadcast_select_fusion.2.own_ref), channel_id=1, source_target_pairs={{0,8},{1,9},{10,2},{11,3},{20,28},{21,29},{30,22},{31,23}} | collective-permute-start | bytes 2359304 | tf_op jit(solution)/shard_map/ppermute | solution.py:280
  210.3 19.1 %collective-permute-start.24 = (bf16[768,512]{1,0:T(8,128)(2,1)}, bf16[768,512]{1,0:T(8,128)(2,1)}, u32[]{:S(2)}, u32[]{:S(2)}) collective-permute-start(bf16[768,512]{1,0:T(8,128)(2,1)} %broadcast_select_fusion.2.own_ref), channel_id=1, source_target_pairs={{0,16},{1,17},{10,26},{11,27},{20,4},{21,5},{30,14},{31,15}} | collective-permute-start | bytes 2359304 | tf_op jit(solution)/shard_map/ppermute | solution.py:280
  212.5 19.9 %collective-permute-start.20 = (bf16[768,512]{1,0:T(8,128)(2,1)}, bf16[768,512]{1,0:T(8,128)(2,1)S(1)}, u32[]{:S(2)}, u32[]{:S(2)}) collective-permute-start(bf16[768,512]{1,0:T(8,128)(2,1)} %get-tuple-element.102), channel_id=1, source_target_pairs={{0,2},{1,3},{2,0},{3,1},{4,6},{5,7},{6,4},{7,5},{8,10},{9,11},{10,... | collective-permute-start | bytes 2359304 | tf_op jit(solution)/shard_map/ppermute | solution.py:284
  212.6 19.8 %collective-permute-start.21 = (bf16[768,512]{1,0:T(8,128)(2,1)}, bf16[768,512]{1,0:T(8,128)(2,1)}, u32[]{:S(2)}, u32[]{:S(2)}) collective-permute-start(bf16[768,512]{1,0:T(8,128)(2,1)} %get-tuple-element.103), channel_id=1, source_target_pairs={{2,4},{3,5},{4,2},{5,3},{10,12},{11,13},{12,10},{13,11},{18,20},{1... | collective-permute-start | bytes 2359304 | tf_op jit(solution)/shard_map/ppermute | solution.py:284
  214.2 19.1 %collective-permute-start.25 = (bf16[768,512]{1,0:T(8,128)(2,1)}, bf16[768,512]{1,0:T(8,128)(2,1)}, u32[]{:S(2)}, u32[]{:S(2)}) collective-permute-start(bf16[768,512]{1,0:T(8,128)(2,1)} %collective-permute-done.18), channel_id=1, source_target_pairs={{8,24},{9,25},{2,18},{3,19},{28,12},{29,13},{22,6},{23,7}} | collective-permute-start | bytes 2359304 | tf_op jit(solution)/shard_map/ppermute | solution.py:280
  235.5 26.8 %collective-permute-start.27 = (bf16[768,512]{1,0:T(8,128)(2,1)S(1)}, bf16[768,512]{1,0:T(8,128)(2,1)}, u32[]{:S(2)}, u32[]{:S(2)}) collective-permute-start(bf16[768,512]{1,0:T(8,128)(2,1)S(1)} %broadcast_select_fusion.1.refs_1_.refs_2_.refs_3_.refs_4_.refs_5_.own_ref), channel_id=1, source_target_pairs={{0,1},{1,0},{2,3},{3,2},{4,5},{5,4},{6,7},{7,6},{8,9},{9,8},{10,11... | collective-permute-start | bytes 2359304 | tf_op jit(solution)/shard_map/ppermute | solution.py:290
  235.6 26.8 %collective-permute-start.28 = (bf16[768,512]{1,0:T(8,128)(2,1)S(1)}, bf16[768,512]{1,0:T(8,128)(2,1)}, u32[]{:S(2)}, u32[]{:S(2)}) collective-permute-start(bf16[768,512]{1,0:T(8,128)(2,1)S(1)} %broadcast_select_fusion.1.refs_1_.refs_2_.refs_3_.refs_4_.refs_5_.own_ref), channel_id=1, source_target_pairs={{0,8},{1,9},{10,2},{11,3},{20,28},{21,29},{30,22},{31,23}} | collective-permute-start | bytes 2359304 | tf_op jit(solution)/shard_map/ppermute | solution.py:280
  241.4 21.0 %collective-permute-start.29 = (bf16[768,512]{1,0:T(8,128)(2,1)S(1)}, bf16[768,512]{1,0:T(8,128)(2,1)}, u32[]{:S(2)}, u32[]{:S(2)}) collective-permute-start(bf16[768,512]{1,0:T(8,128)(2,1)S(1)} %broadcast_select_fusion.1.refs_1_.refs_2_.refs_3_.refs_4_.refs_5_.own_ref), channel_id=1, source_target_pairs={{0,16},{1,17},{10,26},{11,27},{20,4},{21,5},{30,14},{31,15}} | collective-permute-start | bytes 2359304 | tf_op jit(solution)/shard_map/ppermute | solution.py:280
  243.6 19.8 %collective-permute-start.26 = (bf16[768,512]{1,0:T(8,128)(2,1)S(1)}, bf16[768,512]{1,0:T(8,128)(2,1)}, u32[]{:S(2)}, u32[]{:S(2)}) collective-permute-start(bf16[768,512]{1,0:T(8,128)(2,1)S(1)} %add_convert_fusion.refs_0_.refs_1_.refs_2_), channel_id=1, source_target_pairs={{0,2},{1,3},{2,0},{3,1},{4,6},{5,7},{6,4},{7,5},{8,10},{9,11},{10,... | collective-permute-start | bytes 2359304 | tf_op jit(solution)/shard_map/ppermute | solution.py:284
  244.7 18.7 %collective-permute-start.30 = (bf16[768,512]{1,0:T(8,128)(2,1)S(1)}, bf16[768,512]{1,0:T(8,128)(2,1)}, u32[]{:S(2)}, u32[]{:S(2)}) collective-permute-start(bf16[768,512]{1,0:T(8,128)(2,1)S(1)} %collective-permute-done.23.refs_4_.refs_5_.refs_6_), channel_id=1, source_target_pairs={{8,24},{9,25},{2,18},{3,19},{28,12},{29,13},{22,6},{23,7}} | collective-permute-start | bytes 2359304 | tf_op jit(solution)/shard_map/ppermute | solution.py:280
  264.6 20.1 %collective-permute-start.35 = (bf16[768,512]{1,0:T(8,128)(2,1)S(1)}, bf16[768,512]{1,0:T(8,128)(2,1)S(1)}, u32[]{:S(2)}, u32[]{:S(2)}) collective-permute-start(bf16[768,512]{1,0:T(8,128)(2,1)S(1)} %broadcast_select_fusion.refs_2_.own_ref), channel_id=1, source_target_pairs={{0,1},{1,0},{2,3},{3,2},{4,5},{5,4},{6,7},{7,6},{8,9},{9,8},{10,11... | collective-permute-start | bytes 2359304 | tf_op jit(solution)/shard_map/ppermute | solution.py:290
  264.7 19.9 %collective-permute-start.31 = (bf16[384,512]{1,0:T(8,128)(2,1)S(1)}, bf16[384,512]{1,0:T(8,128)(2,1)S(1)}, u32[]{:S(2)}, u32[]{:S(2)}) collective-permute-start(bf16[384,512]{1,0:T(8,128)(2,1)S(1)} %get-tuple-element.164), channel_id=1, source_target_pairs={{0,8},{1,9},{10,2},{11,3},{20,28},{21,29},{30,22},{31,23}} | collective-permute-start | bytes 1179656 | tf_op jit(solution)/shard_map/ppermute | solution.py:280
  286.4 22.5 %collective-permute-start.36 = (bf16[384,512]{1,0:T(8,128)(2,1)S(1)}, bf16[384,512]{1,0:T(8,128)(2,1)S(1)}, u32[]{:S(2)}, u32[]{:S(2)}) collective-permute-start(bf16[384,512]{1,0:T(8,128)(2,1)S(1)} %get-tuple-element.162), channel_id=1, source_target_pairs={{0,8},{1,9},{10,2},{11,3},{20,28},{21,29},{30,22},{31,23}} | collective-permute-start | bytes 1179656 | tf_op jit(solution)/shard_map/ppermute | solution.py:280
  290.0 18.9 %collective-permute-start.37 = (bf16[384,512]{1,0:T(8,128)(2,1)S(1)}, bf16[384,512]{1,0:T(8,128)(2,1)S(1)}, u32[]{:S(2)}, u32[]{:S(2)}) collective-permute-start(bf16[384,512]{1,0:T(8,128)(2,1)S(1)} %get-tuple-element.161), channel_id=1, source_target_pairs={{0,16},{1,17},{10,26},{11,27},{20,4},{21,5},{30,14},{31,15}} | collective-permute-start | bytes 1179656 | tf_op jit(solution)/shard_map/ppermute | solution.py:280
  291.3 17.6 %collective-permute-start.38 = (bf16[384,512]{1,0:T(8,128)(2,1)S(1)}, bf16[384,512]{1,0:T(8,128)(2,1)S(1)}, u32[]{:S(2)}, u32[]{:S(2)}) collective-permute-start(bf16[384,512]{1,0:T(8,128)(2,1)S(1)} %collective-permute-done.31.refs_3_), channel_id=1, source_target_pairs={{8,24},{9,25},{2,18},{3,19},{28,12},{29,13},{22,6},{23,7}} | collective-permute-start | bytes 1179656 | tf_op jit(solution)/shard_map/ppermute | solution.py:280
  292.0 16.9 %collective-permute-start.39 = (bf16[384,512]{1,0:T(8,128)(2,1)S(1)}, bf16[384,512]{1,0:T(8,128)(2,1)S(1)}, u32[]{:S(2)}, u32[]{:S(2)}) collective-permute-start(bf16[384,512]{1,0:T(8,128)(2,1)S(1)} %collective-permute-done.32.refs_4_), channel_id=1, source_target_pairs={{16,24},{17,25},{26,18},{27,19},{4,12},{5,13},{14,6},{15,7}} | collective-permute-start | bytes 1179656 | tf_op jit(solution)/shard_map/ppermute | solution.py:280
  (41 other events, 517.4 us)

commit v3 on v2

--- a/solution.py
+++ b/solution.py
@@ -8,7 +8,7 @@
 from jax.sharding import PartitionSpec as P
 
 BF16, F32 = jnp.bfloat16, jnp.float32
-VMEM_LIMIT = 56 * 1024 * 1024
+VMEM_LIMIT = 20 * 1024 * 1024
 CHUNKS = 4
 
 
@@ -179,6 +179,61 @@
         cost_estimate=cost(4 * size * width * vectors, 4 * size * width + 2 * width * vectors),
         name="new_rows",
     )(core, own, oth, cols, gap_rows, gap_cols, *state, *after)
+
+
+def last_rows_kernel(k_ref, own0_ref, oth0_ref, own1_ref, oth1_ref, cols_ref, gr_ref, gc_ref, *refs):
+    out_ref, wr_ref, token_ref = refs[-3:]
+    token_ref[...] = jnp.zeros_like(token_ref)
+    step = pl.program_id(0)
+    for i, source in enumerate((own0_ref, own1_ref, oth0_ref, oth1_ref)):
+
+        @pl.when(step == i)
+        def _():
+            wr_ref[...] = source[...]
+
+    piece = wr_ref.shape[0]
+    for first in range(0, cols_ref.shape[0], piece):
+        here = slice(first, first + piece)
+        out_ref[:, here] = block_out(wr_ref[...], cols_ref[here, :], gr_ref[...], gc_ref[:, here])
+
+
+def last_rows(core, pieces, cols, gap_rows, gap_cols, start, width, state, after):
+    out, wr = state
+    size, vectors = pieces[0].shape
+    per_half = wr.shape[0] // 2 // size
+    first = start // size
+
+    def row(i, k):
+        return lax.rem(k[0] + i // 2, 2) * per_half + first + lax.rem(i, 2)
+
+    return pl.pallas_call(
+        last_rows_kernel,
+        grid_spec=pltpu.PrefetchScalarGridSpec(
+            num_scalar_prefetch=1,
+            grid=(4,),
+            in_specs=[pl.BlockSpec((size, vectors), lambda i, k: (0, 0))] * 4
+            + [
+                pl.BlockSpec((width, vectors), lambda i, k: (0, 0)),
+                pl.BlockSpec((size, gap_rows.shape[1]), lambda i, k: (row(i, k), 0)),
+                pl.BlockSpec((1, width), lambda i, k: (0, 0)),
+            ]
+            + [pl.BlockSpec(memory_space=pl.ANY)] * (2 + len(after)),
+            out_specs=[
+                pl.BlockSpec((size, width), lambda i, k: (row(i, k), 0)),
+                pl.BlockSpec((size, vectors), lambda i, k: (row(i, k), 0)),
+                pl.BlockSpec((8, 128), lambda i, k: (0, 0)),
+            ],
+        ),
+        out_shape=[
+            jax.ShapeDtypeStruct(out.shape, BF16),
+            jax.ShapeDtypeStruct(wr.shape, BF16),
+            TOKEN,
+        ],
+        input_output_aliases={8: 0, 9: 1},
+        compiler_params=params(),
+        cost_estimate=cost(8 * size * width * vectors, 8 * size * width + 2 * width * vectors),
+        name="last_rows",
+    )(core, *pieces, cols, gap_rows, gap_cols, out, wr, *after)
 
 
 def new_cols_kernel(wr_ref, cols_ref, gr_ref, gc_ref, *refs):
@@ -399,8 +454,10 @@
     low, high = final[c][: size // 2], final[c][size // 2 :]
     high_x, low_y = root_x(high), root_y(low)
     low_far, high_far = x_far(low_x), y_far(high_y)
-    out, wr, _ = rows(c - 1, wc, [last, low_x, high_y], [out, wr])
-    out, wr, last = rows(c, wc, [], [out, wr])
+    out, wr, last = last_rows(
+        core_arg, (final[c - 1], across[c - 1], final[c], across[c]), wc, gap_rows, gap_cols,
+        (c - 1) * size, (c - 1) * size, (out, wr), [last, low_x, high_y],
+    )
     high_x, low_y, low_far, high_far, last = lax.optimization_barrier(
         (high_x, low_y, low_far, high_far, last)
     )

time: 328 us -> 323 us (0.985)
  Pallas kernels: 96.1 us -> 80.1 us
  waiting for transfers between devices: 116 us -> 121 us
  starting transfers between devices: 72.2 us -> 75.5 us
    pallas_call x4 -> x2, Pallas kernels: 22.1 us -> 6.52 us  [new_rows(): pl.pallas_call(new_rows_kernel, grid_spec=pltpu.PrefetchScalarGridSpec(nu...]
    pallas_call x0 -> x1, Pallas kernels: none -> 9.08 us  [last_rows(): pl.pallas_call(last_rows_kernel, grid_spec=pltpu.PrefetchScalarGridSpec(n...]
    ppermute x22, waiting for transfers between devices: 82.8 us -> 86.8 us  [in_plane(): return lambda value: lax.ppermute(value, ('row', 'col'), pairs_list)]
    ppermute x22, starting transfers between devices: 53.6 us -> 57.4 us  [in_plane(): return lambda value: lax.ppermute(value, ('row', 'col'), pairs_list)]
    pallas_call x2, Pallas kernels: 10.9 us -> 7.14 us  [new_cols(): pl.pallas_call(new_cols_kernel, grid=(2 * count,), in_specs=[pl.BlockSpec...]
    pallas_call x1, Pallas kernels: 16.8 us -> 13.1 us  [last_cols(): pl.pallas_call(last_cols_kernel, grid=(rows // size,), in_specs=[pl.Block...]
    select_n x4, other arithmetic: 2.39 us -> 5.93 us  [planned_shards(): final[c] = jnp.where(in_middle, dressed[c], arrived)]
    unnamed x66 -> x38, local copies, waits for them, and re-layouts: 1.01 us -> 4.4 us
  transfers between devices with their start and end apart: 40 -> 40, of which waited for: 12 -> 14; matrix products, arithmetic and copies ran while one was open for 6% -> 5% of each run, Pallas kernels for 21% -> 17%
where the time goes in v3:
time: 323 us; the launch traced here: 322 us
  waiting for transfers between devices  121 us (37%)
  Pallas kernels  80.1 us (25%)
  starting transfers between devices  75.5 us (23%)
  other arithmetic  33.6 us (10%)
  local copies, waits for them, and re-layouts  11.2 us (3%)
    ppermute x22, waiting for transfers between devices, in_plane(): return lambda value: lax.ppermute(value, ('row', 'col'), pairs_list)  86.8 us
    ppermute x22, starting transfers between devices, in_plane(): return lambda value: lax.ppermute(value, ('row', 'col'), pairs_list)  57.4 us
    pallas_call x4, Pallas kernels, partial_sums(): pl.pallas_call(partial_kernel, grid_spec=pltpu.PrefetchScalarGridSpec(num...  44.2 us
    ppermute x10, waiting for transfers between devices, in_line(): return lambda value: lax.ppermute(value, 'col', pairs_list)  31.8 us
    ppermute x10, starting transfers between devices, in_line(): return lambda value: lax.ppermute(value, 'col', pairs_list)  17.4 us
    pallas_call x1, Pallas kernels, last_cols(): pl.pallas_call(last_cols_kernel, grid=(rows // size,), in_specs=[pl.Block...  13.1 us
    pallas_call x1, Pallas kernels, last_rows(): pl.pallas_call(last_rows_kernel, grid_spec=pltpu.PrefetchScalarGridSpec(n...  9.08 us
    pallas_call x2, Pallas kernels, new_cols(): pl.pallas_call(new_cols_kernel, grid=(2 * count,), in_specs=[pl.BlockSpec...  7.14 us
  transfers between devices with their start and end apart: 40, of which 14 were waited for; matrix products, arithmetic and copies ran while one was open for 5% of the time, Pallas kernels for 17%

profile of v3, /device:TPU:0, one launch (start us, length us, event | category | flops | bytes accessed | tf_op | source)
XLA Modules:
  0.0 321.7 jit_solution(1815926653581631305)
XLA Ops:
  0.0 3.8 %constant_dynamic-slice_fusion = (bf16[1536,512]{1,0:T(8,128)(2,1)}, bf16[1536,512]{1,0:T(8,128)(2,1)}) fusion(bf16[6144,512]{1,0:T(8,128)(2,1)} %param.4, s32[]{:T(128)S(6)} %select_n.88, s32[]{:T(128)S(6)} %select_n.89), kind=kLoop, calls=%fused_computation.31 | loop fusion | bytes 6291464 | tf_op jit(solution)/shard_map/dynamic_slice | solution.py:357
  3.8 6.0 %collective-permute-start = (bf16[1536,512]{1,0:T(8,128)(2,1)}, bf16[1536,512]{1,0:T(8,128)(2,1)}, u32[]{:S(2)}, u32[]{:S(2)}) collective-permute-start(bf16[1536,512]{1,0:T(8,128)(2,1)} %get-tuple-element.154.refs_0_), channel_id=1, source_target_pairs={{0,8},{1,9},{10,2},{11,3},{20,28},{21,29},{30,22},{31,23}} | collective-permute-start | bytes 4718600 | tf_op jit(solution)/shard_map/ppermute | solution.py:335
  18.6 25.1 %collective-permute-done.refs_1_ = bf16[1536,512]{1,0:T(8,128)(2,1)} collective-permute-done((bf16[1536,512]{1,0:T(8,128)(2,1)}, bf16[1536,512]{1,0:T(8,128)(2,1)}, u32[]{:S(2)}, u32[]{:S(2)}) %collective-permute-start) | collective-permute-done | bytes 1572896 | tf_op jit(solution)/shard_map/ppermute | solution.py:335
  48.5 30.3 %collective-permute-done.1.refs_2_ = bf16[1536,512]{1,0:T(8,128)(2,1)} collective-permute-done((bf16[1536,512]{1,0:T(8,128)(2,1)}, bf16[1536,512]{1,0:T(8,128)(2,1)}, u32[]{:S(2)}, u32[]{:S(2)}) %collective-permute-start.1) | collective-permute-done | bytes 1572896 | tf_op jit(solution)/shard_map/ppermute | solution.py:335
  78.7 10.7 %partial_sums.4 = (f32[768,512]{1,0:T(8,128)S(1)}, bf16[768,512]{1,0:T(8,128)(2,1)S(1)}) custom-call(s32[2]{0:T(128)S(1)} %pad_add_fusion.where_ref, bf16[6144,3072]{1,0:T(8,128)(2,1)} %a1_ref.7, bf16[6144,3072]{1,0:T(8,128)(2,1)} %a1_ref.7, bf16[1536,512]{1,0:T(8,128)(2,1)} %get-tuple-element.154.refs_0_, bf16[1536,512]{1,0:T(8,128)(2,1)} %collective-permute-done.refs_1_, ...), custom_call_target="tpu_custom_call" | custom-call | flops 4831838208 | bytes 14155776 | tf_op jit(solution)/shard_map/partial_sums/pallas_call | solution.py:97
  94.1 11.4 %partial_sums.5 = (f32[768,512]{1,0:T(8,128)S(1)}, bf16[768,512]{1,0:T(8,128)(2,1)}) custom-call(s32[2]{0:T(128)S(1)} %pad_add_fusion.where_ref, bf16[6144,3072]{1,0:T(8,128)(2,1)} %a1_ref.7, bf16[6144,3072]{1,0:T(8,128)(2,1)} %a1_ref.7, bf16[1536,512]{1,0:T(8,128)(2,1)} %get-tuple-element.154.refs_0_, bf16[1536,512]{1,0:T(8,128)(2,1)} %collective-permute-done.refs_1_, ...), custom_call_target="tpu_custom_call" | custom-call | flops 4831838208 | bytes 14155776 | tf_op jit(solution)/shard_map/partial_sums/pallas_call | solution.py:97
  106.7 10.7 %partial_sums.6 = (f32[768,512]{1,0:T(8,128)S(1)}, bf16[768,512]{1,0:T(8,128)(2,1)S(1)}) custom-call(s32[2]{0:T(128)S(1)} %pad_add_fusion.where_ref, bf16[6144,3072]{1,0:T(8,128)(2,1)} %a1_ref.7, bf16[6144,3072]{1,0:T(8,128)(2,1)} %a1_ref.7, bf16[1536,512]{1,0:T(8,128)(2,1)} %get-tuple-element.154.refs_0_, bf16[1536,512]{1,0:T(8,128)(2,1)} %collective-permute-done.refs_1_, ...), custom_call_target="tpu_custom_call" | custom-call | flops 4831838208 | bytes 14155776 | tf_op jit(solution)/shard_map/partial_sums/pallas_call | solution.py:97
  121.8 6.9 %collective-permute-start.9 = (bf16[768,512]{1,0:T(8,128)(2,1)}, bf16[768,512]{1,0:T(8,128)(2,1)}, u32[]{:S(2)}, u32[]{:S(2)}) collective-permute-start(bf16[768,512]{1,0:T(8,128)(2,1)} %add_convert_fusion.6.refs_8_), channel_id=1, source_target_pairs={{0,2},{1,3},{2,0},{3,1},{4,6},{5,7},{6,4},{7,5},{8,10},{9,11},{10,... | collective-permute-start | bytes 2359304 | tf_op jit(solution)/shard_map/ppermute | solution.py:339
  128.7 11.4 %partial_sums.7 = (f32[768,512]{1,0:T(8,128)S(1)}, bf16[768,512]{1,0:T(8,128)(2,1)}) custom-call(s32[2]{0:T(128)S(1)} %pad_add_fusion.where_ref, bf16[6144,3072]{1,0:T(8,128)(2,1)} %a1_ref.7, bf16[6144,3072]{1,0:T(8,128)(2,1)} %a1_ref.7, bf16[1536,512]{1,0:T(8,128)(2,1)} %get-tuple-element.154.refs_0_, bf16[1536,512]{1,0:T(8,128)(2,1)} %collective-permute-done.refs_1_, ...), custom_call_target="tpu_custom_call" | custom-call | flops 4831838208 | bytes 14155776 | tf_op jit(solution)/shard_map/partial_sums/pallas_call | solution.py:97
  141.3 5.7 %collective-permute-done.9 = bf16[768,512]{1,0:T(8,128)(2,1)} collective-permute-done((bf16[768,512]{1,0:T(8,128)(2,1)}, bf16[768,512]{1,0:T(8,128)(2,1)}, u32[]{:S(2)}, u32[]{:S(2)}) %collective-permute-start.9) | collective-permute-done | bytes 786464 | tf_op jit(solution)/shard_map/ppermute | solution.py:339
  147.0 2.5 fusion.1
  151.1 3.5 %broadcast_select_fusion.5 = (bf16[768,512]{1,0:T(8,128)(2,1)}, bf16[768,512]{1,0:T(8,128)(2,1)}, bf16[768,512]{1,0:T(8,128)(2,1)}) fusion(pred[]{:T(512)S(6)} %or.3, f32[768,512]{1,0:T(8,128)S(1)} %copy-done.5, bf16[768,512]{1,0:T(8,128)(2,1)} %collective-permute-done.11, bf16[768,512]{1,0:T(8,128)(2,1)} %collective-permute-done.10, ...), kind=kLoop, calls=%fused_computation.26 | loop fusion | flops 5111808 | bytes 7864325 | tf_op jit(solution)/shard_map/jit(_where)/select_n | solution.py:404
  156.7 17.5 %collective-permute-done.12 = bf16[768,512]{1,0:T(8,128)(2,1)} collective-permute-done((bf16[768,512]{1,0:T(8,128)(2,1)}, bf16[768,512]{1,0:T(8,128)(2,1)}, u32[]{:S(2)}, u32[]{:S(2)}) %collective-permute-start.12) | collective-permute-done | bytes 786464 | tf_op jit(solution)/shard_map/ppermute | solution.py:339
  175.8 2.9 broadcast_select_fusion.4
  180.4 3.0 collective-permute-start.18
  186.6 13.3 %collective-permute-done.18 = bf16[768,512]{1,0:T(8,128)(2,1)} collective-permute-done((bf16[768,512]{1,0:T(8,128)(2,1)S(1)}, bf16[768,512]{1,0:T(8,128)(2,1)}, u32[]{:S(2)}, u32[]{:S(2)}) %collective-permute-start.18) | collective-permute-done | bytes 786464 | tf_op jit(solution)/shard_map/ppermute | solution.py:335
  204.5 3.5 %add_convert_fusion.1 = (bf16[768,512]{1,0:T(8,128)(2,1)}, bf16[768,512]{1,0:T(8,128)(2,1)}) fusion(bf16[768,512]{1,0:T(8,128)(2,1)S(1)} %collective-permute-done.16, bf16[768,512]{1,0:T(8,128)(2,1)} %collective-permute-done.12, bf16[768,512]{1,0:T(8,128)(2,1)S(1)} %copy-done.13, bf16[6144,512]{1,0:T(8,128)(2,1)} %param.4, s32[]{:T(128)S(6)} %select_n.88, ...), kind=kLoop, calls=%fused_computation.2 | loop fusion | flops 5111808 | bytes 6291460 | tf_op jit(solution)/shard_map/convert_element_type | solution.py:399
  209.0 3.2 collective-permute-start.23
  219.2 9.8 %collective-permute-done.23.refs_4_.refs_5_.refs_6_ = bf16[768,512]{1,0:T(8,128)(2,1)} collective-permute-done((bf16[768,512]{1,0:T(8,128)(2,1)}, bf16[768,512]{1,0:T(8,128)(2,1)}, u32[]{:S(2)}, u32[]{:S(2)}) %collective-permute-start.23) | collective-permute-done | bytes 786464 | tf_op jit(solution)/shard_map/ppermute | solution.py:335
  231.2 3.1 collective-permute-done.20
  234.3 3.2 %add_convert_fusion.refs_0_.refs_1_.refs_2_ = bf16[768,512]{1,0:T(8,128)(2,1)} fusion(bf16[768,512]{1,0:T(8,128)(2,1)} %collective-permute-done.21, bf16[768,512]{1,0:T(8,128)(2,1)} %copy-done.14, bf16[768,512]{1,0:T(8,128)(2,1)} %copy-done.12, bf16[6144,512]{1,0:T(8,128)(2,1)} %param.4, s32[]{:T(128)S(6)} %select_n.96), kind=kLoop, calls=%fused_computation | loop fusion | flops 3538944 | bytes 3932164 | tf_op jit(solution)/shard_map/convert_element_type | solution.py:399
  239.7 9.0 %collective-permute-start.28 = (bf16[768,512]{1,0:T(8,128)(2,1)}, bf16[768,512]{1,0:T(8,128)(2,1)}, u32[]{:S(2)}, u32[]{:S(2)}) collective-permute-start(bf16[768,512]{1,0:T(8,128)(2,1)} %broadcast_select_fusion.1.refs_1_.refs_2_.refs_3_.refs_4_.refs_5_.own0_ref), channel_id=1, source_target_pairs={{0,8},{1,9},{10,2},{11,3},{20,28},{21,29},{30,22},{31,23}} | collective-permute-start | bytes 2359304 | tf_op jit(solution)/shard_map/ppermute | solution.py:335
  254.8 2.7 new_rows.2
  257.5 2.7 new_cols.2
  260.2 3.8 %new_rows.3 = (bf16[6144,3072]{1,0:T(8,128)(2,1)}, bf16[6144,512]{1,0:T(8,128)(2,1)S(1)}, f32[8,128]{1,0:T(8,128)S(1)}) custom-call(s32[1]{0:T(128)} %bitcast.k_ref, bf16[768,512]{1,0:T(8,128)(2,1)} %broadcast_select_fusion.2.own_ref, bf16[768,512]{1,0:T(8,128)(2,1)S(1)} %copy-done.11, ...), custom_call_target="tpu_custom_call", output_to_operand_aliasing={{0}: (6, {}), {1}: (7, {})} | custom-call | flops 1207959552 | bytes 3145728 | tf_op jit(solution)/shard_map/new_rows/pallas_call | solution.py:153
  267.8 3.1 collective-permute-done.26
  272.3 4.6 %collective-permute-start.31 = (bf16[384,512]{1,0:T(8,128)(2,1)S(1)}, bf16[384,512]{1,0:T(8,128)(2,1)S(1)}, u32[]{:S(2)}, u32[]{:S(2)}) collective-permute-start(bf16[384,512]{1,0:T(8,128)(2,1)S(1)} %get-tuple-element.160), channel_id=1, source_target_pairs={{0,8},{1,9},{10,2},{11,3},{20,28},{21,29},{30,22},{31,23}} | collective-permute-start | bytes 1179656 | tf_op jit(solution)/shard_map/ppermute | solution.py:335
  283.6 4.4 %new_cols.3 = (bf16[6144,3072]{1,0:T(8,128)(2,1)}, bf16[3072,512]{1,0:T(8,128)(2,1)S(1)}, f32[8,128]{1,0:T(8,128)S(1)}) custom-call(bf16[6144,512]{1,0:T(8,128)(2,1)S(1)} %get-tuple-element.124.wr_ref.refs_1_, bf16[768,512]{1,0:T(8,128)(2,1)S(1)} %add_select_fusion.cols_ref, ...), custom_call_target="tpu_custom_call", output_to_operand_aliasing={{0}: (4, {}), {1}: (5, {})} | custom-call | flops 2415919104 | bytes 15728640 | tf_op jit(solution)/shard_map/new_cols/pallas_call | solution.py:259
  288.1 4.6 %collective-permute-start.36 = (bf16[384,512]{1,0:T(8,128)(2,1)S(1)}, bf16[384,512]{1,0:T(8,128)(2,1)S(1)}, u32[]{:S(2)}, u32[]{:S(2)}) collective-permute-start(bf16[384,512]{1,0:T(8,128)(2,1)S(1)} %get-tuple-element.158), channel_id=1, source_target_pairs={{0,8},{1,9},{10,2},{11,3},{20,28},{21,29},{30,22},{31,23}} | collective-permute-start | bytes 1179656 | tf_op jit(solution)/shard_map/ppermute | solution.py:335
  292.7 3.0 collective-permute-start.37
  299.2 9.1 %last_rows.1 = (bf16[6144,3072]{1,0:T(8,128)(2,1)}, bf16[6144,512]{1,0:T(8,128)(2,1)S(1)}, f32[8,128]{1,0:T(8,128)S(1)}) custom-call(s32[1]{0:T(128)} %bitcast.k_ref, bf16[768,512]{1,0:T(8,128)(2,1)} %broadcast_select_fusion.1.refs_1_.refs_2_.refs_3_.refs_4_.refs_5_.own0_ref, ...), custom_call_target="tpu_custom_call", output_to_operand_aliasing={{0}: (8, {}), {1}: (9, {})} | custom-call | flops 4831838208 | bytes 11010048 | tf_op jit(solution)/shard_map/last_rows/pallas_call | solution.py:209
  308.5 13.1 %last_cols.1 = bf16[6144,3072]{1,0:T(8,128)(2,1)} custom-call(bf16[6144,512]{1,0:T(8,128)(2,1)S(1)} %get-tuple-element.137.wr_ref, bf16[768,512]{1,0:T(8,128)(2,1)S(1)} %fusion.4.c0_ref, bf16[768,512]{1,0:T(8,128)(2,1)S(1)} %pad_maximum_fusion.c1_ref, f32[6144,128]{1,0:T(8,128)S(1)} %broadcast_in_dim.4.gr_ref, ...), custom_call_target="tpu_custom_call", output_to_operand_aliasing={{}: (5, {})} | custom-call | flops 9663676416 | bytes 18874368 | tf_op jit(solution)/shard_map/last_cols/pallas_call | solution.py:298
  (123 shorter events, 73.5 us)
Async XLA Ops:
  3.8 39.9 %collective-permute-start = (bf16[1536,512]{1,0:T(8,128)(2,1)}, bf16[1536,512]{1,0:T(8,128)(2,1)}, u32[]{:S(2)}, u32[]{:S(2)}) collective-permute-start(bf16[1536,512]{1,0:T(8,128)(2,1)} %get-tuple-element.154.refs_0_), channel_id=1, source_target_pairs={{0,8},{1,9},{10,2},{11,3},{20,28},{21,29},{30,22},{31,23}} | collective-permute-start | bytes 4718600 | tf_op jit(solution)/shard_map/ppermute | solution.py:335
  9.8 36.7 %collective-permute-start.4 = (bf16[1536,512]{1,0:T(8,128)(2,1)}, bf16[1536,512]{1,0:T(8,128)(2,1)}, u32[]{:S(2)}, u32[]{:S(2)}) collective-permute-start(bf16[1536,512]{1,0:T(8,128)(2,1)} %get-tuple-element.153.refs_4_), channel_id=1, source_target_pairs={{0,16},{1,17},{10,26},{11,27},{20,4},{21,5},{30,14},{31,15}} | collective-permute-start | bytes 4718600 | tf_op jit(solution)/shard_map/ppermute | solution.py:335
  12.2 66.5 %collective-permute-start.1 = (bf16[1536,512]{1,0:T(8,128)(2,1)}, bf16[1536,512]{1,0:T(8,128)(2,1)}, u32[]{:S(2)}, u32[]{:S(2)}) collective-permute-start(bf16[1536,512]{1,0:T(8,128)(2,1)} %get-tuple-element.154.refs_0_), channel_id=1, source_target_pairs={{0,16},{1,17},{10,26},{11,27},{20,4},{21,5},{30,14},{31,15}} | collective-permute-start | bytes 4718600 | tf_op jit(solution)/shard_map/ppermute | solution.py:335
  14.7 64.0 %collective-permute-start.3 = (bf16[1536,512]{1,0:T(8,128)(2,1)}, bf16[1536,512]{1,0:T(8,128)(2,1)}, u32[]{:S(2)}, u32[]{:S(2)}) collective-permute-start(bf16[1536,512]{1,0:T(8,128)(2,1)} %get-tuple-element.153.refs_4_), channel_id=1, source_target_pairs={{0,8},{1,9},{10,2},{11,3},{20,28},{21,29},{30,22},{31,23}} | collective-permute-start | bytes 4718600 | tf_op jit(solution)/shard_map/ppermute | solution.py:335
  44.6 34.2 %collective-permute-start.2 = (bf16[1536,512]{1,0:T(8,128)(2,1)}, bf16[1536,512]{1,0:T(8,128)(2,1)}, u32[]{:S(2)}, u32[]{:S(2)}) collective-permute-start(bf16[1536,512]{1,0:T(8,128)(2,1)} %collective-permute-done.refs_1_), channel_id=1, source_target_pairs={{8,24},{9,25},{2,18},{3,19},{28,12},{29,13},{22,6},{23,7}} | collective-permute-start | bytes 4718600 | tf_op jit(solution)/shard_map/ppermute | solution.py:335
  46.5 32.2 %collective-permute-start.5 = (bf16[1536,512]{1,0:T(8,128)(2,1)}, bf16[1536,512]{1,0:T(8,128)(2,1)}, u32[]{:S(2)}, u32[]{:S(2)}) collective-permute-start(bf16[1536,512]{1,0:T(8,128)(2,1)} %collective-permute-done.4.refs_6_), channel_id=1, source_target_pairs={{16,24},{17,25},{26,18},{27,19},{4,12},{5,13},{14,6},{15,7}} | collective-permute-start | bytes 4718600 | tf_op jit(solution)/shard_map/ppermute | solution.py:335
  92.1 25.3 %collective-permute-start.7 = (bf16[768,512]{1,0:T(8,128)(2,1)S(1)}, bf16[768,512]{1,0:T(8,128)(2,1)S(1)}, u32[]{:S(2)}, u32[]{:S(2)}) collective-permute-start(bf16[768,512]{1,0:T(8,128)(2,1)S(1)} %add_convert_fusion.7.refs_8_), channel_id=1, source_target_pairs={{0,2},{1,3},{2,0},{3,1},{4,6},{5,7},{6,4},{7,5},{8,10},{9,11},{10,... | collective-permute-start | bytes 2359304 | tf_op jit(solution)/shard_map/ppermute | solution.py:339
  118.6 22.7 %collective-permute-start.10 = (bf16[768,512]{1,0:T(8,128)(2,1)}, bf16[768,512]{1,0:T(8,128)(2,1)}, u32[]{:S(2)}, u32[]{:S(2)}) collective-permute-start(bf16[768,512]{1,0:T(8,128)(2,1)} %fusion.refs_9_), channel_id=1, source_target_pairs={{2,4},{3,5},{4,2},{5,3},{10,12},{11,13},{12,10},{13,11},{18,20},{1... | collective-permute-start | bytes 2359304 | tf_op jit(solution)/shard_map/ppermute | solution.py:339
  120.2 21.1 %collective-permute-start.11 = (bf16[768,512]{1,0:T(8,128)(2,1)}, bf16[768,512]{1,0:T(8,128)(2,1)}, u32[]{:S(2)}, u32[]{:S(2)}) collective-permute-start(bf16[768,512]{1,0:T(8,128)(2,1)} %get-tuple-element.85), channel_id=1, source_target_pairs={{0,1},{1,0},{2,3},{3,2},{4,5},{5,4},{6,7},{7,6},{8,9},{9,8},{10,11... | collective-permute-start | bytes 2359304 | tf_op jit(solution)/shard_map/ppermute | solution.py:345
  121.8 25.2 %collective-permute-start.9 = (bf16[768,512]{1,0:T(8,128)(2,1)}, bf16[768,512]{1,0:T(8,128)(2,1)}, u32[]{:S(2)}, u32[]{:S(2)}) collective-permute-start(bf16[768,512]{1,0:T(8,128)(2,1)} %add_convert_fusion.6.refs_8_), channel_id=1, source_target_pairs={{0,2},{1,3},{2,0},{3,1},{4,6},{5,7},{6,4},{7,5},{8,10},{9,11},{10,... | collective-permute-start | bytes 2359304 | tf_op jit(solution)/shard_map/ppermute | solution.py:339
  154.6 19.7 %collective-permute-start.12 = (bf16[768,512]{1,0:T(8,128)(2,1)}, bf16[768,512]{1,0:T(8,128)(2,1)}, u32[]{:S(2)}, u32[]{:S(2)}) collective-permute-start(bf16[768,512]{1,0:T(8,128)(2,1)} %get-tuple-element.150), channel_id=1, source_target_pairs={{0,2},{1,3},{2,0},{3,1},{4,6},{5,7},{6,4},{7,5},{8,10},{9,11},{10,... | collective-permute-start | bytes 2359304 | tf_op jit(solution)/shard_map/ppermute | solution.py:339
  156.7 17.5 %collective-permute-start.14 = (bf16[768,512]{1,0:T(8,128)(2,1)}, bf16[768,512]{1,0:T(8,128)(2,1)}, u32[]{:S(2)}, u32[]{:S(2)}) collective-permute-start(bf16[768,512]{1,0:T(8,128)(2,1)} %get-tuple-element.90), channel_id=1, source_target_pairs={{0,1},{1,0},{2,3},{3,2},{4,5},{5,4},{6,7},{7,6},{8,9},{9,8},{10,11... | collective-permute-start | bytes 2359304 | tf_op jit(solution)/shard_map/ppermute | solution.py:345
  180.4 19.6 %collective-permute-start.18 = (bf16[768,512]{1,0:T(8,128)(2,1)S(1)}, bf16[768,512]{1,0:T(8,128)(2,1)}, u32[]{:S(2)}, u32[]{:S(2)}) collective-permute-start(bf16[768,512]{1,0:T(8,128)(2,1)S(1)} %broadcast_select_fusion.3.own_ref), channel_id=1, source_target_pairs={{0,8},{1,9},{10,2},{11,3},{20,28},{21,29},{30,22},{31,23}} | collective-permute-start | bytes 2359304 | tf_op jit(solution)/shard_map/ppermute | solution.py:335
  183.4 18.7 %collective-permute-start.19 = (bf16[768,512]{1,0:T(8,128)(2,1)S(1)}, bf16[768,512]{1,0:T(8,128)(2,1)S(1)}, u32[]{:S(2)}, u32[]{:S(2)}) collective-permute-start(bf16[768,512]{1,0:T(8,128)(2,1)S(1)} %broadcast_select_fusion.3.own_ref), channel_id=1, source_target_pairs={{0,16},{1,17},{10,26},{11,27},{20,4},{21,5},{30,14},{31,15}} | collective-permute-start | bytes 2359304 | tf_op jit(solution)/shard_map/ppermute | solution.py:335
  184.7 19.7 %collective-permute-start.15 = (bf16[768,512]{1,0:T(8,128)(2,1)S(1)}, bf16[768,512]{1,0:T(8,128)(2,1)S(1)}, u32[]{:S(2)}, u32[]{:S(2)}) collective-permute-start(bf16[768,512]{1,0:T(8,128)(2,1)S(1)} %get-tuple-element.95), channel_id=1, source_target_pairs={{0,2},{1,3},{2,0},{3,1},{4,6},{5,7},{6,4},{7,5},{8,10},{9,11},{10,... | collective-permute-start | bytes 2359304 | tf_op jit(solution)/shard_map/ppermute | solution.py:339
  184.8 19.6 %collective-permute-start.16 = (bf16[768,512]{1,0:T(8,128)(2,1)S(1)}, bf16[768,512]{1,0:T(8,128)(2,1)S(1)}, u32[]{:S(2)}, u32[]{:S(2)}) collective-permute-start(bf16[768,512]{1,0:T(8,128)(2,1)S(1)} %fusion.2), channel_id=1, source_target_pairs={{2,4},{3,5},{4,2},{5,3},{10,12},{11,13},{12,10},{13,11},{18,20},{1... | collective-permute-start | bytes 2359304 | tf_op jit(solution)/shard_map/ppermute | solution.py:339
  209.0 20.1 %collective-permute-start.23 = (bf16[768,512]{1,0:T(8,128)(2,1)}, bf16[768,512]{1,0:T(8,128)(2,1)}, u32[]{:S(2)}, u32[]{:S(2)}) collective-permute-start(bf16[768,512]{1,0:T(8,128)(2,1)} %broadcast_select_fusion.2.own_ref), channel_id=1, source_target_pairs={{0,8},{1,9},{10,2},{11,3},{20,28},{21,29},{30,22},{31,23}} | collective-permute-start | bytes 2359304 | tf_op jit(solution)/shard_map/ppermute | solution.py:335
  212.2 19.1 %collective-permute-start.24 = (bf16[768,512]{1,0:T(8,128)(2,1)}, bf16[768,512]{1,0:T(8,128)(2,1)}, u32[]{:S(2)}, u32[]{:S(2)}) collective-permute-start(bf16[768,512]{1,0:T(8,128)(2,1)} %broadcast_select_fusion.2.own_ref), channel_id=1, source_target_pairs={{0,16},{1,17},{10,26},{11,27},{20,4},{21,5},{30,14},{31,15}} | collective-permute-start | bytes 2359304 | tf_op jit(solution)/shard_map/ppermute | solution.py:335
  214.3 20.0 %collective-permute-start.20 = (bf16[768,512]{1,0:T(8,128)(2,1)}, bf16[768,512]{1,0:T(8,128)(2,1)}, u32[]{:S(2)}, u32[]{:S(2)}) collective-permute-start(bf16[768,512]{1,0:T(8,128)(2,1)} %get-tuple-element.100), channel_id=1, source_target_pairs={{0,2},{1,3},{2,0},{3,1},{4,6},{5,7},{6,4},{7,5},{8,10},{9,11},{10,... | collective-permute-start | bytes 2359304 | tf_op jit(solution)/shard_map/ppermute | solution.py:339
  215.2 19.2 %collective-permute-start.21 = (bf16[768,512]{1,0:T(8,128)(2,1)}, bf16[768,512]{1,0:T(8,128)(2,1)}, u32[]{:S(2)}, u32[]{:S(2)}) collective-permute-start(bf16[768,512]{1,0:T(8,128)(2,1)} %get-tuple-element.101), channel_id=1, source_target_pairs={{2,4},{3,5},{4,2},{5,3},{10,12},{11,13},{12,10},{13,11},{18,20},{1... | collective-permute-start | bytes 2359304 | tf_op jit(solution)/shard_map/ppermute | solution.py:339
  217.7 16.7 %collective-permute-start.25 = (bf16[768,512]{1,0:T(8,128)(2,1)}, bf16[768,512]{1,0:T(8,128)(2,1)}, u32[]{:S(2)}, u32[]{:S(2)}) collective-permute-start(bf16[768,512]{1,0:T(8,128)(2,1)} %collective-permute-done.18), channel_id=1, source_target_pairs={{8,24},{9,25},{2,18},{3,19},{28,12},{29,13},{22,6},{23,7}} | collective-permute-start | bytes 2359304 | tf_op jit(solution)/shard_map/ppermute | solution.py:335
  239.7 24.3 %collective-permute-start.27 = (bf16[768,512]{1,0:T(8,128)(2,1)}, bf16[768,512]{1,0:T(8,128)(2,1)}, u32[]{:S(2)}, u32[]{:S(2)}) collective-permute-start(bf16[768,512]{1,0:T(8,128)(2,1)} %broadcast_select_fusion.1.refs_1_.refs_2_.refs_3_.refs_4_.refs_5_.own0_ref), channel_id=1, source_target_pairs={{0,1},{1,0},{2,3},{3,2},{4,5},{5,4},{6,7},{7,6},{8,9},{9,8},{10,11... | collective-permute-start | bytes 2359304 | tf_op jit(solution)/shard_map/ppermute | solution.py:345
  239.7 25.9 %collective-permute-start.28 = (bf16[768,512]{1,0:T(8,128)(2,1)}, bf16[768,512]{1,0:T(8,128)(2,1)}, u32[]{:S(2)}, u32[]{:S(2)}) collective-permute-start(bf16[768,512]{1,0:T(8,128)(2,1)} %broadcast_select_fusion.1.refs_1_.refs_2_.refs_3_.refs_4_.refs_5_.own0_ref), channel_id=1, source_target_pairs={{0,8},{1,9},{10,2},{11,3},{20,28},{21,29},{30,22},{31,23}} | collective-permute-start | bytes 2359304 | tf_op jit(solution)/shard_map/ppermute | solution.py:335
  248.7 19.1 %collective-permute-start.29 = (bf16[768,512]{1,0:T(8,128)(2,1)}, bf16[768,512]{1,0:T(8,128)(2,1)}, u32[]{:S(2)}, u32[]{:S(2)}) collective-permute-start(bf16[768,512]{1,0:T(8,128)(2,1)} %broadcast_select_fusion.1.refs_1_.refs_2_.refs_3_.refs_4_.refs_5_.own0_ref), channel_id=1, source_target_pairs={{0,16},{1,17},{10,26},{11,27},{20,4},{21,5},{30,14},{31,15}} | collective-permute-start | bytes 2359304 | tf_op jit(solution)/shard_map/ppermute | solution.py:335
  250.9 20.0 %collective-permute-start.26 = (bf16[768,512]{1,0:T(8,128)(2,1)}, bf16[768,512]{1,0:T(8,128)(2,1)}, u32[]{:S(2)}, u32[]{:S(2)}) collective-permute-start(bf16[768,512]{1,0:T(8,128)(2,1)} %add_convert_fusion.refs_0_.refs_1_.refs_2_), channel_id=1, source_target_pairs={{0,2},{1,3},{2,0},{3,1},{4,6},{5,7},{6,4},{7,5},{8,10},{9,11},{10,... | collective-permute-start | bytes 2359304 | tf_op jit(solution)/shard_map/ppermute | solution.py:339
  250.9 20.0 %collective-permute-start.30 = (bf16[768,512]{1,0:T(8,128)(2,1)}, bf16[768,512]{1,0:T(8,128)(2,1)}, u32[]{:S(2)}, u32[]{:S(2)}) collective-permute-start(bf16[768,512]{1,0:T(8,128)(2,1)} %collective-permute-done.23.refs_4_.refs_5_.refs_6_), channel_id=1, source_target_pairs={{8,24},{9,25},{2,18},{3,19},{28,12},{29,13},{22,6},{23,7}} | collective-permute-start | bytes 2359304 | tf_op jit(solution)/shard_map/ppermute | solution.py:335
  272.1 15.9 %collective-permute-start.35 = (bf16[768,512]{1,0:T(8,128)(2,1)S(1)}, bf16[768,512]{1,0:T(8,128)(2,1)S(1)}, u32[]{:S(2)}, u32[]{:S(2)}) collective-permute-start(bf16[768,512]{1,0:T(8,128)(2,1)S(1)} %broadcast_select_fusion.refs_2_.own1_ref), channel_id=1, source_target_pairs={{0,1},{1,0},{2,3},{3,2},{4,5},{5,4},{6,7},{7,6},{8,9},{9,8},{10,11... | collective-permute-start | bytes 2359304 | tf_op jit(solution)/shard_map/ppermute | solution.py:345
  272.3 15.8 %collective-permute-start.31 = (bf16[384,512]{1,0:T(8,128)(2,1)S(1)}, bf16[384,512]{1,0:T(8,128)(2,1)S(1)}, u32[]{:S(2)}, u32[]{:S(2)}) collective-permute-start(bf16[384,512]{1,0:T(8,128)(2,1)S(1)} %get-tuple-element.160), channel_id=1, source_target_pairs={{0,8},{1,9},{10,2},{11,3},{20,28},{21,29},{30,22},{31,23}} | collective-permute-start | bytes 1179656 | tf_op jit(solution)/shard_map/ppermute | solution.py:335
  288.1 20.1 %collective-permute-start.36 = (bf16[384,512]{1,0:T(8,128)(2,1)S(1)}, bf16[384,512]{1,0:T(8,128)(2,1)S(1)}, u32[]{:S(2)}, u32[]{:S(2)}) collective-permute-start(bf16[384,512]{1,0:T(8,128)(2,1)S(1)} %get-tuple-element.158), channel_id=1, source_target_pairs={{0,8},{1,9},{10,2},{11,3},{20,28},{21,29},{30,22},{31,23}} | collective-permute-start | bytes 1179656 | tf_op jit(solution)/shard_map/ppermute | solution.py:335
  292.7 15.5 %collective-permute-start.37 = (bf16[384,512]{1,0:T(8,128)(2,1)S(1)}, bf16[384,512]{1,0:T(8,128)(2,1)S(1)}, u32[]{:S(2)}, u32[]{:S(2)}) collective-permute-start(bf16[384,512]{1,0:T(8,128)(2,1)S(1)} %get-tuple-element.157), channel_id=1, source_target_pairs={{0,16},{1,17},{10,26},{11,27},{20,4},{21,5},{30,14},{31,15}} | collective-permute-start | bytes 1179656 | tf_op jit(solution)/shard_map/ppermute | solution.py:335
  295.7 12.5 %collective-permute-start.38 = (bf16[384,512]{1,0:T(8,128)(2,1)S(1)}, bf16[384,512]{1,0:T(8,128)(2,1)S(1)}, u32[]{:S(2)}, u32[]{:S(2)}) collective-permute-start(bf16[384,512]{1,0:T(8,128)(2,1)S(1)} %collective-permute-done.31.refs_3_), channel_id=1, source_target_pairs={{8,24},{9,25},{2,18},{3,19},{28,12},{29,13},{22,6},{23,7}} | collective-permute-start | bytes 1179656 | tf_op jit(solution)/shard_map/ppermute | solution.py:335
  296.4 11.8 %collective-permute-start.39 = (bf16[384,512]{1,0:T(8,128)(2,1)S(1)}, bf16[384,512]{1,0:T(8,128)(2,1)S(1)}, u32[]{:S(2)}, u32[]{:S(2)}) collective-permute-start(bf16[384,512]{1,0:T(8,128)(2,1)S(1)} %collective-permute-done.32.refs_4_), channel_id=1, source_target_pairs={{16,24},{17,25},{26,18},{27,19},{4,12},{5,13},{14,6},{15,7}} | collective-permute-start | bytes 1179656 | tf_op jit(solution)/shard_map/ppermute | solution.py:335
  (27 other events, 225.6 us)

commit v4 on v3

--- a/solution.py
+++ b/solution.py
@@ -8,8 +8,8 @@
 from jax.sharding import PartitionSpec as P
 
 BF16, F32 = jnp.bfloat16, jnp.float32
-VMEM_LIMIT = 20 * 1024 * 1024
-CHUNKS = 4
+VMEM_LIMIT = 28 * 1024 * 1024
+CHUNKS = 6
 
 
 def spread(value, axis, source):

time: 323 us -> 332 us (1.028)
  waiting for transfers between devices: 121 us -> 77 us
  local copies, waits for them, and re-layouts: 11.2 us -> 29.6 us
  starting transfers between devices: 75.5 us -> 90.7 us
  Pallas kernels: 80.1 us -> 93.6 us
  other arithmetic: 33.6 us -> 38.7 us
    ppermute x22 -> x28, waiting for transfers between devices: 86.8 us -> 64.7 us  [in_plane(): return lambda value: lax.ppermute(value, ('row', 'col'), pairs_list)]
    ppermute x10 -> x14, waiting for transfers between devices: 31.8 us -> 10.4 us  [in_line(): return lambda value: lax.ppermute(value, 'col', pairs_list)]
    unnamed x38 -> x96, local copies, waits for them, and re-layouts: 4.4 us -> 24.8 us
    ppermute x22 -> x28, starting transfers between devices: 57.4 us -> 68.7 us  [in_plane(): return lambda value: lax.ppermute(value, ('row', 'col'), pairs_list)]
    pallas_call x4 -> x6, Pallas kernels: 44.2 us -> 51.3 us  [partial_sums(): pl.pallas_call(partial_kernel, grid_spec=pltpu.PrefetchScalarGridSpec(num...]
    pallas_call x2 -> x4, Pallas kernels: 7.14 us -> 12.9 us  [new_cols(): pl.pallas_call(new_cols_kernel, grid=(2 * count,), in_specs=[pl.BlockSpec...]
    pallas_call x2 -> x4, Pallas kernels: 6.52 us -> 11.5 us  [new_rows(): pl.pallas_call(new_rows_kernel, grid_spec=pltpu.PrefetchScalarGridSpec(nu...]
    select_n x2 -> x4, other arithmetic: 6.39 us -> 11 us  [planned_shards(): send = mine[t] if send is None else jnp.where(in_middle, send, mine[t])]
  transfers between devices with their start and end apart: 40 -> 54, of which waited for: 14 -> 12; matrix products, arithmetic and copies ran while one was open for 5% -> 4% of each run, Pallas kernels for 17% -> 23%
where the time goes in v4:
time: 332 us; the launch traced here: 330 us
  Pallas kernels  93.6 us (28%)
  starting transfers between devices  90.7 us (27%)
  waiting for transfers between devices  77 us (23%)
  other arithmetic  38.7 us (12%)
  local copies, waits for them, and re-layouts  29.6 us (9%)
    ppermute x28, starting transfers between devices, in_plane(): return lambda value: lax.ppermute(value, ('row', 'col'), pairs_list)  68.7 us
    ppermute x28, waiting for transfers between devices, in_plane(): return lambda value: lax.ppermute(value, ('row', 'col'), pairs_list)  64.7 us
    pallas_call x6, Pallas kernels, partial_sums(): pl.pallas_call(partial_kernel, grid_spec=pltpu.PrefetchScalarGridSpec(num...  51.3 us
    unnamed x96, local copies, waits for them, and re-layouts  24.8 us
    ppermute x14, starting transfers between devices, in_line(): return lambda value: lax.ppermute(value, 'col', pairs_list)  20.4 us
    pallas_call x4, Pallas kernels, new_cols(): pl.pallas_call(new_cols_kernel, grid=(2 * count,), in_specs=[pl.BlockSpec...  12.9 us
    pallas_call x4, Pallas kernels, new_rows(): pl.pallas_call(new_rows_kernel, grid_spec=pltpu.PrefetchScalarGridSpec(nu...  11.5 us
    pallas_call x1, Pallas kernels, last_cols(): pl.pallas_call(last_cols_kernel, grid=(rows // size,), in_specs=[pl.Block...  11.1 us
  transfers between devices with their start and end apart: 54, of which 12 were waited for; matrix products, arithmetic and copies ran while one was open for 4% of the time, Pallas kernels for 23%

profile of v4, /device:TPU:0, one launch (start us, length us, event | category | flops | bytes accessed | tf_op | source)
XLA Modules:
  0.0 330.3 jit_solution(12632364094399416116)
XLA Ops:
  0.0 3.8 %constant_dynamic-slice_fusion = (bf16[1536,512]{1,0:T(8,128)(2,1)}, bf16[1536,512]{1,0:T(8,128)(2,1)}) fusion(bf16[6144,512]{1,0:T(8,128)(2,1)} %param.4, s32[]{:T(128)S(6)} %select_n.122, s32[]{:T(128)S(6)} %select_n.119), kind=kLoop, calls=%fused_computation.45 | loop fusion | bytes 6291464 | tf_op jit(solution)/shard_map/dynamic_slice | solution.py:357
  3.8 4.9 %collective-permute-start = (bf16[1536,512]{1,0:T(8,128)(2,1)}, bf16[1536,512]{1,0:T(8,128)(2,1)S(1)}, u32[]{:S(2)}, u32[]{:S(2)}) collective-permute-start(bf16[1536,512]{1,0:T(8,128)(2,1)} %get-tuple-element.236.refs_0_), channel_id=1, source_target_pairs={{0,8},{1,9},{10,2},{11,3},{20,28},{21,29},{30,22},{31,23}} | collective-permute-start | bytes 4718600 | tf_op jit(solution)/shard_map/ppermute | solution.py:335
  17.6 26.1 %collective-permute-done.refs_1_ = bf16[1536,512]{1,0:T(8,128)(2,1)S(1)} collective-permute-done((bf16[1536,512]{1,0:T(8,128)(2,1)}, bf16[1536,512]{1,0:T(8,128)(2,1)S(1)}, u32[]{:S(2)}, u32[]{:S(2)}) %collective-permute-start) | collective-permute-done | bytes 1572896 | tf_op jit(solution)/shard_map/ppermute | solution.py:335
  49.8 27.9 %collective-permute-done.1.refs_2_ = bf16[1536,512]{1,0:T(8,128)(2,1)} collective-permute-done((bf16[1536,512]{1,0:T(8,128)(2,1)}, bf16[1536,512]{1,0:T(8,128)(2,1)}, u32[]{:S(2)}, u32[]{:S(2)}) %collective-permute-start.1) | collective-permute-done | bytes 1572896 | tf_op jit(solution)/shard_map/ppermute | solution.py:335
  79.1 8.2 %partial_sums.6 = (f32[512,512]{1,0:T(8,128)S(1)}, bf16[512,512]{1,0:T(8,128)(2,1)S(1)}) custom-call(s32[2]{0:T(128)S(1)} %pad_add_fusion.where_ref, bf16[6144,3072]{1,0:T(8,128)(2,1)} %a1_ref.11, bf16[6144,3072]{1,0:T(8,128)(2,1)} %a1_ref.11, bf16[1536,512]{1,0:T(8,128)(2,1)} %get-tuple-element.236.refs_0_, bf16[1536,512]{1,0:T(8,128)(2,1)S(1)} %copy-done.8, ...), custom_call_target="tpu_custom_call" | custom-call | flops 3221225472 | bytes 9437184 | tf_op jit(solution)/shard_map/partial_sums/pallas_call | solution.py:97
  89.5 3.7 %collective-permute-start.7 = (bf16[512,512]{1,0:T(8,128)(2,1)S(1)}, bf16[512,512]{1,0:T(8,128)(2,1)S(1)}, u32[]{:S(2)}, u32[]{:S(2)}) collective-permute-start(bf16[512,512]{1,0:T(8,128)(2,1)S(1)} %add_convert_fusion.11.refs_8_), channel_id=1, source_target_pairs={{0,2},{1,3},{2,0},{3,1},{4,6},{5,7},{6,4},{7,5},{8,10},{9,11},{10,... | collective-permute-start | bytes 1572872 | tf_op jit(solution)/shard_map/ppermute | solution.py:339
  93.2 8.9 %partial_sums.8 = (f32[512,512]{1,0:T(8,128)S(1)}, bf16[512,512]{1,0:T(8,128)(2,1)}) custom-call(s32[2]{0:T(128)S(1)} %pad_add_fusion.where_ref, bf16[6144,3072]{1,0:T(8,128)(2,1)} %a1_ref.11, bf16[6144,3072]{1,0:T(8,128)(2,1)} %a1_ref.11, bf16[1536,512]{1,0:T(8,128)(2,1)} %get-tuple-element.236.refs_0_, bf16[1536,512]{1,0:T(8,128)(2,1)S(1)} %copy-done.8, ...), custom_call_target="tpu_custom_call" | custom-call | flops 3221225472 | bytes 9437184 | tf_op jit(solution)/shard_map/partial_sums/pallas_call | solution.py:97
  103.1 8.2 %partial_sums.7 = (f32[512,512]{1,0:T(8,128)S(1)}, bf16[512,512]{1,0:T(8,128)(2,1)S(1)}) custom-call(s32[2]{0:T(128)S(1)} %pad_add_fusion.where_ref, bf16[6144,3072]{1,0:T(8,128)(2,1)} %a1_ref.11, bf16[6144,3072]{1,0:T(8,128)(2,1)} %a1_ref.11, bf16[1536,512]{1,0:T(8,128)(2,1)} %get-tuple-element.236.refs_0_, bf16[1536,512]{1,0:T(8,128)(2,1)S(1)} %copy-done.8, ...), custom_call_target="tpu_custom_call" | custom-call | flops 3221225472 | bytes 9437184 | tf_op jit(solution)/shard_map/partial_sums/pallas_call | solution.py:97
  115.2 5.8 %collective-permute-start.9 = (bf16[512,512]{1,0:T(8,128)(2,1)}, bf16[512,512]{1,0:T(8,128)(2,1)}, u32[]{:S(2)}, u32[]{:S(2)}) collective-permute-start(bf16[512,512]{1,0:T(8,128)(2,1)} %add_convert_fusion.10.refs_8_), channel_id=1, source_target_pairs={{0,2},{1,3},{2,0},{3,1},{4,6},{5,7},{6,4},{7,5},{8,10},{9,11},{10,... | collective-permute-start | bytes 1572872 | tf_op jit(solution)/shard_map/ppermute | solution.py:339
  122.4 9.0 %partial_sums.9 = (f32[512,512]{1,0:T(8,128)S(1)}, bf16[512,512]{1,0:T(8,128)(2,1)}) custom-call(s32[2]{0:T(128)S(1)} %pad_add_fusion.where_ref, bf16[6144,3072]{1,0:T(8,128)(2,1)} %a1_ref.11, bf16[6144,3072]{1,0:T(8,128)(2,1)} %a1_ref.11, bf16[1536,512]{1,0:T(8,128)(2,1)} %get-tuple-element.236.refs_0_, bf16[1536,512]{1,0:T(8,128)(2,1)S(1)} %copy-done.9, ...), custom_call_target="tpu_custom_call" | custom-call | flops 3221225472 | bytes 9437184 | tf_op jit(solution)/shard_map/partial_sums/pallas_call | solution.py:97
  137.3 2.9 broadcast_select_fusion.9
  143.9 8.9 %partial_sums.10 = (f32[512,512]{1,0:T(8,128)S(1)}, bf16[512,512]{1,0:T(8,128)(2,1)}) custom-call(s32[2]{0:T(128)S(1)} %pad_add_fusion.where_ref, bf16[6144,3072]{1,0:T(8,128)(2,1)} %a1_ref.11, bf16[6144,3072]{1,0:T(8,128)(2,1)} %a1_ref.11, bf16[1536,512]{1,0:T(8,128)(2,1)} %get-tuple-element.236.refs_0_, bf16[1536,512]{1,0:T(8,128)(2,1)S(1)} %copy-done.10, ...), custom_call_target="tpu_custom_call" | custom-call | flops 3221225472 | bytes 9437184 | tf_op jit(solution)/shard_map/partial_sums/pallas_call | solution.py:97
  156.4 3.2 broadcast_select_fusion.8
  161.5 3.0 collective-permute-start.18
  170.5 8.3 %partial_sums.11 = (f32[512,512]{1,0:T(8,128)S(1)}, bf16[512,512]{1,0:T(8,128)(2,1)S(1)}) custom-call(s32[2]{0:T(128)S(1)} %pad_add_fusion.where_ref, bf16[6144,3072]{1,0:T(8,128)(2,1)} %a1_ref.11, bf16[6144,3072]{1,0:T(8,128)(2,1)} %a1_ref.11, bf16[1536,512]{1,0:T(8,128)(2,1)} %get-tuple-element.236.refs_0_, bf16[1536,512]{1,0:T(8,128)(2,1)S(1)} %copy-done.11, ...), custom_call_target="tpu_custom_call" | custom-call | flops 3221225472 | bytes 9437184 | tf_op jit(solution)/shard_map/partial_sums/pallas_call | solution.py:97
  185.6 3.5 %collective-permute-start.24 = (bf16[512,512]{1,0:T(8,128)(2,1)S(1)}, bf16[512,512]{1,0:T(8,128)(2,1)}, u32[]{:S(2)}, u32[]{:S(2)}) collective-permute-start(bf16[512,512]{1,0:T(8,128)(2,1)S(1)} %broadcast_select_fusion.5.own_ref), channel_id=1, source_target_pairs={{0,8},{1,9},{10,2},{11,3},{20,28},{21,29},{30,22},{31,23}} | collective-permute-start | bytes 1572872 | tf_op jit(solution)/shard_map/ppermute | solution.py:335
  193.4 6.7 %collective-permute-done.24.refs_5_.refs_6_.refs_7_ = bf16[512,512]{1,0:T(8,128)(2,1)} collective-permute-done((bf16[512,512]{1,0:T(8,128)(2,1)S(1)}, bf16[512,512]{1,0:T(8,128)(2,1)}, u32[]{:S(2)}, u32[]{:S(2)}) %collective-permute-start.24) | collective-permute-done | bytes 524320 | tf_op jit(solution)/shard_map/ppermute | solution.py:335
  202.2 3.0 collective-permute-done.21
  206.4 2.8 broadcast_select_fusion.4
  210.0 6.9 %collective-permute-start.31 = (bf16[512,512]{1,0:T(8,128)(2,1)}, bf16[512,512]{1,0:T(8,128)(2,1)}, u32[]{:S(2)}, u32[]{:S(2)}) collective-permute-start(bf16[512,512]{1,0:T(8,128)(2,1)} %broadcast_select_fusion.3.refs_2_.refs_3_.refs_4_.refs_5_.refs_6_.own_ref), channel_id=1, source_target_pairs={{0,8},{1,9},{10,2},{11,3},{20,28},{21,29},{30,22},{31,23}} | collective-permute-start | bytes 1572872 | tf_op jit(solution)/shard_map/ppermute | solution.py:335
  226.0 2.8 new_rows.4
  239.7 7.0 %collective-permute-start.37 = (bf16[512,512]{1,0:T(8,128)(2,1)S(1)}, bf16[512,512]{1,0:T(8,128)(2,1)}, u32[]{:S(2)}, u32[]{:S(2)}) collective-permute-start(bf16[512,512]{1,0:T(8,128)(2,1)S(1)} %broadcast_select_fusion.2.refs_4_.refs_5_.refs_6_.own_ref), channel_id=1, source_target_pairs={{0,8},{1,9},{10,2},{11,3},{20,28},{21,29},{30,22},{31,23}} | collective-permute-start | bytes 1572872 | tf_op jit(solution)/shard_map/ppermute | solution.py:335
  254.2 2.8 copy-done.1
  264.8 3.6 %new_rows.6 = (bf16[6144,3072]{1,0:T(8,128)(2,1)}, bf16[6144,512]{1,0:T(8,128)(2,1)S(1)}, f32[8,128]{1,0:T(8,128)S(1)}) custom-call(s32[1]{0:T(128)} %bitcast.k_ref, bf16[512,512]{1,0:T(8,128)(2,1)} %broadcast_select_fusion.3.refs_2_.refs_3_.refs_4_.refs_5_.refs_6_.own_ref, ...), custom_call_target="tpu_custom_call", output_to_operand_aliasing={{0}: (6, {}), {1}: (7, {})} | custom-call | flops 1073741824 | bytes 3145728 | tf_op jit(solution)/shard_map/new_rows/pallas_call | solution.py:153
  271.5 5.2 %collective-permute-start.42 = (bf16[512,512]{1,0:T(8,128)(2,1)S(1)}, bf16[512,512]{1,0:T(8,128)(2,1)S(1)}, u32[]{:S(2)}, u32[]{:S(2)}) collective-permute-start(bf16[512,512]{1,0:T(8,128)(2,1)S(1)} %broadcast_select_fusion.1.refs_3_.refs_4_.refs_5_.own0_ref), channel_id=1, source_target_pairs={{0,8},{1,9},{10,2},{11,3},{20,28},{21,29},{30,22},{31,23}} | collective-permute-start | bytes 1572872 | tf_op jit(solution)/shard_map/ppermute | solution.py:335
  280.5 4.4 %new_cols.6 = (bf16[6144,3072]{1,0:T(8,128)(2,1)}, bf16[3072,512]{1,0:T(8,128)(2,1)S(1)}, f32[8,128]{1,0:T(8,128)}) custom-call(bf16[6144,512]{1,0:T(8,128)(2,1)S(1)} %get-tuple-element.188.wr_ref.refs_1_, bf16[512,512]{1,0:T(8,128)(2,1)S(1)} %add_select_fusion.1.cols_ref, f32[6144,128]{1,0:T(8,128)S(1)} %copy-done.4, ...), custom_call_target="tpu_custom_call", output_to_operand_aliasing={{0}: (4, {}), {1}: (5, {})} | custom-call | flops 1610612736 | bytes 12582912 | tf_op jit(solution)/shard_map/new_cols/pallas_call | solution.py:259
  284.8 3.2 new_rows.7
  292.3 4.2 %collective-permute-start.45 = (bf16[256,512]{1,0:T(8,128)(2,1)S(1)}, bf16[256,512]{1,0:T(8,128)(2,1)S(1)}, u32[]{:S(2)}, u32[]{:S(2)}) collective-permute-start(bf16[256,512]{1,0:T(8,128)(2,1)S(1)} %get-tuple-element.242), channel_id=1, source_target_pairs={{0,8},{1,9},{10,2},{11,3},{20,28},{21,29},{30,22},{31,23}} | collective-permute-start | bytes 786440 | tf_op jit(solution)/shard_map/ppermute | solution.py:335
  300.7 4.3 %new_cols.7 = (bf16[6144,3072]{1,0:T(8,128)(2,1)}, bf16[3072,512]{1,0:T(8,128)(2,1)S(1)}, f32[8,128]{1,0:T(8,128)S(1)}) custom-call(bf16[6144,512]{1,0:T(8,128)(2,1)S(1)} %get-tuple-element.200.wr_ref.refs_1_, bf16[512,512]{1,0:T(8,128)(2,1)S(1)} %add_select_fusion.cols_ref, ...), custom_call_target="tpu_custom_call", output_to_operand_aliasing={{0}: (4, {}), {1}: (5, {})} | custom-call | flops 2147483648 | bytes 16777216 | tf_op jit(solution)/shard_map/new_cols/pallas_call | solution.py:259
  305.0 3.7 %collective-permute-start.50 = (bf16[256,512]{1,0:T(8,128)(2,1)S(1)}, bf16[256,512]{1,0:T(8,128)(2,1)S(1)}, u32[]{:S(2)}, u32[]{:S(2)}) collective-permute-start(bf16[256,512]{1,0:T(8,128)(2,1)S(1)} %get-tuple-element.240), channel_id=1, source_target_pairs={{0,8},{1,9},{10,2},{11,3},{20,28},{21,29},{30,22},{31,23}} | collective-permute-start | bytes 786440 | tf_op jit(solution)/shard_map/ppermute | solution.py:335
  311.9 6.9 %last_rows.1 = (bf16[6144,3072]{1,0:T(8,128)(2,1)}, bf16[6144,512]{1,0:T(8,128)(2,1)S(1)}, f32[8,128]{1,0:T(8,128)S(1)}) custom-call(s32[1]{0:T(128)} %bitcast.k_ref, bf16[512,512]{1,0:T(8,128)(2,1)S(1)} %broadcast_select_fusion.1.refs_3_.refs_4_.refs_5_.own0_ref, ...), custom_call_target="tpu_custom_call", output_to_operand_aliasing={{0}: (8, {}), {1}: (9, {})} | custom-call | flops 4294967296 | bytes 10485760 | tf_op jit(solution)/shard_map/last_rows/pallas_call | solution.py:209
  319.2 11.1 %last_cols.1 = bf16[6144,3072]{1,0:T(8,128)(2,1)} custom-call(bf16[6144,512]{1,0:T(8,128)(2,1)S(1)} %get-tuple-element.213.wr_ref, bf16[512,512]{1,0:T(8,128)(2,1)S(1)} %fusion.6.c0_ref, bf16[512,512]{1,0:T(8,128)(2,1)S(1)} %pad_maximum_fusion.c1_ref, f32[6144,128]{1,0:T(8,128)S(1)} %copy-done.4, ...), custom_call_target="tpu_custom_call", output_to_operand_aliasing={{}: (5, {})} | custom-call | flops 6442450944 | bytes 12582912 | tf_op jit(solution)/shard_map/last_cols/pallas_call | solution.py:298
  (224 shorter events, 114.9 us)
Async XLA Ops:
  3.8 39.9 %collective-permute-start = (bf16[1536,512]{1,0:T(8,128)(2,1)}, bf16[1536,512]{1,0:T(8,128)(2,1)S(1)}, u32[]{:S(2)}, u32[]{:S(2)}) collective-permute-start(bf16[1536,512]{1,0:T(8,128)(2,1)} %get-tuple-element.236.refs_0_), channel_id=1, source_target_pairs={{0,8},{1,9},{10,2},{11,3},{20,28},{21,29},{30,22},{31,23}} | collective-permute-start | bytes 4718600 | tf_op jit(solution)/shard_map/ppermute | solution.py:335
  8.7 39.2 %collective-permute-start.4 = (bf16[1536,512]{1,0:T(8,128)(2,1)}, bf16[1536,512]{1,0:T(8,128)(2,1)}, u32[]{:S(2)}, u32[]{:S(2)}) collective-permute-start(bf16[1536,512]{1,0:T(8,128)(2,1)} %get-tuple-element.235.refs_4_), channel_id=1, source_target_pairs={{0,16},{1,17},{10,26},{11,27},{20,4},{21,5},{30,14},{31,15}} | collective-permute-start | bytes 4718600 | tf_op jit(solution)/shard_map/ppermute | solution.py:335
  11.2 66.5 %collective-permute-start.1 = (bf16[1536,512]{1,0:T(8,128)(2,1)}, bf16[1536,512]{1,0:T(8,128)(2,1)}, u32[]{:S(2)}, u32[]{:S(2)}) collective-permute-start(bf16[1536,512]{1,0:T(8,128)(2,1)} %get-tuple-element.236.refs_0_), channel_id=1, source_target_pairs={{0,16},{1,17},{10,26},{11,27},{20,4},{21,5},{30,14},{31,15}} | collective-permute-start | bytes 4718600 | tf_op jit(solution)/shard_map/ppermute | solution.py:335
  13.6 64.1 %collective-permute-start.3 = (bf16[1536,512]{1,0:T(8,128)(2,1)}, bf16[1536,512]{1,0:T(8,128)(2,1)}, u32[]{:S(2)}, u32[]{:S(2)}) collective-permute-start(bf16[1536,512]{1,0:T(8,128)(2,1)} %get-tuple-element.235.refs_4_), channel_id=1, source_target_pairs={{0,8},{1,9},{10,2},{11,3},{20,28},{21,29},{30,22},{31,23}} | collective-permute-start | bytes 4718600 | tf_op jit(solution)/shard_map/ppermute | solution.py:335
  45.8 31.9 %collective-permute-start.2 = (bf16[1536,512]{1,0:T(8,128)(2,1)}, bf16[1536,512]{1,0:T(8,128)(2,1)}, u32[]{:S(2)}, u32[]{:S(2)}) collective-permute-start(bf16[1536,512]{1,0:T(8,128)(2,1)} %copy-done.7), channel_id=1, source_target_pairs={{8,24},{9,25},{2,18},{3,19},{28,12},{29,13},{22,6},{23,7}} | collective-permute-start | bytes 4718600 | tf_op jit(solution)/shard_map/ppermute | solution.py:335
  47.9 29.8 %collective-permute-start.5 = (bf16[1536,512]{1,0:T(8,128)(2,1)}, bf16[1536,512]{1,0:T(8,128)(2,1)}, u32[]{:S(2)}, u32[]{:S(2)}) collective-permute-start(bf16[1536,512]{1,0:T(8,128)(2,1)} %collective-permute-done.4.refs_6_), channel_id=1, source_target_pairs={{16,24},{17,25},{26,18},{27,19},{4,12},{5,13},{14,6},{15,7}} | collective-permute-start | bytes 4718600 | tf_op jit(solution)/shard_map/ppermute | solution.py:335
  89.5 21.8 %collective-permute-start.7 = (bf16[512,512]{1,0:T(8,128)(2,1)S(1)}, bf16[512,512]{1,0:T(8,128)(2,1)S(1)}, u32[]{:S(2)}, u32[]{:S(2)}) collective-permute-start(bf16[512,512]{1,0:T(8,128)(2,1)S(1)} %add_convert_fusion.11.refs_8_), channel_id=1, source_target_pairs={{0,2},{1,3},{2,0},{3,1},{4,6},{5,7},{6,4},{7,5},{8,10},{9,11},{10,... | collective-permute-start | bytes 1572872 | tf_op jit(solution)/shard_map/ppermute | solution.py:339
  112.3 19.1 %collective-permute-start.10 = (bf16[512,512]{1,0:T(8,128)(2,1)}, bf16[512,512]{1,0:T(8,128)(2,1)}, u32[]{:S(2)}, u32[]{:S(2)}) collective-permute-start(bf16[512,512]{1,0:T(8,128)(2,1)} %fusion.refs_9_), channel_id=1, source_target_pairs={{2,4},{3,5},{4,2},{5,3},{10,12},{11,13},{12,10},{13,11},{18,20},{1... | collective-permute-start | bytes 1572872 | tf_op jit(solution)/shard_map/ppermute | solution.py:339
  113.8 17.6 %collective-permute-start.11 = (bf16[512,512]{1,0:T(8,128)(2,1)}, bf16[512,512]{1,0:T(8,128)(2,1)}, u32[]{:S(2)}, u32[]{:S(2)}) collective-permute-start(bf16[512,512]{1,0:T(8,128)(2,1)} %get-tuple-element.122), channel_id=1, source_target_pairs={{0,1},{1,0},{2,3},{3,2},{4,5},{5,4},{6,7},{7,6},{8,9},{9,8},{10,11... | collective-permute-start | bytes 1572872 | tf_op jit(solution)/shard_map/ppermute | solution.py:345
  115.2 18.5 %collective-permute-start.9 = (bf16[512,512]{1,0:T(8,128)(2,1)}, bf16[512,512]{1,0:T(8,128)(2,1)}, u32[]{:S(2)}, u32[]{:S(2)}) collective-permute-start(bf16[512,512]{1,0:T(8,128)(2,1)} %add_convert_fusion.10.refs_8_), channel_id=1, source_target_pairs={{0,2},{1,3},{2,0},{3,1},{4,6},{5,7},{6,4},{7,5},{8,10},{9,11},{10,... | collective-permute-start | bytes 1572872 | tf_op jit(solution)/shard_map/ppermute | solution.py:339
  135.8 17.9 %collective-permute-start.13 = (bf16[512,512]{1,0:T(8,128)(2,1)}, bf16[512,512]{1,0:T(8,128)(2,1)}, u32[]{:S(2)}, u32[]{:S(2)}) collective-permute-start(bf16[512,512]{1,0:T(8,128)(2,1)} %fusion.1.refs_9_), channel_id=1, source_target_pairs={{2,4},{3,5},{4,2},{5,3},{10,12},{11,13},{12,10},{13,11},{18,20},{1... | collective-permute-start | bytes 1572872 | tf_op jit(solution)/shard_map/ppermute | solution.py:339
  140.2 14.1 %collective-permute-start.12 = (bf16[512,512]{1,0:T(8,128)(2,1)}, bf16[512,512]{1,0:T(8,128)(2,1)}, u32[]{:S(2)}, u32[]{:S(2)}) collective-permute-start(bf16[512,512]{1,0:T(8,128)(2,1)} %get-tuple-element.232.refs_8_), channel_id=1, source_target_pairs={{0,2},{1,3},{2,0},{3,1},{4,6},{5,7},{6,4},{7,5},{8,10},{9,11},{10,... | collective-permute-start | bytes 1572872 | tf_op jit(solution)/shard_map/ppermute | solution.py:339
  161.5 17.3 %collective-permute-start.18 = (bf16[512,512]{1,0:T(8,128)(2,1)}, bf16[512,512]{1,0:T(8,128)(2,1)}, u32[]{:S(2)}, u32[]{:S(2)}) collective-permute-start(bf16[512,512]{1,0:T(8,128)(2,1)} %broadcast_select_fusion.7.refs_10_.refs_11_.refs_12_.own_ref), channel_id=1, source_target_pairs={{0,8},{1,9},{10,2},{11,3},{20,28},{21,29},{30,22},{31,23}} | collective-permute-start | bytes 1572872 | tf_op jit(solution)/shard_map/ppermute | solution.py:335
  164.5 14.3 %collective-permute-start.19 = (bf16[512,512]{1,0:T(8,128)(2,1)}, bf16[512,512]{1,0:T(8,128)(2,1)}, u32[]{:S(2)}, u32[]{:S(2)}) collective-permute-start(bf16[512,512]{1,0:T(8,128)(2,1)} %broadcast_select_fusion.7.refs_10_.refs_11_.refs_12_.own_ref), channel_id=1, source_target_pairs={{0,16},{1,17},{10,26},{11,27},{20,4},{21,5},{30,14},{31,15}} | collective-permute-start | bytes 1572872 | tf_op jit(solution)/shard_map/ppermute | solution.py:335
  166.6 14.4 %collective-permute-start.15 = (bf16[512,512]{1,0:T(8,128)(2,1)}, bf16[512,512]{1,0:T(8,128)(2,1)}, u32[]{:S(2)}, u32[]{:S(2)}) collective-permute-start(bf16[512,512]{1,0:T(8,128)(2,1)} %get-tuple-element.135.refs_8_), channel_id=1, source_target_pairs={{0,2},{1,3},{2,0},{3,1},{4,6},{5,7},{6,4},{7,5},{8,10},{9,11},{10,... | collective-permute-start | bytes 1572872 | tf_op jit(solution)/shard_map/ppermute | solution.py:339
  166.6 14.4 %collective-permute-start.16 = (bf16[512,512]{1,0:T(8,128)(2,1)}, bf16[512,512]{1,0:T(8,128)(2,1)}, u32[]{:S(2)}, u32[]{:S(2)}) collective-permute-start(bf16[512,512]{1,0:T(8,128)(2,1)} %fusion.2.refs_9_), channel_id=1, source_target_pairs={{2,4},{3,5},{4,2},{5,3},{10,12},{11,13},{12,10},{13,11},{18,20},{1... | collective-permute-start | bytes 1572872 | tf_op jit(solution)/shard_map/ppermute | solution.py:339
  185.6 14.5 %collective-permute-start.24 = (bf16[512,512]{1,0:T(8,128)(2,1)S(1)}, bf16[512,512]{1,0:T(8,128)(2,1)}, u32[]{:S(2)}, u32[]{:S(2)}) collective-permute-start(bf16[512,512]{1,0:T(8,128)(2,1)S(1)} %broadcast_select_fusion.5.own_ref), channel_id=1, source_target_pairs={{0,8},{1,9},{10,2},{11,3},{20,28},{21,29},{30,22},{31,23}} | collective-permute-start | bytes 1572872 | tf_op jit(solution)/shard_map/ppermute | solution.py:335
  191.2 14.0 %collective-permute-start.21 = (bf16[512,512]{1,0:T(8,128)(2,1)S(1)}, bf16[512,512]{1,0:T(8,128)(2,1)S(1)}, u32[]{:S(2)}, u32[]{:S(2)}) collective-permute-start(bf16[512,512]{1,0:T(8,128)(2,1)S(1)} %get-tuple-element.143), channel_id=1, source_target_pairs={{0,2},{1,3},{2,0},{3,1},{4,6},{5,7},{6,4},{7,5},{8,10},{9,11},{10,... | collective-permute-start | bytes 1572872 | tf_op jit(solution)/shard_map/ppermute | solution.py:339
  191.2 14.0 %collective-permute-start.22 = (bf16[512,512]{1,0:T(8,128)(2,1)S(1)}, bf16[512,512]{1,0:T(8,128)(2,1)S(1)}, u32[]{:S(2)}, u32[]{:S(2)}) collective-permute-start(bf16[512,512]{1,0:T(8,128)(2,1)S(1)} %fusion.3), channel_id=1, source_target_pairs={{2,4},{3,5},{4,2},{5,3},{10,12},{11,13},{12,10},{13,11},{18,20},{1... | collective-permute-start | bytes 1572872 | tf_op jit(solution)/shard_map/ppermute | solution.py:339
  210.0 25.4 %collective-permute-start.31 = (bf16[512,512]{1,0:T(8,128)(2,1)}, bf16[512,512]{1,0:T(8,128)(2,1)}, u32[]{:S(2)}, u32[]{:S(2)}) collective-permute-start(bf16[512,512]{1,0:T(8,128)(2,1)} %broadcast_select_fusion.3.refs_2_.refs_3_.refs_4_.refs_5_.refs_6_.own_ref), channel_id=1, source_target_pairs={{0,8},{1,9},{10,2},{11,3},{20,28},{21,29},{30,22},{31,23}} | collective-permute-start | bytes 1572872 | tf_op jit(solution)/shard_map/ppermute | solution.py:335
  216.9 18.5 %collective-permute-start.32 = (bf16[512,512]{1,0:T(8,128)(2,1)}, bf16[512,512]{1,0:T(8,128)(2,1)}, u32[]{:S(2)}, u32[]{:S(2)}) collective-permute-start(bf16[512,512]{1,0:T(8,128)(2,1)} %broadcast_select_fusion.3.refs_2_.refs_3_.refs_4_.refs_5_.refs_6_.own_ref), channel_id=1, source_target_pairs={{0,16},{1,17},{10,26},{11,27},{20,4},{21,5},{30,14},{31,15}} | collective-permute-start | bytes 1572872 | tf_op jit(solution)/shard_map/ppermute | solution.py:335
  219.0 16.4 %collective-permute-start.28 = (bf16[512,512]{1,0:T(8,128)(2,1)}, bf16[512,512]{1,0:T(8,128)(2,1)}, u32[]{:S(2)}, u32[]{:S(2)}) collective-permute-start(bf16[512,512]{1,0:T(8,128)(2,1)} %get-tuple-element.152.refs_0_.refs_1_.refs_2_), channel_id=1, source_target_pairs={{0,2},{1,3},{2,0},{3,1},{4,6},{5,7},{6,4},{7,5},{8,10},{9,11},{10,... | collective-permute-start | bytes 1572872 | tf_op jit(solution)/shard_map/ppermute | solution.py:339
  219.6 15.8 %collective-permute-start.29 = (bf16[512,512]{1,0:T(8,128)(2,1)}, bf16[512,512]{1,0:T(8,128)(2,1)}, u32[]{:S(2)}, u32[]{:S(2)}) collective-permute-start(bf16[512,512]{1,0:T(8,128)(2,1)} %fusion.4.refs_1_.refs_2_.refs_3_), channel_id=1, source_target_pairs={{2,4},{3,5},{4,2},{5,3},{10,12},{11,13},{12,10},{13,11},{18,20},{1... | collective-permute-start | bytes 1572872 | tf_op jit(solution)/shard_map/ppermute | solution.py:339
  239.7 28.6 %collective-permute-start.37 = (bf16[512,512]{1,0:T(8,128)(2,1)S(1)}, bf16[512,512]{1,0:T(8,128)(2,1)}, u32[]{:S(2)}, u32[]{:S(2)}) collective-permute-start(bf16[512,512]{1,0:T(8,128)(2,1)S(1)} %broadcast_select_fusion.2.refs_4_.refs_5_.refs_6_.own_ref), channel_id=1, source_target_pairs={{0,8},{1,9},{10,2},{11,3},{20,28},{21,29},{30,22},{31,23}} | collective-permute-start | bytes 1572872 | tf_op jit(solution)/shard_map/ppermute | solution.py:335
  246.8 21.6 %collective-permute-start.38 = (bf16[512,512]{1,0:T(8,128)(2,1)S(1)}, bf16[512,512]{1,0:T(8,128)(2,1)}, u32[]{:S(2)}, u32[]{:S(2)}) collective-permute-start(bf16[512,512]{1,0:T(8,128)(2,1)S(1)} %broadcast_select_fusion.2.refs_4_.refs_5_.refs_6_.own_ref), channel_id=1, source_target_pairs={{0,16},{1,17},{10,26},{11,27},{20,4},{21,5},{30,14},{31,15}} | collective-permute-start | bytes 1572872 | tf_op jit(solution)/shard_map/ppermute | solution.py:335
  248.9 19.5 %collective-permute-start.34 = (bf16[512,512]{1,0:T(8,128)(2,1)S(1)}, bf16[512,512]{1,0:T(8,128)(2,1)}, u32[]{:S(2)}, u32[]{:S(2)}) collective-permute-start(bf16[512,512]{1,0:T(8,128)(2,1)S(1)} %get-tuple-element.169.refs_2_), channel_id=1, source_target_pairs={{0,2},{1,3},{2,0},{3,1},{4,6},{5,7},{6,4},{7,5},{8,10},{9,11},{10,... | collective-permute-start | bytes 1572872 | tf_op jit(solution)/shard_map/ppermute | solution.py:339
  248.9 19.5 %collective-permute-start.35 = (bf16[512,512]{1,0:T(8,128)(2,1)}, bf16[512,512]{1,0:T(8,128)(2,1)}, u32[]{:S(2)}, u32[]{:S(2)}) collective-permute-start(bf16[512,512]{1,0:T(8,128)(2,1)} %get-tuple-element.170.refs_3_), channel_id=1, source_target_pairs={{2,4},{3,5},{4,2},{5,3},{10,12},{11,13},{12,10},{13,11},{18,20},{1... | collective-permute-start | bytes 1572872 | tf_op jit(solution)/shard_map/ppermute | solution.py:339
  251.2 17.2 %collective-permute-start.39 = (bf16[512,512]{1,0:T(8,128)(2,1)}, bf16[512,512]{1,0:T(8,128)(2,1)}, u32[]{:S(2)}, u32[]{:S(2)}) collective-permute-start(bf16[512,512]{1,0:T(8,128)(2,1)} %collective-permute-done.31.refs_7_), channel_id=1, source_target_pairs={{8,24},{9,25},{2,18},{3,19},{28,12},{29,13},{22,6},{23,7}} | collective-permute-start | bytes 1572872 | tf_op jit(solution)/shard_map/ppermute | solution.py:335
  271.3 16.8 %collective-permute-start.41 = (bf16[512,512]{1,0:T(8,128)(2,1)S(1)}, bf16[512,512]{1,0:T(8,128)(2,1)S(1)}, u32[]{:S(2)}, u32[]{:S(2)}) collective-permute-start(bf16[512,512]{1,0:T(8,128)(2,1)S(1)} %broadcast_select_fusion.1.refs_3_.refs_4_.refs_5_.own0_ref), channel_id=1, source_target_pairs={{0,1},{1,0},{2,3},{3,2},{4,5},{5,4},{6,7},{7,6},{8,9},{9,8},{10,11... | collective-permute-start | bytes 1572872 | tf_op jit(solution)/shard_map/ppermute | solution.py:345
  271.5 17.0 %collective-permute-start.42 = (bf16[512,512]{1,0:T(8,128)(2,1)S(1)}, bf16[512,512]{1,0:T(8,128)(2,1)S(1)}, u32[]{:S(2)}, u32[]{:S(2)}) collective-permute-start(bf16[512,512]{1,0:T(8,128)(2,1)S(1)} %broadcast_select_fusion.1.refs_3_.refs_4_.refs_5_.own0_ref), channel_id=1, source_target_pairs={{0,8},{1,9},{10,2},{11,3},{20,28},{21,29},{30,22},{31,23}} | collective-permute-start | bytes 1572872 | tf_op jit(solution)/shard_map/ppermute | solution.py:335
  278.0 14.1 %collective-permute-start.40 = (bf16[512,512]{1,0:T(8,128)(2,1)S(1)}, bf16[512,512]{1,0:T(8,128)(2,1)S(1)}, u32[]{:S(2)}, u32[]{:S(2)}) collective-permute-start(bf16[512,512]{1,0:T(8,128)(2,1)S(1)} %add_convert_fusion.refs_2_), channel_id=1, source_target_pairs={{0,2},{1,3},{2,0},{3,1},{4,6},{5,7},{6,4},{7,5},{8,10},{9,11},{10,... | collective-permute-start | bytes 1572872 | tf_op jit(solution)/shard_map/ppermute | solution.py:339
  278.1 14.0 %collective-permute-start.44 = (bf16[512,512]{1,0:T(8,128)(2,1)}, bf16[512,512]{1,0:T(8,128)(2,1)S(1)}, u32[]{:S(2)}, u32[]{:S(2)}) collective-permute-start(bf16[512,512]{1,0:T(8,128)(2,1)} %collective-permute-done.37.refs_6_), channel_id=1, source_target_pairs={{8,24},{9,25},{2,18},{3,19},{28,12},{29,13},{22,6},{23,7}} | collective-permute-start | bytes 1572872 | tf_op jit(solution)/shard_map/ppermute | solution.py:335
  (70 other events, 723.5 us)
